TPU v7x, 256 devices: a whole 4x4x8 slice. The times are simulated.
256 devices in a mesh: loop: 32 (over z, x_hi, core), slab: 8 (over y, x_lo).
Axes of the slice: x: 4 (x_hi: 2, x_lo: 2; x = x_hi * 2 + x_lo), y: 4, z: 8, core: 2. Of those that a mesh axis runs over, the one named last changes fastest.
Arguments:
- points: bfloat16 [4096, 768], P('loop'), may hold values from -20 to 20
- centroids: bfloat16 [131072, 768], P(('loop', 'slab')), may hold values from -6 to 6
Outputs:
- new_centroids: float32 [131072, 768], P(('loop', 'slab'))
All inputs are finite; a program needn't handle non-finite values.
Results may differ from a plain program's by a relative error of at most 0.0007.
Values may be sent and summed in bfloat16 or wider, within the bound.
No kernel may reach another device: no remote copies, remote signals or barrier semaphores. Data moves between devices by JAX's collectives and lax.ppermute only.
A program may use at most 64 MiB of HBM per device.

v0:
```python
import jax
import jax.numpy as jnp
from jax import lax
from jax.sharding import PartitionSpec as P

SHARP = 20.0
PRIOR = 0.25


def from_behind(block, axis, distance):
    devices = range(lax.axis_size(axis))
    route = [((i - distance) % len(devices), i) for i in devices]
    return lax.ppermute(block, axis, route)


def combined_all(array, axis, combine):
    everything = jax.tree.map(lambda part: lax.all_gather(part, axis), array)
    first = jax.tree.map(lambda part: part[0], everything)

    def step(k, so_far):
        return combine(so_far, jax.tree.map(lambda part: part[k], everything))

    return lax.fori_loop(1, lax.axis_size(axis), step, first)


def row_squares(block):
    return jnp.einsum("pd,pd->p", block, block, preferred_element_type=jnp.float32)


def tile_logits(xblock, xsq, cblock, csq):
    dots = jnp.dot(xblock, cblock.T, preferred_element_type=jnp.float32)
    return -(SHARP / xblock.shape[1]) * (xsq[:, None] + csq[None, :] - 2.0 * dots)


def absorb(high, total, logits):
    top = jnp.maximum(high, jnp.max(logits, axis=1))
    total = total * jnp.exp(high - top) + jnp.sum(jnp.exp(logits - top[:, None]), axis=1)
    return (top, total)


def combine_norms(first, second):
    top = jnp.maximum(first[0], second[0])
    return (top, first[1] * jnp.exp(first[0] - top) + second[1] * jnp.exp(second[0] - top))


def assign_block(block, norms, centroids, csq, sums, mass):
    lg = tile_logits(block, row_squares(block), centroids, csq)
    resp = jnp.exp(lg - norms[:, None]).astype(jnp.bfloat16)
    mass = mass + jnp.sum(resp.astype(jnp.float32), axis=0)
    sums = sums + lax.dot_general(
        resp, block, (((0,), (0,)), ((), ())), preferred_element_type=jnp.float32
    )
    return (sums, mass)


def shards(points, centroids):
    count = points.shape[0]
    steps = lax.axis_size("loop")
    csq = row_squares(centroids)
    start_sums = jnp.zeros(centroids.shape, jnp.float32)
    start_mass = jnp.zeros((centroids.shape[0],), jnp.float32)
    start_high = jnp.full((count,), -jnp.inf, jnp.float32)
    start_total = jnp.zeros((count,), jnp.float32)

    def first_pass(index, carry):
        block, high, total = carry
        lg = tile_logits(block, row_squares(block), centroids, csq)
        high, total = absorb(high, total, lg)
        block = from_behind(block, "loop", 1)
        high, total = from_behind((high, total), "loop", 1)
        return (block, high, total)

    unused, high, total = lax.fori_loop(0, steps, first_pass, (points, start_high, start_total))
    high, total = combined_all((high, total), "slab", combine_norms)
    lognorm = high + jnp.log(total)

    def second_pass(index, carry):
        block, norms, sums, mass = carry
        sums, mass = assign_block(block, norms, centroids, csq, sums, mass)
        block = from_behind(block, "loop", 1)
        norms = from_behind(norms, "loop", 1)
        return (block, norms, sums, mass)

    unused, unused_norms, sums, mass = lax.fori_loop(
        0, steps, second_pass, (points, lognorm, start_sums, start_mass)
    )
    return (sums + PRIOR * centroids.astype(jnp.float32)) / (mass[:, None] + PRIOR)


def solution(mesh):
    return jax.shard_map(
        shards,
        mesh=mesh,
        in_specs=(P("loop", None), P(("loop", "slab"), None)),
        out_specs=P(("loop", "slab"), None),
        check_vma=False,
    )
```

profile of v0, /device:TPU:1, one launch (start us, length us, event | category | flops | bytes accessed | tf_op | source)
XLA Modules:
  0.0 601.8 jit_solution(3446068699384330740)
XLA Ops:
  2.4 284.7 %while.48 = (s32[]{:T(128)}, bf16[128,768]{1,0:T(8,128)(2,1)S(1)}, f32[128]{0:T(128)S(1)}, f32[128]{0:T(128)S(1)}, f32[512]{0:T(512)S(1)}, /*index=5*/bf16[512,768]{1,0:T(8,128)(2,1)S(1)}, s32[]{:T(128)}) while((s32[]{:T(128)}, bf16[128,768]{1,0:T(8,128)(2,1)S(1)}, f32[128]{0:T(128)S(1)}, f32[128]{0:T(128)S(1)}, f32[512]{0:T(512)S(1)}, ...), condition=%wide.region_3.0_spmd, body=%wide.region_0.0_spmd.sunk | while | flops 101417088 | bytes 2897605 | solution.py:73
  2.4 4.2 collective-permute-start
  15.1 4.1 collective-permute-start.2
  32.3 3.9 collective-permute-start.2
  37.0 3.8 collective-permute-start
  49.5 3.8 collective-permute-start.2
  62.8 3.8 collective-permute-start
  68.1 4.7 collective-permute-start.2
  82.5 3.8 collective-permute-start
  109.2 3.8 collective-permute-start
  127.0 3.8 collective-permute-start
  135.9 3.8 collective-permute-start
  153.7 3.8 collective-permute-start
  287.1 14.2 %all-gather.3 = f32[8,1,128]{2,1,0:T(1,128)S(1)} all-gather(f32[1,1,128]{2,1,0:T(1,128)S(1)} %bitcast.41), channel_id=3, replica_groups=mesh['loop'=32,'slab'=8] {'slab'}, dimensions={0}, use_global_device_ids=true | all-gather | bytes 4608 | tf_op jit(solution)/shard_map/all_gather | solution.py:17
  301.3 11.5 %all-gather.2 = f32[8,1,128]{2,1,0:T(1,128)S(1)} all-gather(f32[1,1,128]{2,1,0:T(1,128)S(1)} %bitcast.40), channel_id=2, replica_groups=mesh['loop'=32,'slab'=8] {'slab'}, dimensions={0}, use_global_device_ids=true | all-gather | bytes 4608 | tf_op jit(solution)/shard_map/all_gather | solution.py:17
  313.1 287.2 %while.50 = (s32[]{:T(128)}, bf16[128,768]{1,0:T(8,128)(2,1)S(1)}, f32[128]{0:T(128)S(1)}, f32[512,768]{1,0:T(8,128)S(1)}, f32[512]{0:T(512)S(1)}, /*index=5*/f3...) while((s32[]{:T(128)}, bf16[128,768]{1,0:T(8,128)(2,1)S(1)}, f32[128]{0:T(128)S(1)}, ...), condition=%wide.region_8.0_spmd.clone, body=%wide.region_6.0_spmd.clone.sunk | while | flops 202932608 | bytes 5978808 | solution.py:84
  313.2 11.7 %collective-permute-start.3 = (bf16[128,768]{1,0:T(8,128)(2,1)S(1)}, bf16[128,768]{1,0:T(8,128)(2,1)S(1)}, u32[]{:S(2)}, u32[]{:S(2)}) collective-permute-start(bf16[128,768]{1,0:T(8,128)(2,1)S(1)} %copy.42), channel_id=1, source_target_pairs={{248,0},{0,8},{8,16},{16,24},{24,32},{32,40},{40,48},{48,56},{56,6... | collective-permute-start | bytes 589832 | tf_op jit(solution)/shard_map/while/body/eval_jaxpr/ppermute | solution.py:13
  327.5 4.1 collective-permute-start.3
  334.3 4.1 collective-permute-start.3
  346.9 5.1 collective-permute-done.4
  354.6 6.3 %collective-permute-done.4 = f32[128]{0:T(128)S(1)} collective-permute-done((f32[128]{0:T(128)S(1)}, f32[128]{0:T(128)S(1)}, u32[]{:S(2)}, u32[]{:S(2)}) %collective-permute-start.4) | collective-permute-done | bytes 544 | tf_op jit(solution)/shard_map/while/body/eval_jaxpr/ppermute | solution.py:13
  362.3 7.4 %collective-permute-done.4 = f32[128]{0:T(128)S(1)} collective-permute-done((f32[128]{0:T(128)S(1)}, f32[128]{0:T(128)S(1)}, u32[]{:S(2)}, u32[]{:S(2)}) %collective-permute-start.4) | collective-permute-done | bytes 544 | tf_op jit(solution)/shard_map/while/body/eval_jaxpr/ppermute | solution.py:13
  371.2 7.4 %collective-permute-done.4 = f32[128]{0:T(128)S(1)} collective-permute-done((f32[128]{0:T(128)S(1)}, f32[128]{0:T(128)S(1)}, u32[]{:S(2)}, u32[]{:S(2)}) %collective-permute-start.4) | collective-permute-done | bytes 544 | tf_op jit(solution)/shard_map/while/body/eval_jaxpr/ppermute | solution.py:13
  380.1 7.4 %collective-permute-done.4 = f32[128]{0:T(128)S(1)} collective-permute-done((f32[128]{0:T(128)S(1)}, f32[128]{0:T(128)S(1)}, u32[]{:S(2)}, u32[]{:S(2)}) %collective-permute-start.4) | collective-permute-done | bytes 544 | tf_op jit(solution)/shard_map/while/body/eval_jaxpr/ppermute | solution.py:13
  388.9 7.4 %collective-permute-done.4 = f32[128]{0:T(128)S(1)} collective-permute-done((f32[128]{0:T(128)S(1)}, f32[128]{0:T(128)S(1)}, u32[]{:S(2)}, u32[]{:S(2)}) %collective-permute-start.4) | collective-permute-done | bytes 544 | tf_op jit(solution)/shard_map/while/body/eval_jaxpr/ppermute | solution.py:13
  397.8 7.4 %collective-permute-done.4 = f32[128]{0:T(128)S(1)} collective-permute-done((f32[128]{0:T(128)S(1)}, f32[128]{0:T(128)S(1)}, u32[]{:S(2)}, u32[]{:S(2)}) %collective-permute-start.4) | collective-permute-done | bytes 544 | tf_op jit(solution)/shard_map/while/body/eval_jaxpr/ppermute | solution.py:13
  406.7 7.4 %collective-permute-done.4 = f32[128]{0:T(128)S(1)} collective-permute-done((f32[128]{0:T(128)S(1)}, f32[128]{0:T(128)S(1)}, u32[]{:S(2)}, u32[]{:S(2)}) %collective-permute-start.4) | collective-permute-done | bytes 544 | tf_op jit(solution)/shard_map/while/body/eval_jaxpr/ppermute | solution.py:13
  415.5 7.4 %collective-permute-done.4 = f32[128]{0:T(128)S(1)} collective-permute-done((f32[128]{0:T(128)S(1)}, f32[128]{0:T(128)S(1)}, u32[]{:S(2)}, u32[]{:S(2)}) %collective-permute-start.4) | collective-permute-done | bytes 544 | tf_op jit(solution)/shard_map/while/body/eval_jaxpr/ppermute | solution.py:13
  424.4 7.4 %collective-permute-done.4 = f32[128]{0:T(128)S(1)} collective-permute-done((f32[128]{0:T(128)S(1)}, f32[128]{0:T(128)S(1)}, u32[]{:S(2)}, u32[]{:S(2)}) %collective-permute-start.4) | collective-permute-done | bytes 544 | tf_op jit(solution)/shard_map/while/body/eval_jaxpr/ppermute | solution.py:13
  433.3 7.4 %collective-permute-done.4 = f32[128]{0:T(128)S(1)} collective-permute-done((f32[128]{0:T(128)S(1)}, f32[128]{0:T(128)S(1)}, u32[]{:S(2)}, u32[]{:S(2)}) %collective-permute-start.4) | collective-permute-done | bytes 544 | tf_op jit(solution)/shard_map/while/body/eval_jaxpr/ppermute | solution.py:13
  442.1 7.4 %collective-permute-done.4 = f32[128]{0:T(128)S(1)} collective-permute-done((f32[128]{0:T(128)S(1)}, f32[128]{0:T(128)S(1)}, u32[]{:S(2)}, u32[]{:S(2)}) %collective-permute-start.4) | collective-permute-done | bytes 544 | tf_op jit(solution)/shard_map/while/body/eval_jaxpr/ppermute | solution.py:13
  451.0 7.4 %collective-permute-done.4 = f32[128]{0:T(128)S(1)} collective-permute-done((f32[128]{0:T(128)S(1)}, f32[128]{0:T(128)S(1)}, u32[]{:S(2)}, u32[]{:S(2)}) %collective-permute-start.4) | collective-permute-done | bytes 544 | tf_op jit(solution)/shard_map/while/body/eval_jaxpr/ppermute | solution.py:13
  459.9 7.4 %collective-permute-done.4 = f32[128]{0:T(128)S(1)} collective-permute-done((f32[128]{0:T(128)S(1)}, f32[128]{0:T(128)S(1)}, u32[]{:S(2)}, u32[]{:S(2)}) %collective-permute-start.4) | collective-permute-done | bytes 544 | tf_op jit(solution)/shard_map/while/body/eval_jaxpr/ppermute | solution.py:13
  468.8 7.4 %collective-permute-done.4 = f32[128]{0:T(128)S(1)} collective-permute-done((f32[128]{0:T(128)S(1)}, f32[128]{0:T(128)S(1)}, u32[]{:S(2)}, u32[]{:S(2)}) %collective-permute-start.4) | collective-permute-done | bytes 544 | tf_op jit(solution)/shard_map/while/body/eval_jaxpr/ppermute | solution.py:13
  477.6 7.4 %collective-permute-done.4 = f32[128]{0:T(128)S(1)} collective-permute-done((f32[128]{0:T(128)S(1)}, f32[128]{0:T(128)S(1)}, u32[]{:S(2)}, u32[]{:S(2)}) %collective-permute-start.4) | collective-permute-done | bytes 544 | tf_op jit(solution)/shard_map/while/body/eval_jaxpr/ppermute | solution.py:13
  486.5 7.4 %collective-permute-done.4 = f32[128]{0:T(128)S(1)} collective-permute-done((f32[128]{0:T(128)S(1)}, f32[128]{0:T(128)S(1)}, u32[]{:S(2)}, u32[]{:S(2)}) %collective-permute-start.4) | collective-permute-done | bytes 544 | tf_op jit(solution)/shard_map/while/body/eval_jaxpr/ppermute | solution.py:13
  495.4 7.4 %collective-permute-done.4 = f32[128]{0:T(128)S(1)} collective-permute-done((f32[128]{0:T(128)S(1)}, f32[128]{0:T(128)S(1)}, u32[]{:S(2)}, u32[]{:S(2)}) %collective-permute-start.4) | collective-permute-done | bytes 544 | tf_op jit(solution)/shard_map/while/body/eval_jaxpr/ppermute | solution.py:13
  504.2 7.4 %collective-permute-done.4 = f32[128]{0:T(128)S(1)} collective-permute-done((f32[128]{0:T(128)S(1)}, f32[128]{0:T(128)S(1)}, u32[]{:S(2)}, u32[]{:S(2)}) %collective-permute-start.4) | collective-permute-done | bytes 544 | tf_op jit(solution)/shard_map/while/body/eval_jaxpr/ppermute | solution.py:13
  513.1 7.4 %collective-permute-done.4 = f32[128]{0:T(128)S(1)} collective-permute-done((f32[128]{0:T(128)S(1)}, f32[128]{0:T(128)S(1)}, u32[]{:S(2)}, u32[]{:S(2)}) %collective-permute-start.4) | collective-permute-done | bytes 544 | tf_op jit(solution)/shard_map/while/body/eval_jaxpr/ppermute | solution.py:13
  522.0 7.4 %collective-permute-done.4 = f32[128]{0:T(128)S(1)} collective-permute-done((f32[128]{0:T(128)S(1)}, f32[128]{0:T(128)S(1)}, u32[]{:S(2)}, u32[]{:S(2)}) %collective-permute-start.4) | collective-permute-done | bytes 544 | tf_op jit(solution)/shard_map/while/body/eval_jaxpr/ppermute | solution.py:13
  530.8 7.4 %collective-permute-done.4 = f32[128]{0:T(128)S(1)} collective-permute-done((f32[128]{0:T(128)S(1)}, f32[128]{0:T(128)S(1)}, u32[]{:S(2)}, u32[]{:S(2)}) %collective-permute-start.4) | collective-permute-done | bytes 544 | tf_op jit(solution)/shard_map/while/body/eval_jaxpr/ppermute | solution.py:13
  539.7 7.4 %collective-permute-done.4 = f32[128]{0:T(128)S(1)} collective-permute-done((f32[128]{0:T(128)S(1)}, f32[128]{0:T(128)S(1)}, u32[]{:S(2)}, u32[]{:S(2)}) %collective-permute-start.4) | collective-permute-done | bytes 544 | tf_op jit(solution)/shard_map/while/body/eval_jaxpr/ppermute | solution.py:13
  548.6 7.4 %collective-permute-done.4 = f32[128]{0:T(128)S(1)} collective-permute-done((f32[128]{0:T(128)S(1)}, f32[128]{0:T(128)S(1)}, u32[]{:S(2)}, u32[]{:S(2)}) %collective-permute-start.4) | collective-permute-done | bytes 544 | tf_op jit(solution)/shard_map/while/body/eval_jaxpr/ppermute | solution.py:13
  557.5 7.4 %collective-permute-done.4 = f32[128]{0:T(128)S(1)} collective-permute-done((f32[128]{0:T(128)S(1)}, f32[128]{0:T(128)S(1)}, u32[]{:S(2)}, u32[]{:S(2)}) %collective-permute-start.4) | collective-permute-done | bytes 544 | tf_op jit(solution)/shard_map/while/body/eval_jaxpr/ppermute | solution.py:13
  566.3 7.4 %collective-permute-done.4 = f32[128]{0:T(128)S(1)} collective-permute-done((f32[128]{0:T(128)S(1)}, f32[128]{0:T(128)S(1)}, u32[]{:S(2)}, u32[]{:S(2)}) %collective-permute-start.4) | collective-permute-done | bytes 544 | tf_op jit(solution)/shard_map/while/body/eval_jaxpr/ppermute | solution.py:13
  575.2 7.4 %collective-permute-done.4 = f32[128]{0:T(128)S(1)} collective-permute-done((f32[128]{0:T(128)S(1)}, f32[128]{0:T(128)S(1)}, u32[]{:S(2)}, u32[]{:S(2)}) %collective-permute-start.4) | collective-permute-done | bytes 544 | tf_op jit(solution)/shard_map/while/body/eval_jaxpr/ppermute | solution.py:13
  584.1 7.4 %collective-permute-done.4 = f32[128]{0:T(128)S(1)} collective-permute-done((f32[128]{0:T(128)S(1)}, f32[128]{0:T(128)S(1)}, u32[]{:S(2)}, u32[]{:S(2)}) %collective-permute-start.4) | collective-permute-done | bytes 544 | tf_op jit(solution)/shard_map/while/body/eval_jaxpr/ppermute | solution.py:13
  592.9 7.4 %collective-permute-done.4 = f32[128]{0:T(128)S(1)} collective-permute-done((f32[128]{0:T(128)S(1)}, f32[128]{0:T(128)S(1)}, u32[]{:S(2)}, u32[]{:S(2)}) %collective-permute-start.4) | collective-permute-done | bytes 544 | tf_op jit(solution)/shard_map/while/body/eval_jaxpr/ppermute | solution.py:13
  (714 shorter events, 294.3 us)
Async XLA Ops:
  10.3 9.6 %collective-permute-start = (bf16[128,768]{1,0:T(8,128)(2,1)S(1)}, bf16[128,768]{1,0:T(8,128)(2,1)S(1)}, u32[]{:S(2)}, u32[]{:S(2)}) collective-permute-start(bf16[128,768]{1,0:T(8,128)(2,1)S(1)} %copy.20), channel_id=1, source_target_pairs={{248,0},{0,8},{8,16},{16,24},{24,32},{32,40},{40,48},{48,56},{56,6... | collective-permute-start | bytes 589832 | tf_op jit(solution)/shard_map/while/body/eval_jaxpr/ppermute | solution.py:13
  27.6 9.4 %collective-permute-start = (bf16[128,768]{1,0:T(8,128)(2,1)S(1)}, bf16[128,768]{1,0:T(8,128)(2,1)S(1)}, u32[]{:S(2)}, u32[]{:S(2)}) collective-permute-start(bf16[128,768]{1,0:T(8,128)(2,1)S(1)} %copy.20), channel_id=1, source_target_pairs={{248,0},{0,8},{8,16},{16,24},{24,32},{32,40},{40,48},{48,56},{56,6... | collective-permute-start | bytes 589832 | tf_op jit(solution)/shard_map/while/body/eval_jaxpr/ppermute | solution.py:13
  44.8 9.3 %collective-permute-start = (bf16[128,768]{1,0:T(8,128)(2,1)S(1)}, bf16[128,768]{1,0:T(8,128)(2,1)S(1)}, u32[]{:S(2)}, u32[]{:S(2)}) collective-permute-start(bf16[128,768]{1,0:T(8,128)(2,1)S(1)} %copy.20), channel_id=1, source_target_pairs={{248,0},{0,8},{8,16},{16,24},{24,32},{32,40},{40,48},{48,56},{56,6... | collective-permute-start | bytes 589832 | tf_op jit(solution)/shard_map/while/body/eval_jaxpr/ppermute | solution.py:13
  62.8 10.8 %collective-permute-start = (bf16[128,768]{1,0:T(8,128)(2,1)S(1)}, bf16[128,768]{1,0:T(8,128)(2,1)S(1)}, u32[]{:S(2)}, u32[]{:S(2)}) collective-permute-start(bf16[128,768]{1,0:T(8,128)(2,1)S(1)} %copy.20), channel_id=1, source_target_pairs={{248,0},{0,8},{8,16},{16,24},{24,32},{32,40},{40,48},{48,56},{56,6... | collective-permute-start | bytes 589832 | tf_op jit(solution)/shard_map/while/body/eval_jaxpr/ppermute | solution.py:13
  73.6 8.9 %collective-permute-start = (bf16[128,768]{1,0:T(8,128)(2,1)S(1)}, bf16[128,768]{1,0:T(8,128)(2,1)S(1)}, u32[]{:S(2)}, u32[]{:S(2)}) collective-permute-start(bf16[128,768]{1,0:T(8,128)(2,1)S(1)} %copy.20), channel_id=1, source_target_pairs={{248,0},{0,8},{8,16},{16,24},{24,32},{32,40},{40,48},{48,56},{56,6... | collective-permute-start | bytes 589832 | tf_op jit(solution)/shard_map/while/body/eval_jaxpr/ppermute | solution.py:13
  82.5 8.9 %collective-permute-start = (bf16[128,768]{1,0:T(8,128)(2,1)S(1)}, bf16[128,768]{1,0:T(8,128)(2,1)S(1)}, u32[]{:S(2)}, u32[]{:S(2)}) collective-permute-start(bf16[128,768]{1,0:T(8,128)(2,1)S(1)} %copy.20), channel_id=1, source_target_pairs={{248,0},{0,8},{8,16},{16,24},{24,32},{32,40},{40,48},{48,56},{56,6... | collective-permute-start | bytes 589832 | tf_op jit(solution)/shard_map/while/body/eval_jaxpr/ppermute | solution.py:13
  91.4 8.9 %collective-permute-start = (bf16[128,768]{1,0:T(8,128)(2,1)S(1)}, bf16[128,768]{1,0:T(8,128)(2,1)S(1)}, u32[]{:S(2)}, u32[]{:S(2)}) collective-permute-start(bf16[128,768]{1,0:T(8,128)(2,1)S(1)} %copy.20), channel_id=1, source_target_pairs={{248,0},{0,8},{8,16},{16,24},{24,32},{32,40},{40,48},{48,56},{56,6... | collective-permute-start | bytes 589832 | tf_op jit(solution)/shard_map/while/body/eval_jaxpr/ppermute | solution.py:13
  100.3 8.9 %collective-permute-start = (bf16[128,768]{1,0:T(8,128)(2,1)S(1)}, bf16[128,768]{1,0:T(8,128)(2,1)S(1)}, u32[]{:S(2)}, u32[]{:S(2)}) collective-permute-start(bf16[128,768]{1,0:T(8,128)(2,1)S(1)} %copy.20), channel_id=1, source_target_pairs={{248,0},{0,8},{8,16},{16,24},{24,32},{32,40},{40,48},{48,56},{56,6... | collective-permute-start | bytes 589832 | tf_op jit(solution)/shard_map/while/body/eval_jaxpr/ppermute | solution.py:13
  109.2 8.9 %collective-permute-start = (bf16[128,768]{1,0:T(8,128)(2,1)S(1)}, bf16[128,768]{1,0:T(8,128)(2,1)S(1)}, u32[]{:S(2)}, u32[]{:S(2)}) collective-permute-start(bf16[128,768]{1,0:T(8,128)(2,1)S(1)} %copy.20), channel_id=1, source_target_pairs={{248,0},{0,8},{8,16},{16,24},{24,32},{32,40},{40,48},{48,56},{56,6... | collective-permute-start | bytes 589832 | tf_op jit(solution)/shard_map/while/body/eval_jaxpr/ppermute | solution.py:13
  118.1 8.9 %collective-permute-start = (bf16[128,768]{1,0:T(8,128)(2,1)S(1)}, bf16[128,768]{1,0:T(8,128)(2,1)S(1)}, u32[]{:S(2)}, u32[]{:S(2)}) collective-permute-start(bf16[128,768]{1,0:T(8,128)(2,1)S(1)} %copy.20), channel_id=1, source_target_pairs={{248,0},{0,8},{8,16},{16,24},{24,32},{32,40},{40,48},{48,56},{56,6... | collective-permute-start | bytes 589832 | tf_op jit(solution)/shard_map/while/body/eval_jaxpr/ppermute | solution.py:13
  127.0 8.9 %collective-permute-start = (bf16[128,768]{1,0:T(8,128)(2,1)S(1)}, bf16[128,768]{1,0:T(8,128)(2,1)S(1)}, u32[]{:S(2)}, u32[]{:S(2)}) collective-permute-start(bf16[128,768]{1,0:T(8,128)(2,1)S(1)} %copy.20), channel_id=1, source_target_pairs={{248,0},{0,8},{8,16},{16,24},{24,32},{32,40},{40,48},{48,56},{56,6... | collective-permute-start | bytes 589832 | tf_op jit(solution)/shard_map/while/body/eval_jaxpr/ppermute | solution.py:13
  135.9 8.9 %collective-permute-start = (bf16[128,768]{1,0:T(8,128)(2,1)S(1)}, bf16[128,768]{1,0:T(8,128)(2,1)S(1)}, u32[]{:S(2)}, u32[]{:S(2)}) collective-permute-start(bf16[128,768]{1,0:T(8,128)(2,1)S(1)} %copy.20), channel_id=1, source_target_pairs={{248,0},{0,8},{8,16},{16,24},{24,32},{32,40},{40,48},{48,56},{56,6... | collective-permute-start | bytes 589832 | tf_op jit(solution)/shard_map/while/body/eval_jaxpr/ppermute | solution.py:13
  144.8 8.9 %collective-permute-start = (bf16[128,768]{1,0:T(8,128)(2,1)S(1)}, bf16[128,768]{1,0:T(8,128)(2,1)S(1)}, u32[]{:S(2)}, u32[]{:S(2)}) collective-permute-start(bf16[128,768]{1,0:T(8,128)(2,1)S(1)} %copy.20), channel_id=1, source_target_pairs={{248,0},{0,8},{8,16},{16,24},{24,32},{32,40},{40,48},{48,56},{56,6... | collective-permute-start | bytes 589832 | tf_op jit(solution)/shard_map/while/body/eval_jaxpr/ppermute | solution.py:13
  153.7 8.9 %collective-permute-start = (bf16[128,768]{1,0:T(8,128)(2,1)S(1)}, bf16[128,768]{1,0:T(8,128)(2,1)S(1)}, u32[]{:S(2)}, u32[]{:S(2)}) collective-permute-start(bf16[128,768]{1,0:T(8,128)(2,1)S(1)} %copy.20), channel_id=1, source_target_pairs={{248,0},{0,8},{8,16},{16,24},{24,32},{32,40},{40,48},{48,56},{56,6... | collective-permute-start | bytes 589832 | tf_op jit(solution)/shard_map/while/body/eval_jaxpr/ppermute | solution.py:13
  162.5 8.9 %collective-permute-start = (bf16[128,768]{1,0:T(8,128)(2,1)S(1)}, bf16[128,768]{1,0:T(8,128)(2,1)S(1)}, u32[]{:S(2)}, u32[]{:S(2)}) collective-permute-start(bf16[128,768]{1,0:T(8,128)(2,1)S(1)} %copy.20), channel_id=1, source_target_pairs={{248,0},{0,8},{8,16},{16,24},{24,32},{32,40},{40,48},{48,56},{56,6... | collective-permute-start | bytes 589832 | tf_op jit(solution)/shard_map/while/body/eval_jaxpr/ppermute | solution.py:13
  171.4 8.9 %collective-permute-start = (bf16[128,768]{1,0:T(8,128)(2,1)S(1)}, bf16[128,768]{1,0:T(8,128)(2,1)S(1)}, u32[]{:S(2)}, u32[]{:S(2)}) collective-permute-start(bf16[128,768]{1,0:T(8,128)(2,1)S(1)} %copy.20), channel_id=1, source_target_pairs={{248,0},{0,8},{8,16},{16,24},{24,32},{32,40},{40,48},{48,56},{56,6... | collective-permute-start | bytes 589832 | tf_op jit(solution)/shard_map/while/body/eval_jaxpr/ppermute | solution.py:13
  180.3 8.9 %collective-permute-start = (bf16[128,768]{1,0:T(8,128)(2,1)S(1)}, bf16[128,768]{1,0:T(8,128)(2,1)S(1)}, u32[]{:S(2)}, u32[]{:S(2)}) collective-permute-start(bf16[128,768]{1,0:T(8,128)(2,1)S(1)} %copy.20), channel_id=1, source_target_pairs={{248,0},{0,8},{8,16},{16,24},{24,32},{32,40},{40,48},{48,56},{56,6... | collective-permute-start | bytes 589832 | tf_op jit(solution)/shard_map/while/body/eval_jaxpr/ppermute | solution.py:13
  189.2 8.9 %collective-permute-start = (bf16[128,768]{1,0:T(8,128)(2,1)S(1)}, bf16[128,768]{1,0:T(8,128)(2,1)S(1)}, u32[]{:S(2)}, u32[]{:S(2)}) collective-permute-start(bf16[128,768]{1,0:T(8,128)(2,1)S(1)} %copy.20), channel_id=1, source_target_pairs={{248,0},{0,8},{8,16},{16,24},{24,32},{32,40},{40,48},{48,56},{56,6... | collective-permute-start | bytes 589832 | tf_op jit(solution)/shard_map/while/body/eval_jaxpr/ppermute | solution.py:13
  198.2 8.9 %collective-permute-start = (bf16[128,768]{1,0:T(8,128)(2,1)S(1)}, bf16[128,768]{1,0:T(8,128)(2,1)S(1)}, u32[]{:S(2)}, u32[]{:S(2)}) collective-permute-start(bf16[128,768]{1,0:T(8,128)(2,1)S(1)} %copy.20), channel_id=1, source_target_pairs={{248,0},{0,8},{8,16},{16,24},{24,32},{32,40},{40,48},{48,56},{56,6... | collective-permute-start | bytes 589832 | tf_op jit(solution)/shard_map/while/body/eval_jaxpr/ppermute | solution.py:13
  207.0 8.9 %collective-permute-start = (bf16[128,768]{1,0:T(8,128)(2,1)S(1)}, bf16[128,768]{1,0:T(8,128)(2,1)S(1)}, u32[]{:S(2)}, u32[]{:S(2)}) collective-permute-start(bf16[128,768]{1,0:T(8,128)(2,1)S(1)} %copy.20), channel_id=1, source_target_pairs={{248,0},{0,8},{8,16},{16,24},{24,32},{32,40},{40,48},{48,56},{56,6... | collective-permute-start | bytes 589832 | tf_op jit(solution)/shard_map/while/body/eval_jaxpr/ppermute | solution.py:13
  215.9 8.9 %collective-permute-start = (bf16[128,768]{1,0:T(8,128)(2,1)S(1)}, bf16[128,768]{1,0:T(8,128)(2,1)S(1)}, u32[]{:S(2)}, u32[]{:S(2)}) collective-permute-start(bf16[128,768]{1,0:T(8,128)(2,1)S(1)} %copy.20), channel_id=1, source_target_pairs={{248,0},{0,8},{8,16},{16,24},{24,32},{32,40},{40,48},{48,56},{56,6... | collective-permute-start | bytes 589832 | tf_op jit(solution)/shard_map/while/body/eval_jaxpr/ppermute | solution.py:13
  224.8 8.9 %collective-permute-start = (bf16[128,768]{1,0:T(8,128)(2,1)S(1)}, bf16[128,768]{1,0:T(8,128)(2,1)S(1)}, u32[]{:S(2)}, u32[]{:S(2)}) collective-permute-start(bf16[128,768]{1,0:T(8,128)(2,1)S(1)} %copy.20), channel_id=1, source_target_pairs={{248,0},{0,8},{8,16},{16,24},{24,32},{32,40},{40,48},{48,56},{56,6... | collective-permute-start | bytes 589832 | tf_op jit(solution)/shard_map/while/body/eval_jaxpr/ppermute | solution.py:13
  233.7 8.9 %collective-permute-start = (bf16[128,768]{1,0:T(8,128)(2,1)S(1)}, bf16[128,768]{1,0:T(8,128)(2,1)S(1)}, u32[]{:S(2)}, u32[]{:S(2)}) collective-permute-start(bf16[128,768]{1,0:T(8,128)(2,1)S(1)} %copy.20), channel_id=1, source_target_pairs={{248,0},{0,8},{8,16},{16,24},{24,32},{32,40},{40,48},{48,56},{56,6... | collective-permute-start | bytes 589832 | tf_op jit(solution)/shard_map/while/body/eval_jaxpr/ppermute | solution.py:13
  242.6 8.9 %collective-permute-start = (bf16[128,768]{1,0:T(8,128)(2,1)S(1)}, bf16[128,768]{1,0:T(8,128)(2,1)S(1)}, u32[]{:S(2)}, u32[]{:S(2)}) collective-permute-start(bf16[128,768]{1,0:T(8,128)(2,1)S(1)} %copy.20), channel_id=1, source_target_pairs={{248,0},{0,8},{8,16},{16,24},{24,32},{32,40},{40,48},{48,56},{56,6... | collective-permute-start | bytes 589832 | tf_op jit(solution)/shard_map/while/body/eval_jaxpr/ppermute | solution.py:13
  251.5 8.9 %collective-permute-start = (bf16[128,768]{1,0:T(8,128)(2,1)S(1)}, bf16[128,768]{1,0:T(8,128)(2,1)S(1)}, u32[]{:S(2)}, u32[]{:S(2)}) collective-permute-start(bf16[128,768]{1,0:T(8,128)(2,1)S(1)} %copy.20), channel_id=1, source_target_pairs={{248,0},{0,8},{8,16},{16,24},{24,32},{32,40},{40,48},{48,56},{56,6... | collective-permute-start | bytes 589832 | tf_op jit(solution)/shard_map/while/body/eval_jaxpr/ppermute | solution.py:13
  260.4 8.9 %collective-permute-start = (bf16[128,768]{1,0:T(8,128)(2,1)S(1)}, bf16[128,768]{1,0:T(8,128)(2,1)S(1)}, u32[]{:S(2)}, u32[]{:S(2)}) collective-permute-start(bf16[128,768]{1,0:T(8,128)(2,1)S(1)} %copy.20), channel_id=1, source_target_pairs={{248,0},{0,8},{8,16},{16,24},{24,32},{32,40},{40,48},{48,56},{56,6... | collective-permute-start | bytes 589832 | tf_op jit(solution)/shard_map/while/body/eval_jaxpr/ppermute | solution.py:13
  269.3 8.9 %collective-permute-start = (bf16[128,768]{1,0:T(8,128)(2,1)S(1)}, bf16[128,768]{1,0:T(8,128)(2,1)S(1)}, u32[]{:S(2)}, u32[]{:S(2)}) collective-permute-start(bf16[128,768]{1,0:T(8,128)(2,1)S(1)} %copy.20), channel_id=1, source_target_pairs={{248,0},{0,8},{8,16},{16,24},{24,32},{32,40},{40,48},{48,56},{56,6... | collective-permute-start | bytes 589832 | tf_op jit(solution)/shard_map/while/body/eval_jaxpr/ppermute | solution.py:13
  278.2 8.9 %collective-permute-start = (bf16[128,768]{1,0:T(8,128)(2,1)S(1)}, bf16[128,768]{1,0:T(8,128)(2,1)S(1)}, u32[]{:S(2)}, u32[]{:S(2)}) collective-permute-start(bf16[128,768]{1,0:T(8,128)(2,1)S(1)} %copy.20), channel_id=1, source_target_pairs={{248,0},{0,8},{8,16},{16,24},{24,32},{32,40},{40,48},{48,56},{56,6... | collective-permute-start | bytes 589832 | tf_op jit(solution)/shard_map/while/body/eval_jaxpr/ppermute | solution.py:13
  313.2 14.3 %collective-permute-start.3 = (bf16[128,768]{1,0:T(8,128)(2,1)S(1)}, bf16[128,768]{1,0:T(8,128)(2,1)S(1)}, u32[]{:S(2)}, u32[]{:S(2)}) collective-permute-start(bf16[128,768]{1,0:T(8,128)(2,1)S(1)} %copy.42), channel_id=1, source_target_pairs={{248,0},{0,8},{8,16},{16,24},{24,32},{32,40},{40,48},{48,56},{56,6... | collective-permute-start | bytes 589832 | tf_op jit(solution)/shard_map/while/body/eval_jaxpr/ppermute | solution.py:13
  334.3 8.9 %collective-permute-start.3 = (bf16[128,768]{1,0:T(8,128)(2,1)S(1)}, bf16[128,768]{1,0:T(8,128)(2,1)S(1)}, u32[]{:S(2)}, u32[]{:S(2)}) collective-permute-start(bf16[128,768]{1,0:T(8,128)(2,1)S(1)} %copy.42), channel_id=1, source_target_pairs={{248,0},{0,8},{8,16},{16,24},{24,32},{32,40},{40,48},{48,56},{56,6... | collective-permute-start | bytes 589832 | tf_op jit(solution)/shard_map/while/body/eval_jaxpr/ppermute | solution.py:13
  343.2 8.9 %collective-permute-start.3 = (bf16[128,768]{1,0:T(8,128)(2,1)S(1)}, bf16[128,768]{1,0:T(8,128)(2,1)S(1)}, u32[]{:S(2)}, u32[]{:S(2)}) collective-permute-start(bf16[128,768]{1,0:T(8,128)(2,1)S(1)} %copy.42), channel_id=1, source_target_pairs={{248,0},{0,8},{8,16},{16,24},{24,32},{32,40},{40,48},{48,56},{56,6... | collective-permute-start | bytes 589832 | tf_op jit(solution)/shard_map/while/body/eval_jaxpr/ppermute | solution.py:13
  352.0 8.9 %collective-permute-start.3 = (bf16[128,768]{1,0:T(8,128)(2,1)S(1)}, bf16[128,768]{1,0:T(8,128)(2,1)S(1)}, u32[]{:S(2)}, u32[]{:S(2)}) collective-permute-start(bf16[128,768]{1,0:T(8,128)(2,1)S(1)} %copy.42), channel_id=1, source_target_pairs={{248,0},{0,8},{8,16},{16,24},{24,32},{32,40},{40,48},{48,56},{56,6... | collective-permute-start | bytes 589832 | tf_op jit(solution)/shard_map/while/body/eval_jaxpr/ppermute | solution.py:13
  360.9 8.9 %collective-permute-start.3 = (bf16[128,768]{1,0:T(8,128)(2,1)S(1)}, bf16[128,768]{1,0:T(8,128)(2,1)S(1)}, u32[]{:S(2)}, u32[]{:S(2)}) collective-permute-start(bf16[128,768]{1,0:T(8,128)(2,1)S(1)} %copy.42), channel_id=1, source_target_pairs={{248,0},{0,8},{8,16},{16,24},{24,32},{32,40},{40,48},{48,56},{56,6... | collective-permute-start | bytes 589832 | tf_op jit(solution)/shard_map/while/body/eval_jaxpr/ppermute | solution.py:13
  369.8 8.9 %collective-permute-start.3 = (bf16[128,768]{1,0:T(8,128)(2,1)S(1)}, bf16[128,768]{1,0:T(8,128)(2,1)S(1)}, u32[]{:S(2)}, u32[]{:S(2)}) collective-permute-start(bf16[128,768]{1,0:T(8,128)(2,1)S(1)} %copy.42), channel_id=1, source_target_pairs={{248,0},{0,8},{8,16},{16,24},{24,32},{32,40},{40,48},{48,56},{56,6... | collective-permute-start | bytes 589832 | tf_op jit(solution)/shard_map/while/body/eval_jaxpr/ppermute | solution.py:13
  378.7 8.9 %collective-permute-start.3 = (bf16[128,768]{1,0:T(8,128)(2,1)S(1)}, bf16[128,768]{1,0:T(8,128)(2,1)S(1)}, u32[]{:S(2)}, u32[]{:S(2)}) collective-permute-start(bf16[128,768]{1,0:T(8,128)(2,1)S(1)} %copy.42), channel_id=1, source_target_pairs={{248,0},{0,8},{8,16},{16,24},{24,32},{32,40},{40,48},{48,56},{56,6... | collective-permute-start | bytes 589832 | tf_op jit(solution)/shard_map/while/body/eval_jaxpr/ppermute | solution.py:13
  387.5 8.9 %collective-permute-start.3 = (bf16[128,768]{1,0:T(8,128)(2,1)S(1)}, bf16[128,768]{1,0:T(8,128)(2,1)S(1)}, u32[]{:S(2)}, u32[]{:S(2)}) collective-permute-start(bf16[128,768]{1,0:T(8,128)(2,1)S(1)} %copy.42), channel_id=1, source_target_pairs={{248,0},{0,8},{8,16},{16,24},{24,32},{32,40},{40,48},{48,56},{56,6... | collective-permute-start | bytes 589832 | tf_op jit(solution)/shard_map/while/body/eval_jaxpr/ppermute | solution.py:13
  396.4 8.9 %collective-permute-start.3 = (bf16[128,768]{1,0:T(8,128)(2,1)S(1)}, bf16[128,768]{1,0:T(8,128)(2,1)S(1)}, u32[]{:S(2)}, u32[]{:S(2)}) collective-permute-start(bf16[128,768]{1,0:T(8,128)(2,1)S(1)} %copy.42), channel_id=1, source_target_pairs={{248,0},{0,8},{8,16},{16,24},{24,32},{32,40},{40,48},{48,56},{56,6... | collective-permute-start | bytes 589832 | tf_op jit(solution)/shard_map/while/body/eval_jaxpr/ppermute | solution.py:13
  405.3 8.9 %collective-permute-start.3 = (bf16[128,768]{1,0:T(8,128)(2,1)S(1)}, bf16[128,768]{1,0:T(8,128)(2,1)S(1)}, u32[]{:S(2)}, u32[]{:S(2)}) collective-permute-start(bf16[128,768]{1,0:T(8,128)(2,1)S(1)} %copy.42), channel_id=1, source_target_pairs={{248,0},{0,8},{8,16},{16,24},{24,32},{32,40},{40,48},{48,56},{56,6... | collective-permute-start | bytes 589832 | tf_op jit(solution)/shard_map/while/body/eval_jaxpr/ppermute | solution.py:13
  414.1 8.9 %collective-permute-start.3 = (bf16[128,768]{1,0:T(8,128)(2,1)S(1)}, bf16[128,768]{1,0:T(8,128)(2,1)S(1)}, u32[]{:S(2)}, u32[]{:S(2)}) collective-permute-start(bf16[128,768]{1,0:T(8,128)(2,1)S(1)} %copy.42), channel_id=1, source_target_pairs={{248,0},{0,8},{8,16},{16,24},{24,32},{32,40},{40,48},{48,56},{56,6... | collective-permute-start | bytes 589832 | tf_op jit(solution)/shard_map/while/body/eval_jaxpr/ppermute | solution.py:13
  423.0 8.9 %collective-permute-start.3 = (bf16[128,768]{1,0:T(8,128)(2,1)S(1)}, bf16[128,768]{1,0:T(8,128)(2,1)S(1)}, u32[]{:S(2)}, u32[]{:S(2)}) collective-permute-start(bf16[128,768]{1,0:T(8,128)(2,1)S(1)} %copy.42), channel_id=1, source_target_pairs={{248,0},{0,8},{8,16},{16,24},{24,32},{32,40},{40,48},{48,56},{56,6... | collective-permute-start | bytes 589832 | tf_op jit(solution)/shard_map/while/body/eval_jaxpr/ppermute | solution.py:13
  431.9 8.9 %collective-permute-start.3 = (bf16[128,768]{1,0:T(8,128)(2,1)S(1)}, bf16[128,768]{1,0:T(8,128)(2,1)S(1)}, u32[]{:S(2)}, u32[]{:S(2)}) collective-permute-start(bf16[128,768]{1,0:T(8,128)(2,1)S(1)} %copy.42), channel_id=1, source_target_pairs={{248,0},{0,8},{8,16},{16,24},{24,32},{32,40},{40,48},{48,56},{56,6... | collective-permute-start | bytes 589832 | tf_op jit(solution)/shard_map/while/body/eval_jaxpr/ppermute | solution.py:13
  440.7 8.9 %collective-permute-start.3 = (bf16[128,768]{1,0:T(8,128)(2,1)S(1)}, bf16[128,768]{1,0:T(8,128)(2,1)S(1)}, u32[]{:S(2)}, u32[]{:S(2)}) collective-permute-start(bf16[128,768]{1,0:T(8,128)(2,1)S(1)} %copy.42), channel_id=1, source_target_pairs={{248,0},{0,8},{8,16},{16,24},{24,32},{32,40},{40,48},{48,56},{56,6... | collective-permute-start | bytes 589832 | tf_op jit(solution)/shard_map/while/body/eval_jaxpr/ppermute | solution.py:13
  449.6 8.9 %collective-permute-start.3 = (bf16[128,768]{1,0:T(8,128)(2,1)S(1)}, bf16[128,768]{1,0:T(8,128)(2,1)S(1)}, u32[]{:S(2)}, u32[]{:S(2)}) collective-permute-start(bf16[128,768]{1,0:T(8,128)(2,1)S(1)} %copy.42), channel_id=1, source_target_pairs={{248,0},{0,8},{8,16},{16,24},{24,32},{32,40},{40,48},{48,56},{56,6... | collective-permute-start | bytes 589832 | tf_op jit(solution)/shard_map/while/body/eval_jaxpr/ppermute | solution.py:13
  458.5 8.9 %collective-permute-start.3 = (bf16[128,768]{1,0:T(8,128)(2,1)S(1)}, bf16[128,768]{1,0:T(8,128)(2,1)S(1)}, u32[]{:S(2)}, u32[]{:S(2)}) collective-permute-start(bf16[128,768]{1,0:T(8,128)(2,1)S(1)} %copy.42), channel_id=1, source_target_pairs={{248,0},{0,8},{8,16},{16,24},{24,32},{32,40},{40,48},{48,56},{56,6... | collective-permute-start | bytes 589832 | tf_op jit(solution)/shard_map/while/body/eval_jaxpr/ppermute | solution.py:13
  467.4 8.9 %collective-permute-start.3 = (bf16[128,768]{1,0:T(8,128)(2,1)S(1)}, bf16[128,768]{1,0:T(8,128)(2,1)S(1)}, u32[]{:S(2)}, u32[]{:S(2)}) collective-permute-start(bf16[128,768]{1,0:T(8,128)(2,1)S(1)} %copy.42), channel_id=1, source_target_pairs={{248,0},{0,8},{8,16},{16,24},{24,32},{32,40},{40,48},{48,56},{56,6... | collective-permute-start | bytes 589832 | tf_op jit(solution)/shard_map/while/body/eval_jaxpr/ppermute | solution.py:13
  476.2 8.9 %collective-permute-start.3 = (bf16[128,768]{1,0:T(8,128)(2,1)S(1)}, bf16[128,768]{1,0:T(8,128)(2,1)S(1)}, u32[]{:S(2)}, u32[]{:S(2)}) collective-permute-start(bf16[128,768]{1,0:T(8,128)(2,1)S(1)} %copy.42), channel_id=1, source_target_pairs={{248,0},{0,8},{8,16},{16,24},{24,32},{32,40},{40,48},{48,56},{56,6... | collective-permute-start | bytes 589832 | tf_op jit(solution)/shard_map/while/body/eval_jaxpr/ppermute | solution.py:13
  485.1 8.9 %collective-permute-start.3 = (bf16[128,768]{1,0:T(8,128)(2,1)S(1)}, bf16[128,768]{1,0:T(8,128)(2,1)S(1)}, u32[]{:S(2)}, u32[]{:S(2)}) collective-permute-start(bf16[128,768]{1,0:T(8,128)(2,1)S(1)} %copy.42), channel_id=1, source_target_pairs={{248,0},{0,8},{8,16},{16,24},{24,32},{32,40},{40,48},{48,56},{56,6... | collective-permute-start | bytes 589832 | tf_op jit(solution)/shard_map/while/body/eval_jaxpr/ppermute | solution.py:13
  494.0 8.9 %collective-permute-start.3 = (bf16[128,768]{1,0:T(8,128)(2,1)S(1)}, bf16[128,768]{1,0:T(8,128)(2,1)S(1)}, u32[]{:S(2)}, u32[]{:S(2)}) collective-permute-start(bf16[128,768]{1,0:T(8,128)(2,1)S(1)} %copy.42), channel_id=1, source_target_pairs={{248,0},{0,8},{8,16},{16,24},{24,32},{32,40},{40,48},{48,56},{56,6... | collective-permute-start | bytes 589832 | tf_op jit(solution)/shard_map/while/body/eval_jaxpr/ppermute | solution.py:13
  (113 other events, 651.0 us)
where the time goes:
time: 609 us; the launch traced here: 602 us
  starting transfers between devices  263 us (43%)
  waiting for transfers between devices  242 us (40%)
  matrix products  49.1 us (8%)
  blocking collectives  25.7 us (4%)
  other arithmetic  17.5 us (3%)
    ppermute x160, starting transfers between devices, from_behind(): return lax.ppermute(block, axis, route)  263 us
    ppermute x160, waiting for transfers between devices, from_behind(): return lax.ppermute(block, axis, route)  242 us
    dot_general x64, matrix products, tile_logits(): dots = jnp.dot(xblock, cblock.T, preferred_element_type=jnp.float32)  29.3 us
    all_gather x2, blocking collectives, combined_all(): everything = jax.tree.map(lambda part: lax.all_gather(part, axis), array)  25.7 us
    dot_general x32, matrix products, assign_block(): lax.dot_general(resp, block, (((0,), (0,)), ((), ())), preferred_element_...  19.8 us
  transfers between devices with their start and end apart: 160, of which 64 were waited for; matrix products, arithmetic and copies ran while one was open for 11% of the time, Pallas kernels for 0%

commit v1 on v0

v1 whole, which is shorter than its diff:
```python
import functools
import math

import jax
import jax.numpy as jnp
from jax import lax
from jax.experimental import pallas as pl
from jax.experimental.pallas import tpu as pltpu
from jax.sharding import PartitionSpec as P

SHARP = 20.0
PRIOR = 0.25
LOG2E = 1.0 / math.log(2.0)
AXES = ("loop", "slab")
X, Y, Z, C = 4, 4, 8, 2
TILE = 256
LANES = 128
MIB = 1 << 20


def place(device):
    loop, slab = divmod(device, Y * 2)
    z, rest = divmod(loop, 4)
    return (2 * (rest // 2) + slab % 2, slab // 2, z, rest % 2)


def device_at(x, y, z, core):
    return (z * 4 + (x // 2) * 2 + core) * (Y * 2) + y * 2 + x % 2


def send(block, target):
    route = [(d, device_at(*target(*place(d)))) for d in range(X * Y * Z * C)]
    return lax.ppermute(block, AXES, route)


def along_z(block, step):
    return send(block, lambda x, y, z, c: (x, y, (z + step) % Z, c))


def to_sibling(block):
    return send(block, lambda x, y, z, c: (x, y, z, 1 - c))


def combine(parts):
    top = functools.reduce(jnp.maximum, parts)
    return top + jnp.log(sum(jnp.exp2(part - top) for part in parts)) * LOG2E


def prepare_kernel(other_ref, own_ref, both_ref, squares_ref):
    half = own_ref.shape[0]
    for at, ref in enumerate((other_ref, own_ref)):
        block = ref[...]
        both_ref[pl.ds(at * half, half), :] = block
        wide = block.astype(jnp.float32)
        squares_ref[pl.ds(at * half, half), :] = jnp.sum(wide * wide, axis=1, keepdims=True)


def prepare(other, own):
    rows, width = own.shape
    return pl.pallas_call(
        prepare_kernel,
        out_shape=(
            jax.ShapeDtypeStruct((2 * rows, width), own.dtype),
            jax.ShapeDtypeStruct((2 * rows, 1), jnp.float32),
        ),
        compiler_params=pltpu.CompilerParams(vmem_limit_bytes=16 * MIB),
        cost_estimate=pl.CostEstimate(flops=4 * rows * width, bytes_accessed=8 * rows * width, transcendentals=0),
    )(other, own)


def logits_kernel(count, *refs):
    blocks = refs[:count]
    cent_ref, csq_ref, logits_ref, group_ref, norm_ref, xsq_ref, high_ref, total_ref = refs[count:]
    step = pl.program_id(0)
    width = cent_ref.shape[1]
    scale = SHARP / width * LOG2E

    @pl.when(step == 0)
    def _():
        for at, ref in enumerate(blocks):
            rows = ref.shape[0]
            block = ref[...]
            group_ref[pl.ds(at * rows, rows), :] = block
            wide = block.astype(jnp.float32)
            squares = jnp.sum(wide * wide, axis=1, keepdims=True)
            xsq_ref[:, pl.ds(at * rows, rows)] = jnp.broadcast_to(squares, (rows, LANES)).T[:8]
        high_ref[...] = jnp.full_like(high_ref, -jnp.inf)
        total_ref[...] = jnp.zeros_like(total_ref)

    dots = lax.dot_general(
        cent_ref[...], group_ref[...], (((1,), (1,)), ((), ())), preferred_element_type=jnp.float32
    )
    logits = -scale * (xsq_ref[:1, :] + csq_ref[...] - 2.0 * dots)
    logits_ref[...] = logits
    before = high_ref[...]
    top = jnp.maximum(before, jnp.max(logits, axis=0, keepdims=True))
    high_ref[...] = top
    total_ref[...] = total_ref[...] * jnp.exp2(before - top) + jnp.sum(
        jnp.exp2(logits - top), axis=0, keepdims=True
    )

    @pl.when(step == pl.num_programs(0) - 1)
    def _():
        norm_ref[...] = high_ref[...] + jnp.log(total_ref[...]) * LOG2E


def logits_of(blocks, cents, csq):
    rows, width = blocks[0].shape
    points = rows * len(blocks)
    count = cents.shape[0]
    whole = lambda i: (0, 0)
    return pl.pallas_call(
        functools.partial(logits_kernel, len(blocks)),
        grid=(count // TILE,),
        in_specs=[pl.BlockSpec((rows, width), whole)] * len(blocks)
        + [pl.BlockSpec((TILE, width), lambda i: (i, 0)), pl.BlockSpec((TILE, 1), lambda i: (i, 0))],
        out_specs=(
            pl.BlockSpec((TILE, points), lambda i: (i, 0)),
            pl.BlockSpec((points, width), whole),
            pl.BlockSpec((1, points), whole),
        ),
        out_shape=(
            jax.ShapeDtypeStruct((count, points), jnp.float32),
            jax.ShapeDtypeStruct((points, width), blocks[0].dtype),
            jax.ShapeDtypeStruct((1, points), jnp.float32),
        ),
        scratch_shapes=[
            pltpu.VMEM((8, points), jnp.float32),
            pltpu.VMEM((1, points), jnp.float32),
            pltpu.VMEM((1, points), jnp.float32),
        ],
        compiler_params=pltpu.CompilerParams(vmem_limit_bytes=20 * MIB),
        cost_estimate=pl.CostEstimate(
            flops=2 * count * points * width, bytes_accessed=4 * count * points, transcendentals=count * points
        ),
    )(*blocks, cents, csq)


def sums_kernel(groups, *refs):
    logits, blocks = refs[:groups], refs[groups : 2 * groups]
    norm_ref, sums_ref, mass_ref = refs[2 * groups :]
    at = 0
    total, mass = None, None
    for lg_ref, x_ref in zip(logits, blocks):
        points = x_ref.shape[0]
        resp = jnp.exp2(lg_ref[...] - norm_ref[:, pl.ds(at, points)]).astype(jnp.bfloat16)
        part = jnp.dot(resp, x_ref[...], preferred_element_type=jnp.float32)
        wide = resp.astype(jnp.float32)
        weight = sum(wide[:, k : k + LANES] for k in range(0, points, LANES))
        total = part if total is None else total + part
        mass = weight if mass is None else mass + weight
        at += points
    sums_ref[...] = total
    mass_ref[...] = jnp.sum(mass, axis=1, keepdims=True)


def sums_of(logits, blocks, norms, half):
    rows = logits[0].shape[0] // 2
    width = blocks[0].shape[1]
    steps = rows // TILE
    points = norms.shape[1]
    return pl.pallas_call(
        functools.partial(sums_kernel, len(blocks)),
        grid=(steps,),
        in_specs=[pl.BlockSpec((TILE, lg.shape[1]), lambda i: (i + half * steps, 0)) for lg in logits]
        + [pl.BlockSpec(x.shape, lambda i: (0, 0)) for x in blocks]
        + [pl.BlockSpec(norms.shape, lambda i: (0, 0))],
        out_specs=(pl.BlockSpec((TILE, width), lambda i: (i, 0)), pl.BlockSpec((TILE, 1), lambda i: (i, 0))),
        out_shape=(
            jax.ShapeDtypeStruct((rows, width), jnp.float32),
            jax.ShapeDtypeStruct((rows, 1), jnp.float32),
        ),
        compiler_params=pltpu.CompilerParams(vmem_limit_bytes=24 * MIB),
        cost_estimate=pl.CostEstimate(
            flops=2 * rows * points * width, bytes_accessed=4 * rows * points, transcendentals=rows * points
        ),
    )(*logits, *blocks, norms)


def shards(points, centroids):
    loop, slab = lax.axis_index("loop"), lax.axis_index("slab")
    z, x_hi = loop // 4, (loop // 2) % 2
    rows = points.shape[0]

    other_cents = to_sibling(centroids)
    cents, csq = prepare(other_cents, centroids)

    across = send(points, lambda x, y, z, c: (3 - x, y, z, c))
    groups = [[points, across]]
    up, down = [points, across], [points, across]
    for _ in range(3):
        up = [along_z(b, 1) for b in up]
        down = [along_z(b, -1) for b in down]
        groups.append(up + down)
    groups.append([along_z(up[0], 1), along_z(down[1], -1)])

    logits, blocks, norms = zip(*(logits_of(g, cents, csq) for g in groups))

    parts = [n.reshape(-1, rows) for n in norms]
    by_offset = [parts[0]]
    by_offset += [parts[k][2:] for k in (1, 2, 3)] + [parts[4]] + [parts[k][:2] for k in (3, 2, 1)]
    local = jnp.concatenate(by_offset).reshape(Z, 2, rows)
    local = jnp.where(x_hi == 0, local, local[:, ::-1])
    local = lax.dynamic_slice_in_dim(jnp.concatenate([local, local]), Z - z, Z, 0).reshape(Z * 2, rows)

    for kinds in (
        [lambda x, y, z, c, k=k: ((x + k) % X, y, z, c) for k in (1, 2, 3)],
        [lambda x, y, z, c, k=k: (x, (y + k) % Y, z, c) for k in (1, 2, 3)],
        [lambda x, y, z, c, k=k: (x, y, z ^ k, c) for k in (1, 2, 3)],
        [lambda x, y, z, c: (x, y, z ^ 4, c)],
    ):
        local = combine([local] + [send(local, target) for target in kinds])

    total = local.reshape(Z, 2, rows)
    total = lax.dynamic_slice_in_dim(jnp.concatenate([total, total]), z, Z, 0)
    total = jnp.where(x_hi == 0, total, total[:, ::-1])
    ordered = [total[0]]
    for k in (1, 2, 3):
        ordered += [total[Z - k], total[k]]
    ordered.append(total[4])
    lognorm = jnp.concatenate(ordered).reshape(1, -1)

    other_sums, other_mass = sums_of(logits, blocks, lognorm, 0)
    got_sums, got_mass = to_sibling(other_sums), to_sibling(other_mass)
    sums, mass = sums_of(logits, blocks, lognorm, 1)
    sums, mass = sums + got_sums, mass + got_mass
    return (sums + PRIOR * centroids.astype(jnp.float32)) / (mass + PRIOR)


def solution(mesh):
    return jax.shard_map(
        shards,
        mesh=mesh,
        in_specs=(P("loop", None), P(("loop", "slab"), None)),
        out_specs=P(("loop", "slab"), None),
        check_vma=False,
    )
```

time: 609 us -> 115 us (0.19); the launches traced: 602 us -> 114 us
  waiting for transfers between devices: 242 us -> 23.5 us
  starting transfers between devices: 263 us -> 47.3 us
  matrix products: 49.1 us -> 0 us
  blocking collectives: 25.7 us -> 0 us
  local copies, waits for them, and re-layouts: 2.03 us -> 23.8 us
  Pallas kernels: 0 us -> 16.2 us
  other arithmetic: 17.5 us -> 3.1 us
    ppermute x160 -> x28, waiting for transfers between devices: 242 us -> 23.5 us  [send(): return lax.ppermute(block, AXES, route)]
    ppermute x160 -> x28, starting transfers between devices: 263 us -> 47.3 us  [send(): return lax.ppermute(block, AXES, route)]
    dot_general x96 -> x0, matrix products: 49.1 us -> none  [the longest x64 29.3 us: tile_logits(): dots = jnp.dot(xblock, cblock.T, preferred_element_type=jnp.float32)]
    all_gather x2 -> x0, blocking collectives: 25.7 us -> none  [combined_all(): everything = jax.tree.map(lambda part: lax.all_gather(part, axis), array)]
    unnamed x4 -> x54, local copies, waits for them, and re-layouts: 1.02 us -> 17.8 us
    pallas_call x0 -> x8, Pallas kernels: none -> 16.2 us  [the longest x5 11.7 us: logits_of(): pl.pallas_call(functools.partial(logits_kernel, len(blocks)), grid=(count...]
    dot_general x65 -> x0, other arithmetic: 9.07 us -> none  [row_squares(): jnp.einsum('pd,pd->p', block, block, preferred_element_type=jnp.float32)]
  transfers between devices with their start and end apart: 160 -> 28, of which waited for: 64 -> 12; matrix products, arithmetic and copies ran while one was open for 11% -> 2% of each run, Pallas kernels for 0% -> 11%
where the time goes in v1:
time: 115 us; the launch traced here: 114 us
  starting transfers between devices  47.3 us (41%)
  local copies, waits for them, and re-layouts  23.8 us (21%)
  waiting for transfers between devices  23.5 us (20%)
  Pallas kernels  16.2 us (14%)
  other arithmetic  3.1 us (3%)
    ppermute x28, starting transfers between devices, send(): return lax.ppermute(block, AXES, route)  47.3 us
    ppermute x28, waiting for transfers between devices, send(): return lax.ppermute(block, AXES, route)  23.5 us
    unnamed x54, local copies, waits for them, and re-layouts  17.8 us
    pallas_call x5, Pallas kernels, logits_of(): pl.pallas_call(functools.partial(logits_kernel, len(blocks)), grid=(count...  11.7 us
    pallas_call x2, Pallas kernels, sums_of(): pl.pallas_call(functools.partial(sums_kernel, len(blocks)), grid=(steps,)...  4.08 us
  transfers between devices with their start and end apart: 28, of which 12 were waited for; matrix products, arithmetic and copies ran while one was open for 2% of the time, Pallas kernels for 11%

profile of v1, /device:TPU:1, one launch (start us, length us, event | category | flops | bytes accessed | tf_op | source)
XLA Modules:
  0.0 114.1 jit_solution(4782616043000708463)
XLA Ops:
  0.0 3.2 %collective-permute-start.1 = (bf16[512,768]{1,0:T(8,128)(2,1)}, bf16[512,768]{1,0:T(8,128)(2,1)S(1)}, u32[]{:S(2)}, u32[]{:S(2)}) collective-permute-start(bf16[512,768]{1,0:T(8,128)(2,1)} %own_ref.1), channel_id=1, source_target_pairs={{0,8},{1,9},{2,10},{3,11},{4,12},{5,13},{6,14},{7,15},{8,0},{9,1},... | collective-permute-start | bytes 2359304 | tf_op jit(solution)/shard_map/ppermute | solution.py:33
  3.2 0.7 collective-permute-start
  4.0 1.6 %collective-permute-start.2 = (bf16[128,768]{1,0:T(8,128)(2,1)}, bf16[128,768]{1,0:T(8,128)(2,1)S(1)}, u32[]{:S(2)}, u32[]{:S(2)}) collective-permute-start(bf16[128,768]{1,0:T(8,128)(2,1)} %refs_0_.1), channel_id=1, source_target_pairs={{0,32},{1,33},{2,34},{3,35},{4,36},{5,37},{6,38},{7,39},{8,40},{9,... | collective-permute-start | bytes 589832 | tf_op jit(solution)/shard_map/ppermute | solution.py:33
  5.6 3.9 %collective-permute-start.4 = (bf16[128,768]{1,0:T(8,128)(2,1)}, bf16[128,768]{1,0:T(8,128)(2,1)S(1)}, u32[]{:S(2)}, u32[]{:S(2)}) collective-permute-start(bf16[128,768]{1,0:T(8,128)(2,1)} %refs_0_.1), channel_id=1, source_target_pairs={{0,224},{1,225},{2,226},{3,227},{4,228},{5,229},{6,230},{7,231},{8... | collective-permute-start | bytes 589832 | tf_op jit(solution)/shard_map/ppermute | solution.py:33
  9.6 1.6 %collective-permute-done.refs_1_ = bf16[128,768]{1,0:T(8,128)(2,1)S(1)} collective-permute-done((bf16[128,768]{1,0:T(8,128)(2,1)}, bf16[128,768]{1,0:T(8,128)(2,1)S(1)}, u32[]{:S(2)}, u32[]{:S(2)}) %collective-permute-start) | collective-permute-done | bytes 196640 | tf_op jit(solution)/shard_map/ppermute | solution.py:33
  11.2 3.8 %collective-permute-start.5 = (bf16[128,768]{1,0:T(8,128)(2,1)S(1)}, bf16[128,768]{1,0:T(8,128)(2,1)S(1)}, u32[]{:S(2)}, u32[]{:S(2)}) collective-permute-start(bf16[128,768]{1,0:T(8,128)(2,1)S(1)} %collective-permute-done.refs_1_), channel_id=1, source_target_pairs={{0,224},{1,225},{2,226},{3,227},{4,228},{5,229},{6,230},{7,231},{8... | collective-permute-start | bytes 589832 | tf_op jit(solution)/shard_map/ppermute | solution.py:33
  16.4 2.7 %collective-permute-start.8 = (bf16[128,768]{1,0:T(8,128)(2,1)S(1)}, bf16[128,768]{1,0:T(8,128)(2,1)S(1)}, u32[]{:S(2)}, u32[]{:S(2)}) collective-permute-start(bf16[128,768]{1,0:T(8,128)(2,1)S(1)} %collective-permute-done.4.refs_2_), channel_id=1, source_target_pairs={{0,224},{1,225},{2,226},{3,227},{4,228},{5,229},{6,230},{7,231},{8... | collective-permute-start | bytes 589832 | tf_op jit(solution)/shard_map/ppermute | solution.py:33
  19.8 2.1 %collective-permute-start.9 = (bf16[128,768]{1,0:T(8,128)(2,1)S(1)}, bf16[128,768]{1,0:T(8,128)(2,1)S(1)}, u32[]{:S(2)}, u32[]{:S(2)}) collective-permute-start(bf16[128,768]{1,0:T(8,128)(2,1)S(1)} %collective-permute-done.5.refs_3_), channel_id=1, source_target_pairs={{0,224},{1,225},{2,226},{3,227},{4,228},{5,229},{6,230},{7,231},{8... | collective-permute-start | bytes 589832 | tf_op jit(solution)/shard_map/ppermute | solution.py:33
  23.2 2.5 %collective-permute-done.6.refs_0_ = bf16[128,768]{1,0:T(8,128)(2,1)S(1)} collective-permute-done((bf16[128,768]{1,0:T(8,128)(2,1)S(1)}, bf16[128,768]{1,0:T(8,128)(2,1)S(1)}, u32[]{:S(2)}, u32[]{:S(2)}) %collective-permute-start.6) | collective-permute-done | bytes 196640 | tf_op jit(solution)/shard_map/ppermute | solution.py:33
  25.8 2.7 %collective-permute-start.12 = (bf16[128,768]{1,0:T(8,128)(2,1)S(1)}, bf16[128,768]{1,0:T(8,128)(2,1)S(1)}, u32[]{:S(2)}, u32[]{:S(2)}) collective-permute-start(bf16[128,768]{1,0:T(8,128)(2,1)S(1)} %collective-permute-done.8.refs_2_), channel_id=1, source_target_pairs={{0,224},{1,225},{2,226},{3,227},{4,228},{5,229},{6,230},{7,231},{8... | collective-permute-start | bytes 589832 | tf_op jit(solution)/shard_map/ppermute | solution.py:33
  28.5 1.5 %collective-permute-start.13 = (bf16[128,768]{1,0:T(8,128)(2,1)S(1)}, bf16[128,768]{1,0:T(8,128)(2,1)}, u32[]{:S(2)}, u32[]{:S(2)}) collective-permute-start(bf16[128,768]{1,0:T(8,128)(2,1)S(1)} %collective-permute-done.9.refs_3_), channel_id=1, source_target_pairs={{0,224},{1,225},{2,226},{3,227},{4,228},{5,229},{6,230},{7,231},{8... | collective-permute-start | bytes 589832 | tf_op jit(solution)/shard_map/ppermute | solution.py:33
  30.0 4.0 %collective-permute-done.10.refs_0_ = bf16[128,768]{1,0:T(8,128)(2,1)} collective-permute-done((bf16[128,768]{1,0:T(8,128)(2,1)S(1)}, bf16[128,768]{1,0:T(8,128)(2,1)}, u32[]{:S(2)}, u32[]{:S(2)}) %collective-permute-start.10) | collective-permute-done | bytes 196640 | tf_op jit(solution)/shard_map/ppermute | solution.py:33
  34.0 1.1 copy-done.12
  35.6 2.2 %collective-permute-done.11.refs_1_ = bf16[128,768]{1,0:T(8,128)(2,1)S(1)} collective-permute-done((bf16[128,768]{1,0:T(8,128)(2,1)S(1)}, bf16[128,768]{1,0:T(8,128)(2,1)S(1)}, u32[]{:S(2)}, u32[]{:S(2)}) %collective-permute-start.11) | collective-permute-done | bytes 196640 | tf_op jit(solution)/shard_map/ppermute | solution.py:33
  37.8 3.4 %shard_map.32 = (f32[1024,512]{1,0:T(8,128)S(1)}, bf16[512,768]{1,0:T(8,128)(2,1)S(1)}, f32[1,512]{1,0:T(1,128)S(1)}) custom-call(bf16[128,768]{1,0:T(8,128)(2,1)} %collective-permute-done.10.refs_0_, bf16[128,768]{1,0:T(8,128)(2,1)S(1)} %collective-permute-done.11.refs_1_, bf16[128,768]{1,0:T(8,128)(2,1)S(1)} %collective-permute-done.12.refs_2_, ...), custom_call_target="tpu_custom_call" | custom-call | flops 805306368 | bytes 2097152 | tf_op jit(solution)/shard_map/pallas_call | solution.py:112
  41.8 2.4 %shard_map.31 = (f32[1024,512]{1,0:T(8,128)S(1)}, bf16[512,768]{1,0:T(8,128)(2,1)S(1)}, f32[1,512]{1,0:T(1,128)S(1)}) custom-call(bf16[128,768]{1,0:T(8,128)(2,1)S(1)} %collective-permute-done.6.refs_0_, bf16[128,768]{1,0:T(8,128)(2,1)S(1)} %collective-permute-done.7.refs_1_, bf16[128,768]{1,0:T(8,128)(2,1)S(1)} %collective-permute-done.8.refs_2_, ...), custom_call_target="tpu_custom_call" | custom-call | flops 805306368 | bytes 2097152 | tf_op jit(solution)/shard_map/pallas_call | solution.py:112
  44.2 1.3 %copy-done = f32[1024,512]{1,0:T(8,128)} copy-done((f32[1024,512]{1,0:T(8,128)}, f32[1024,512]{1,0:T(8,128)S(1)}, u32[]{:S(2)}) %copy-start) | copy-done | bytes 2097176
  46.6 1.8 %shard_map.29 = (f32[1024,256]{1,0:T(8,128)S(1)}, bf16[256,768]{1,0:T(8,128)(2,1)S(1)}, f32[1,256]{1,0:T(1,128)S(1)}) custom-call(bf16[128,768]{1,0:T(8,128)(2,1)S(1)} %copy-done.16, bf16[128,768]{1,0:T(8,128)(2,1)S(1)} %copy-done.18, bf16[1024,768]{1,0:T(8,128)(2,1)S(1)} %get-tuple-element.26.refs_2_.refs_4_, f32[1024,1]{1,0:T(8,128)S(1)} %get-tuple-element.27.refs_3_.refs_5_), custom_call_target="tpu_custom_call" | custom-call | flops 402653184 | bytes 1048576 | tf_op jit(solution)/shard_map/pallas_call | solution.py:112
  48.5 2.4 %shard_map.30 = (f32[1024,512]{1,0:T(8,128)S(1)}, bf16[512,768]{1,0:T(8,128)(2,1)S(1)}, f32[1,512]{1,0:T(1,128)S(1)}) custom-call(bf16[128,768]{1,0:T(8,128)(2,1)S(1)} %copy-done.20, bf16[128,768]{1,0:T(8,128)(2,1)S(1)} %copy-done.26, bf16[128,768]{1,0:T(8,128)(2,1)S(1)} %copy-done.22, bf16[128,768]{1,0:T(8,128)(2,1)S(1)} %copy-done.24, ...), custom_call_target="tpu_custom_call" | custom-call | flops 805306368 | bytes 2097152 | tf_op jit(solution)/shard_map/pallas_call | solution.py:112
  50.9 1.4 %copy-done.2 = f32[1024,512]{1,0:T(8,128)} copy-done((f32[1024,512]{1,0:T(8,128)}, f32[1024,512]{1,0:T(8,128)S(1)}, u32[]{:S(2)}) %copy-start.2) | copy-done | bytes 2097176
  52.9 1.8 %shard_map.33 = (f32[1024,256]{1,0:T(8,128)S(1)}, bf16[256,768]{1,0:T(8,128)(2,1)S(1)}, f32[1,256]{1,0:T(1,128)S(1)}) custom-call(bf16[128,768]{1,0:T(8,128)(2,1)S(1)} %collective-permute-done.14.refs_0_, bf16[128,768]{1,0:T(8,128)(2,1)S(1)} %collective-permute-done.15.refs_1_, bf16[1024,768]{1,0:T(8,128)(2,1)S(1)} %get-tuple-element.26.refs_2_.refs_4_, ...), custom_call_target="tpu_custom_call" | custom-call | flops 402653184 | bytes 1048576 | tf_op jit(solution)/shard_map/pallas_call | solution.py:112
  54.7 1.0 copy-done.4
  55.7 0.7 copy-done.14
  56.4 1.4 %concatenate.12 = f32[16,128]{1,0:T(8,128)S(1)} concatenate(f32[2,128]{1,0:T(2,128)S(1)} %bitcast.33, f32[2,128]{1,0:T(2,128)} %bitcast.50, f32[2,128]{1,0:T(2,128)} %bitcast.48, f32[2,128]{1,0:T(2,128)} %bitcast.46, f32[2,128]{1,0:T(2,128)S(1)} %bitcast.34, f32[2,128]{1,0:T(2,128)} %bitcast.45, f32[2,128]{1,0:T(2,128)} %bitcast.47, f32[2,128]{1,0:T(2,128)} %bitcast.49), dimensions={0} | concatenate | bytes 16384 | tf_op jit(solution)/shard_map/concatenate | solution.py:202
  57.9 2.6 %collective-permute-start.18 = (f32[16,128]{1,0:T(8,128)S(1)}, f32[16,128]{1,0:T(8,128)S(1)}, u32[]{:S(2)}, u32[]{:S(2)}) collective-permute-start(f32[16,128]{1,0:T(8,128)S(1)} %bitcast.39), channel_id=1, source_target_pairs={{0,17},{1,0},{2,19},{3,2},{4,21},{5,4},{6,23},{7,6},{8,25},{9,8},{... | collective-permute-start | bytes 24584 | tf_op jit(solution)/shard_map/ppermute | solution.py:33
  61.3 3.2 %collective-permute-done.17 = f32[16,128]{1,0:T(8,128)S(1)} collective-permute-done((f32[16,128]{1,0:T(8,128)S(1)}, f32[16,128]{1,0:T(8,128)S(1)}, u32[]{:S(2)}, u32[]{:S(2)}) %collective-permute-start.17) | collective-permute-done | bytes 8224 | tf_op jit(solution)/shard_map/ppermute | solution.py:33
  64.5 2.8 %collective-permute-start.21 = (f32[16,128]{1,0:T(8,128)S(1)}, f32[16,128]{1,0:T(8,128)S(1)}, u32[]{:S(2)}, u32[]{:S(2)}) collective-permute-start(f32[16,128]{1,0:T(8,128)S(1)} %multiply_add_fusion.3), channel_id=1, source_target_pairs={{0,6},{1,7},{2,0},{3,1},{4,2},{5,3},{6,4},{7,5},{8,14},{9,15},{10,... | collective-permute-start | bytes 24584 | tf_op jit(solution)/shard_map/ppermute | solution.py:33
  68.4 3.0 %collective-permute-done.20 = f32[16,128]{1,0:T(8,128)S(1)} collective-permute-done((f32[16,128]{1,0:T(8,128)S(1)}, f32[16,128]{1,0:T(8,128)S(1)}, u32[]{:S(2)}, u32[]{:S(2)}) %collective-permute-start.20) | collective-permute-done | bytes 8224 | tf_op jit(solution)/shard_map/ppermute | solution.py:33
  71.5 2.2 %collective-permute-start.23 = (f32[16,128]{1,0:T(8,128)S(1)}, f32[16,128]{1,0:T(8,128)S(1)}, u32[]{:S(2)}, u32[]{:S(2)}) collective-permute-start(f32[16,128]{1,0:T(8,128)S(1)} %multiply_add_fusion.2), channel_id=1, source_target_pairs={{0,64},{1,65},{2,66},{3,67},{4,68},{5,69},{6,70},{7,71},{8,72},{9,... | collective-permute-start | bytes 24584 | tf_op jit(solution)/shard_map/ppermute | solution.py:33
  73.7 1.4 %collective-permute-start.22 = (f32[16,128]{1,0:T(8,128)S(1)}, f32[16,128]{1,0:T(8,128)S(1)}, u32[]{:S(2)}, u32[]{:S(2)}) collective-permute-start(f32[16,128]{1,0:T(8,128)S(1)} %multiply_add_fusion.2), channel_id=1, source_target_pairs={{0,32},{1,33},{2,34},{3,35},{4,36},{5,37},{6,38},{7,39},{8,40},{9,... | collective-permute-start | bytes 24584 | tf_op jit(solution)/shard_map/ppermute | solution.py:33
  75.1 0.8 collective-permute-done.24
  76.2 2.3 %collective-permute-start.25 = (f32[16,128]{1,0:T(8,128)S(1)}, f32[16,128]{1,0:T(8,128)}, u32[]{:S(2)}, u32[]{:S(2)}) collective-permute-start(f32[16,128]{1,0:T(8,128)S(1)} %multiply_add_fusion.1), channel_id=1, source_target_pairs={{0,128},{1,129},{2,130},{3,131},{4,132},{5,133},{6,134},{7,135},{8... | collective-permute-start | bytes 24584 | tf_op jit(solution)/shard_map/ppermute | solution.py:33
  78.5 4.3 %collective-permute-done.25 = f32[16,128]{1,0:T(8,128)} collective-permute-done((f32[16,128]{1,0:T(8,128)S(1)}, f32[16,128]{1,0:T(8,128)}, u32[]{:S(2)}, u32[]{:S(2)}) %collective-permute-start.25) | collective-permute-done | bytes 8224 | tf_op jit(solution)/shard_map/ppermute | solution.py:33
  82.8 0.7 multiply_add_fusion
  84.2 0.7 rev.7
  85.5 1.4 %concatenate.15 = f32[16,128]{1,0:T(8,128)S(1)} concatenate(f32[2,128]{1,0:T(2,128)} %get-tuple-element.54, f32[2,128]{1,0:T(2,128)} %get-tuple-element.53, f32[2,128]{1,0:T(2,128)} %get-tuple-element.52, f32[2,128]{1,0:T(2,128)} %get-tuple-element.51, f32[2,128]{1,0:T(2,128)} %get-tuple-element.50, f32[2,128]{1,0:T(2,128)} %get-tuple-element.49, ...), dimensions={0} | concatenate | bytes 16384 | tf_op jit(solution)/shard_map/concatenate | solution.py:221
  86.9 1.6 %copy-done.1 = f32[1024,512]{1,0:T(8,128)S(1)} copy-done((f32[1024,512]{1,0:T(8,128)S(1)}, f32[1024,512]{1,0:T(8,128)}, u32[]{:S(2)}) %copy-start.1) | copy-done | bytes 2097176
  88.5 1.6 %copy-done.3 = f32[1024,512]{1,0:T(8,128)S(1)} copy-done((f32[1024,512]{1,0:T(8,128)S(1)}, f32[1024,512]{1,0:T(8,128)}, u32[]{:S(2)}) %copy-start.3) | copy-done | bytes 2097176
  90.1 1.2 %copy-done.5 = f32[1024,256]{1,0:T(8,128)S(1)} copy-done((f32[1024,256]{1,0:T(8,128)S(1)}, f32[1024,256]{1,0:T(8,128)}, u32[]{:S(2)}) %copy-start.5) | copy-done | bytes 1048600
  91.4 1.1 copy-done.7
  92.5 1.1 copy-done.9
  93.6 1.1 copy-done.11
  94.8 1.0 copy-done.15
  95.8 2.0 %shard_map.35 = (f32[512,768]{1,0:T(8,128)S(1)}, f32[512,1]{1,0:T(8,128)S(1)}) custom-call(f32[1024,256]{1,0:T(8,128)S(1)} %get-tuple-element.28.refs_0_, f32[1024,512]{1,0:T(8,128)S(1)} %copy-done.3, f32[1024,512]{1,0:T(8,128)S(1)} %copy-done.1, f32[1024,512]{1,0:T(8,128)S(1)} %get-tuple-element.31.refs_3_, f32[1024,256]{1,0:T(8,128)S(1)} %copy-done.5, ...), custom_call_target="tpu_custom_call" | custom-call | flops 1610612736 | bytes 4194304 | tf_op jit(solution)/shard_map/pallas_call | solution.py:162
  97.8 11.3 %collective-permute-start.26 = (f32[512,768]{1,0:T(8,128)S(1)}, f32[512,768]{1,0:T(8,128)S(1)}, u32[]{:S(2)}, u32[]{:S(2)}) collective-permute-start(f32[512,768]{1,0:T(8,128)S(1)} %get-tuple-element.44), channel_id=1, source_target_pairs={{0,8},{1,9},{2,10},{3,11},{4,12},{5,13},{6,14},{7,15},{8,0},{9,1},... | collective-permute-start | bytes 4718600 | tf_op jit(solution)/shard_map/ppermute | solution.py:33
  109.2 2.0 %shard_map.34 = (f32[512,768]{1,0:T(8,128)S(1)}, f32[512,1]{1,0:T(8,128)S(1)}) custom-call(f32[1024,256]{1,0:T(8,128)S(1)} %get-tuple-element.28.refs_0_, f32[1024,512]{1,0:T(8,128)S(1)} %copy-done.3, f32[1024,512]{1,0:T(8,128)S(1)} %copy-done.1, f32[1024,512]{1,0:T(8,128)S(1)} %get-tuple-element.31.refs_3_, f32[1024,256]{1,0:T(8,128)S(1)} %copy-done.5, ...), custom_call_target="tpu_custom_call" | custom-call | flops 1610612736 | bytes 4194304 | tf_op jit(solution)/shard_map/pallas_call | solution.py:162
  111.2 1.3 %collective-permute-done.27 = f32[512,1]{1,0:T(8,128)S(1)} collective-permute-done((f32[512,1]{1,0:T(8,128)S(1)}, f32[512,1]{1,0:T(8,128)S(1)}, u32[]{:S(2)}, u32[]{:S(2)}) %collective-permute-start.27) | collective-permute-done | bytes 2080 | tf_op jit(solution)/shard_map/ppermute | solution.py:33
  112.7 1.5 %add_divide_fusion = f32[512,768]{1,0:T(8,128)} fusion(bf16[512,768]{1,0:T(8,128)(2,1)S(1)} %copy-done.13, f32[512,768]{1,0:T(8,128)S(1)} %get-tuple-element.43, f32[512,768]{1,0:T(8,128)S(1)} %collective-permute-done.26, f32[512]{0:T(512)S(1)} %add_reduce_fusion), kind=kLoop, calls=%fused_computation | loop fusion | flops 1966080 | bytes 5507072 | tf_op jit(solution)/shard_map/div | solution.py:227
  (88 shorter events, 10.3 us)
Async XLA Ops:
  0.0 34.0 %collective-permute-start.1 = (bf16[512,768]{1,0:T(8,128)(2,1)}, bf16[512,768]{1,0:T(8,128)(2,1)S(1)}, u32[]{:S(2)}, u32[]{:S(2)}) collective-permute-start(bf16[512,768]{1,0:T(8,128)(2,1)} %own_ref.1), channel_id=1, source_target_pairs={{0,8},{1,9},{2,10},{3,11},{4,12},{5,13},{6,14},{7,15},{8,0},{9,1},... | collective-permute-start | bytes 2359304 | tf_op jit(solution)/shard_map/ppermute | solution.py:33
  3.2 8.0 %collective-permute-start = (bf16[128,768]{1,0:T(8,128)(2,1)}, bf16[128,768]{1,0:T(8,128)(2,1)S(1)}, u32[]{:S(2)}, u32[]{:S(2)}) collective-permute-start(bf16[128,768]{1,0:T(8,128)(2,1)} %refs_0_.1), channel_id=1, source_target_pairs={{0,17},{1,16},{2,19},{3,18},{4,21},{5,20},{6,23},{7,22},{8,25},{9,... | collective-permute-start | bytes 589832 | tf_op jit(solution)/shard_map/ppermute | solution.py:33
  4.0 11.7 %collective-permute-start.2 = (bf16[128,768]{1,0:T(8,128)(2,1)}, bf16[128,768]{1,0:T(8,128)(2,1)S(1)}, u32[]{:S(2)}, u32[]{:S(2)}) collective-permute-start(bf16[128,768]{1,0:T(8,128)(2,1)} %refs_0_.1), channel_id=1, source_target_pairs={{0,32},{1,33},{2,34},{3,35},{4,36},{5,37},{6,38},{7,39},{8,40},{9,... | collective-permute-start | bytes 589832 | tf_op jit(solution)/shard_map/ppermute | solution.py:33
  5.6 10.8 %collective-permute-start.4 = (bf16[128,768]{1,0:T(8,128)(2,1)}, bf16[128,768]{1,0:T(8,128)(2,1)S(1)}, u32[]{:S(2)}, u32[]{:S(2)}) collective-permute-start(bf16[128,768]{1,0:T(8,128)(2,1)} %refs_0_.1), channel_id=1, source_target_pairs={{0,224},{1,225},{2,226},{3,227},{4,228},{5,229},{6,230},{7,231},{8... | collective-permute-start | bytes 589832 | tf_op jit(solution)/shard_map/ppermute | solution.py:33
  11.2 8.6 %collective-permute-start.5 = (bf16[128,768]{1,0:T(8,128)(2,1)S(1)}, bf16[128,768]{1,0:T(8,128)(2,1)S(1)}, u32[]{:S(2)}, u32[]{:S(2)}) collective-permute-start(bf16[128,768]{1,0:T(8,128)(2,1)S(1)} %collective-permute-done.refs_1_), channel_id=1, source_target_pairs={{0,224},{1,225},{2,226},{3,227},{4,228},{5,229},{6,230},{7,231},{8... | collective-permute-start | bytes 589832 | tf_op jit(solution)/shard_map/ppermute | solution.py:33
  15.0 7.5 %collective-permute-start.3 = (bf16[128,768]{1,0:T(8,128)(2,1)S(1)}, bf16[128,768]{1,0:T(8,128)(2,1)S(1)}, u32[]{:S(2)}, u32[]{:S(2)}) collective-permute-start(bf16[128,768]{1,0:T(8,128)(2,1)S(1)} %collective-permute-done.refs_1_), channel_id=1, source_target_pairs={{0,32},{1,33},{2,34},{3,35},{4,36},{5,37},{6,38},{7,39},{8,40},{9,... | collective-permute-start | bytes 589832 | tf_op jit(solution)/shard_map/ppermute | solution.py:33
  15.7 10.1 %collective-permute-start.6 = (bf16[128,768]{1,0:T(8,128)(2,1)S(1)}, bf16[128,768]{1,0:T(8,128)(2,1)S(1)}, u32[]{:S(2)}, u32[]{:S(2)}) collective-permute-start(bf16[128,768]{1,0:T(8,128)(2,1)S(1)} %collective-permute-done.2.refs_0_), channel_id=1, source_target_pairs={{0,32},{1,33},{2,34},{3,35},{4,36},{5,37},{6,38},{7,39},{8,40},{9,... | collective-permute-start | bytes 589832 | tf_op jit(solution)/shard_map/ppermute | solution.py:33
  16.4 9.4 %collective-permute-start.8 = (bf16[128,768]{1,0:T(8,128)(2,1)S(1)}, bf16[128,768]{1,0:T(8,128)(2,1)S(1)}, u32[]{:S(2)}, u32[]{:S(2)}) collective-permute-start(bf16[128,768]{1,0:T(8,128)(2,1)S(1)} %collective-permute-done.4.refs_2_), channel_id=1, source_target_pairs={{0,224},{1,225},{2,226},{3,227},{4,228},{5,229},{6,230},{7,231},{8... | collective-permute-start | bytes 589832 | tf_op jit(solution)/shard_map/ppermute | solution.py:33
  19.8 8.7 %collective-permute-start.9 = (bf16[128,768]{1,0:T(8,128)(2,1)S(1)}, bf16[128,768]{1,0:T(8,128)(2,1)S(1)}, u32[]{:S(2)}, u32[]{:S(2)}) collective-permute-start(bf16[128,768]{1,0:T(8,128)(2,1)S(1)} %collective-permute-done.5.refs_3_), channel_id=1, source_target_pairs={{0,224},{1,225},{2,226},{3,227},{4,228},{5,229},{6,230},{7,231},{8... | collective-permute-start | bytes 589832 | tf_op jit(solution)/shard_map/ppermute | solution.py:33
  22.6 7.5 %collective-permute-start.7 = (bf16[128,768]{1,0:T(8,128)(2,1)S(1)}, bf16[128,768]{1,0:T(8,128)(2,1)S(1)}, u32[]{:S(2)}, u32[]{:S(2)}) collective-permute-start(bf16[128,768]{1,0:T(8,128)(2,1)S(1)} %collective-permute-done.3.refs_1_), channel_id=1, source_target_pairs={{0,32},{1,33},{2,34},{3,35},{4,36},{5,37},{6,38},{7,39},{8,40},{9,... | collective-permute-start | bytes 589832 | tf_op jit(solution)/shard_map/ppermute | solution.py:33
  25.8 8.2 %collective-permute-start.10 = (bf16[128,768]{1,0:T(8,128)(2,1)S(1)}, bf16[128,768]{1,0:T(8,128)(2,1)}, u32[]{:S(2)}, u32[]{:S(2)}) collective-permute-start(bf16[128,768]{1,0:T(8,128)(2,1)S(1)} %collective-permute-done.6.refs_0_), channel_id=1, source_target_pairs={{0,32},{1,33},{2,34},{3,35},{4,36},{5,37},{6,38},{7,39},{8,40},{9,... | collective-permute-start | bytes 589832 | tf_op jit(solution)/shard_map/ppermute | solution.py:33
  25.8 9.8 %collective-permute-start.12 = (bf16[128,768]{1,0:T(8,128)(2,1)S(1)}, bf16[128,768]{1,0:T(8,128)(2,1)S(1)}, u32[]{:S(2)}, u32[]{:S(2)}) collective-permute-start(bf16[128,768]{1,0:T(8,128)(2,1)S(1)} %collective-permute-done.8.refs_2_), channel_id=1, source_target_pairs={{0,224},{1,225},{2,226},{3,227},{4,228},{5,229},{6,230},{7,231},{8... | collective-permute-start | bytes 589832 | tf_op jit(solution)/shard_map/ppermute | solution.py:33
  28.5 7.1 %collective-permute-start.13 = (bf16[128,768]{1,0:T(8,128)(2,1)S(1)}, bf16[128,768]{1,0:T(8,128)(2,1)}, u32[]{:S(2)}, u32[]{:S(2)}) collective-permute-start(bf16[128,768]{1,0:T(8,128)(2,1)S(1)} %collective-permute-done.9.refs_3_), channel_id=1, source_target_pairs={{0,224},{1,225},{2,226},{3,227},{4,228},{5,229},{6,230},{7,231},{8... | collective-permute-start | bytes 589832 | tf_op jit(solution)/shard_map/ppermute | solution.py:33
  30.0 7.8 %collective-permute-start.11 = (bf16[128,768]{1,0:T(8,128)(2,1)S(1)}, bf16[128,768]{1,0:T(8,128)(2,1)S(1)}, u32[]{:S(2)}, u32[]{:S(2)}) collective-permute-start(bf16[128,768]{1,0:T(8,128)(2,1)S(1)} %collective-permute-done.7.refs_1_), channel_id=1, source_target_pairs={{0,32},{1,33},{2,34},{3,35},{4,36},{5,37},{6,38},{7,39},{8,40},{9,... | collective-permute-start | bytes 589832 | tf_op jit(solution)/shard_map/ppermute | solution.py:33
  34.0 18.8 %collective-permute-start.14 = (bf16[128,768]{1,0:T(8,128)(2,1)}, bf16[128,768]{1,0:T(8,128)(2,1)S(1)}, u32[]{:S(2)}, u32[]{:S(2)}) collective-permute-start(bf16[128,768]{1,0:T(8,128)(2,1)} %collective-permute-done.10.refs_0_), channel_id=1, source_target_pairs={{0,32},{1,33},{2,34},{3,35},{4,36},{5,37},{6,38},{7,39},{8,40},{9,... | collective-permute-start | bytes 589832 | tf_op jit(solution)/shard_map/ppermute | solution.py:33
  34.0 1.1 copy-start.12
  41.2 7.2 %copy-start.6 = (bf16[512,768]{1,0:T(8,128)(2,1)}, bf16[512,768]{1,0:T(8,128)(2,1)S(1)}, u32[]{:S(2)}) copy-start(bf16[512,768]{1,0:T(8,128)(2,1)S(1)} %get-tuple-element.36.refs_8_) | copy-start | bytes 2359300
  41.2 5.4 %copy-start.16 = (bf16[128,768]{1,0:T(8,128)(2,1)S(1)}, bf16[128,768]{1,0:T(8,128)(2,1)}, u32[]{:S(2)}) copy-start(bf16[128,768]{1,0:T(8,128)(2,1)} %refs_0_.1) | copy-start | bytes 589828
  41.2 5.4 %copy-start.18 = (bf16[128,768]{1,0:T(8,128)(2,1)S(1)}, bf16[128,768]{1,0:T(8,128)(2,1)}, u32[]{:S(2)}) copy-start(bf16[128,768]{1,0:T(8,128)(2,1)} %copy-done.17) | copy-start | bytes 589828
  44.2 1.3 %copy-start = (f32[1024,512]{1,0:T(8,128)}, f32[1024,512]{1,0:T(8,128)S(1)}, u32[]{:S(2)}) copy-start(f32[1024,512]{1,0:T(8,128)S(1)} %get-tuple-element.30.refs_2_) | copy-start | bytes 6291460
  45.5 5.3 %copy-start.8 = (bf16[512,768]{1,0:T(8,128)(2,1)}, bf16[512,768]{1,0:T(8,128)(2,1)S(1)}, u32[]{:S(2)}) copy-start(bf16[512,768]{1,0:T(8,128)(2,1)S(1)} %get-tuple-element.35.refs_7_) | copy-start | bytes 2359300
  45.5 2.9 %copy-start.20 = (bf16[128,768]{1,0:T(8,128)(2,1)S(1)}, bf16[128,768]{1,0:T(8,128)(2,1)}, u32[]{:S(2)}) copy-start(bf16[128,768]{1,0:T(8,128)(2,1)} %copy-done.19) | copy-start | bytes 589828
  45.5 2.9 %copy-start.22 = (bf16[128,768]{1,0:T(8,128)(2,1)S(1)}, bf16[128,768]{1,0:T(8,128)(2,1)}, u32[]{:S(2)}) copy-start(bf16[128,768]{1,0:T(8,128)(2,1)} %copy-done.21) | copy-start | bytes 589828
  45.5 2.9 %copy-start.24 = (bf16[128,768]{1,0:T(8,128)(2,1)S(1)}, bf16[128,768]{1,0:T(8,128)(2,1)}, u32[]{:S(2)}) copy-start(bf16[128,768]{1,0:T(8,128)(2,1)} %copy-done.23) | copy-start | bytes 589828
  45.5 2.9 %copy-start.26 = (bf16[128,768]{1,0:T(8,128)(2,1)S(1)}, bf16[128,768]{1,0:T(8,128)(2,1)}, u32[]{:S(2)}) copy-start(bf16[128,768]{1,0:T(8,128)(2,1)} %copy-done.25) | copy-start | bytes 589828
  46.1 6.8 %collective-permute-start.15 = (bf16[128,768]{1,0:T(8,128)(2,1)}, bf16[128,768]{1,0:T(8,128)(2,1)S(1)}, u32[]{:S(2)}, u32[]{:S(2)}) collective-permute-start(bf16[128,768]{1,0:T(8,128)(2,1)} %collective-permute-done.13.refs_3_), channel_id=1, source_target_pairs={{0,224},{1,225},{2,226},{3,227},{4,228},{5,229},{6,230},{7,231},{8... | collective-permute-start | bytes 589832 | tf_op jit(solution)/shard_map/ppermute | solution.py:33
  50.9 1.4 %copy-start.2 = (f32[1024,512]{1,0:T(8,128)}, f32[1024,512]{1,0:T(8,128)S(1)}, u32[]{:S(2)}) copy-start(f32[1024,512]{1,0:T(8,128)S(1)} %get-tuple-element.29.refs_1_) | copy-start | bytes 6291460
  52.2 2.5 %copy-start.10 = (bf16[512,768]{1,0:T(8,128)(2,1)}, bf16[512,768]{1,0:T(8,128)(2,1)S(1)}, u32[]{:S(2)}) copy-start(bf16[512,768]{1,0:T(8,128)(2,1)S(1)} %get-tuple-element.34.refs_6_) | copy-start | bytes 2359300
  57.9 3.4 %collective-permute-start.18 = (f32[16,128]{1,0:T(8,128)S(1)}, f32[16,128]{1,0:T(8,128)S(1)}, u32[]{:S(2)}, u32[]{:S(2)}) collective-permute-start(f32[16,128]{1,0:T(8,128)S(1)} %bitcast.39), channel_id=1, source_target_pairs={{0,17},{1,0},{2,19},{3,2},{4,21},{5,4},{6,23},{7,6},{8,25},{9,8},{... | collective-permute-start | bytes 24584 | tf_op jit(solution)/shard_map/ppermute | solution.py:33
  60.5 4.0 %collective-permute-start.17 = (f32[16,128]{1,0:T(8,128)S(1)}, f32[16,128]{1,0:T(8,128)S(1)}, u32[]{:S(2)}, u32[]{:S(2)}) collective-permute-start(f32[16,128]{1,0:T(8,128)S(1)} %bitcast.40), channel_id=1, source_target_pairs={{0,16},{1,17},{2,18},{3,19},{4,20},{5,21},{6,22},{7,23},{8,24},{9,... | collective-permute-start | bytes 24584 | tf_op jit(solution)/shard_map/ppermute | solution.py:33
  60.5 4.0 %collective-permute-start.16 = (f32[16,128]{1,0:T(8,128)S(1)}, f32[16,128]{1,0:T(8,128)S(1)}, u32[]{:S(2)}, u32[]{:S(2)}) collective-permute-start(f32[16,128]{1,0:T(8,128)S(1)} %bitcast.41), channel_id=1, source_target_pairs={{0,1},{1,16},{2,3},{3,18},{4,5},{5,20},{6,7},{7,22},{8,9},{9,24},{... | collective-permute-start | bytes 24584 | tf_op jit(solution)/shard_map/ppermute | solution.py:33
  64.5 3.9 %collective-permute-start.21 = (f32[16,128]{1,0:T(8,128)S(1)}, f32[16,128]{1,0:T(8,128)S(1)}, u32[]{:S(2)}, u32[]{:S(2)}) collective-permute-start(f32[16,128]{1,0:T(8,128)S(1)} %multiply_add_fusion.3), channel_id=1, source_target_pairs={{0,6},{1,7},{2,0},{3,1},{4,2},{5,3},{6,4},{7,5},{8,14},{9,15},{10,... | collective-permute-start | bytes 24584 | tf_op jit(solution)/shard_map/ppermute | solution.py:33
  67.3 4.0 %collective-permute-start.20 = (f32[16,128]{1,0:T(8,128)S(1)}, f32[16,128]{1,0:T(8,128)S(1)}, u32[]{:S(2)}, u32[]{:S(2)}) collective-permute-start(f32[16,128]{1,0:T(8,128)S(1)} %multiply_add_fusion.3), channel_id=1, source_target_pairs={{0,4},{1,5},{2,6},{3,7},{4,0},{5,1},{6,2},{7,3},{8,12},{9,13},{10,... | collective-permute-start | bytes 24584 | tf_op jit(solution)/shard_map/ppermute | solution.py:33
  67.7 3.7 %collective-permute-start.19 = (f32[16,128]{1,0:T(8,128)S(1)}, f32[16,128]{1,0:T(8,128)S(1)}, u32[]{:S(2)}, u32[]{:S(2)}) collective-permute-start(f32[16,128]{1,0:T(8,128)S(1)} %multiply_add_fusion.3), channel_id=1, source_target_pairs={{0,2},{1,3},{2,4},{3,5},{4,6},{5,7},{6,0},{7,1},{8,10},{9,11},{10,... | collective-permute-start | bytes 24584 | tf_op jit(solution)/shard_map/ppermute | solution.py:33
  71.4 4.4 %collective-permute-start.24 = (f32[16,128]{1,0:T(8,128)S(1)}, f32[16,128]{1,0:T(8,128)S(1)}, u32[]{:S(2)}, u32[]{:S(2)}) collective-permute-start(f32[16,128]{1,0:T(8,128)S(1)} %multiply_add_fusion.2), channel_id=1, source_target_pairs={{0,96},{1,97},{2,98},{3,99},{4,100},{5,101},{6,102},{7,103},{8,104... | collective-permute-start | bytes 24584 | tf_op jit(solution)/shard_map/ppermute | solution.py:33
  71.5 4.3 %collective-permute-start.23 = (f32[16,128]{1,0:T(8,128)S(1)}, f32[16,128]{1,0:T(8,128)S(1)}, u32[]{:S(2)}, u32[]{:S(2)}) collective-permute-start(f32[16,128]{1,0:T(8,128)S(1)} %multiply_add_fusion.2), channel_id=1, source_target_pairs={{0,64},{1,65},{2,66},{3,67},{4,68},{5,69},{6,70},{7,71},{8,72},{9,... | collective-permute-start | bytes 24584 | tf_op jit(solution)/shard_map/ppermute | solution.py:33
  73.7 2.5 %collective-permute-start.22 = (f32[16,128]{1,0:T(8,128)S(1)}, f32[16,128]{1,0:T(8,128)S(1)}, u32[]{:S(2)}, u32[]{:S(2)}) collective-permute-start(f32[16,128]{1,0:T(8,128)S(1)} %multiply_add_fusion.2), channel_id=1, source_target_pairs={{0,32},{1,33},{2,34},{3,35},{4,36},{5,37},{6,38},{7,39},{8,40},{9,... | collective-permute-start | bytes 24584 | tf_op jit(solution)/shard_map/ppermute | solution.py:33
  76.2 6.6 %collective-permute-start.25 = (f32[16,128]{1,0:T(8,128)S(1)}, f32[16,128]{1,0:T(8,128)}, u32[]{:S(2)}, u32[]{:S(2)}) collective-permute-start(f32[16,128]{1,0:T(8,128)S(1)} %multiply_add_fusion.1), channel_id=1, source_target_pairs={{0,128},{1,129},{2,130},{3,131},{4,132},{5,133},{6,134},{7,135},{8... | collective-permute-start | bytes 24584 | tf_op jit(solution)/shard_map/ppermute | solution.py:33
  86.9 1.6 %copy-start.1 = (f32[1024,512]{1,0:T(8,128)S(1)}, f32[1024,512]{1,0:T(8,128)}, u32[]{:S(2)}) copy-start(f32[1024,512]{1,0:T(8,128)} %copy-done) | copy-start | bytes 6291460
  88.5 1.6 %copy-start.3 = (f32[1024,512]{1,0:T(8,128)S(1)}, f32[1024,512]{1,0:T(8,128)}, u32[]{:S(2)}) copy-start(f32[1024,512]{1,0:T(8,128)} %copy-done.2) | copy-start | bytes 6291460
  90.1 1.2 %copy-start.5 = (f32[1024,256]{1,0:T(8,128)S(1)}, f32[1024,256]{1,0:T(8,128)}, u32[]{:S(2)}) copy-start(f32[1024,256]{1,0:T(8,128)} %copy-done.4) | copy-start | bytes 3145732
  91.4 1.1 copy-start.7
  92.5 1.1 copy-start.9
  93.6 1.1 copy-start.11
  94.8 1.0 copy-start.15
  97.8 14.9 %collective-permute-start.26 = (f32[512,768]{1,0:T(8,128)S(1)}, f32[512,768]{1,0:T(8,128)S(1)}, u32[]{:S(2)}, u32[]{:S(2)}) collective-permute-start(f32[512,768]{1,0:T(8,128)S(1)} %get-tuple-element.44), channel_id=1, source_target_pairs={{0,8},{1,9},{2,10},{3,11},{4,12},{5,13},{6,14},{7,15},{8,0},{9,1},... | collective-permute-start | bytes 4718600 | tf_op jit(solution)/shard_map/ppermute | solution.py:33
  109.1 3.6 %copy-start.13 = (bf16[512,768]{1,0:T(8,128)(2,1)S(1)}, bf16[512,768]{1,0:T(8,128)(2,1)}, u32[]{:S(2)}) copy-start(bf16[512,768]{1,0:T(8,128)(2,1)} %own_ref.1) | copy-start | bytes 2359300
  109.1 3.4 %collective-permute-start.27 = (f32[512,1]{1,0:T(8,128)S(1)}, f32[512,1]{1,0:T(8,128)S(1)}, u32[]{:S(2)}, u32[]{:S(2)}) collective-permute-start(f32[512,1]{1,0:T(8,128)S(1)} %get-tuple-element.46), channel_id=1, source_target_pairs={{0,8},{1,9},{2,10},{3,11},{4,12},{5,13},{6,14},{7,15},{8,0},{9,1},... | collective-permute-start | bytes 6152 | tf_op jit(solution)/shard_map/ppermute | solution.py:33
  (7 other events, 5.1 us)

commit v2 on v0

v2 whole, which is shorter than its diff:
```python
import functools
import math

import jax
import jax.numpy as jnp
from jax import lax
from jax.experimental import pallas as pl
from jax.experimental.pallas import tpu as pltpu
from jax.sharding import PartitionSpec as P

SHARP = 20.0
PRIOR = 0.25
LOG2E = 1.0 / math.log(2.0)
AXES = ("loop", "slab")
X, Y, Z, C = 4, 4, 8, 2
TILE = 256
LANES = 128
MIB = 1 << 20


def place(device):
    loop, slab = divmod(device, Y * 2)
    z, rest = divmod(loop, 4)
    return (2 * (rest // 2) + slab % 2, slab // 2, z, rest % 2)


def device_at(x, y, z, core):
    return (z * 4 + (x // 2) * 2 + core) * (Y * 2) + y * 2 + x % 2


def send(block, target):
    route = [(d, device_at(*target(*place(d)))) for d in range(X * Y * Z * C)]
    return lax.ppermute(block, AXES, route)


def along_z(block, step):
    return send(block, lambda x, y, z, c: (x, y, (z + step) % Z, c))


def to_sibling(block):
    return send(block, lambda x, y, z, c: (x, y, z, 1 - c))


def groups_by(key):
    groups = {}
    for d in range(X * Y * Z * C):
        groups.setdefault(key(*place(d)), []).append(d)
    return list(groups.values())


def here(shape, dtype):
    return pltpu.VMEM(shape, dtype)


def pinned(*arrays):
    return [pltpu.with_memory_space_constraint(a, pltpu.VMEM) for a in arrays]


IN_VMEM = pl.BlockSpec(memory_space=pltpu.VMEM)


def combine(parts):
    top = jnp.max(parts, axis=0)
    return top + jnp.log(jnp.sum(jnp.exp2(parts - top), axis=0)) * LOG2E


def prepare_kernel(other_ref, own_ref, both_ref, bias_ref):
    half, width = own_ref.shape
    for at, ref in enumerate((other_ref, own_ref)):
        block = ref[...]
        both_ref[pl.ds(at * half, half), :] = block
        wide = block.astype(jnp.float32)
        squares = jnp.sum(wide * wide, axis=1, keepdims=True)
        bias_ref[pl.ds(at * half, half), :] = jnp.broadcast_to(squares * (SHARP / width * LOG2E), (half, LANES))


def prepare(other, own):
    rows, width = own.shape
    return pl.pallas_call(
        prepare_kernel,
        in_specs=[IN_VMEM, IN_VMEM],
        out_specs=(IN_VMEM, IN_VMEM),
        out_shape=(here((2 * rows, width), own.dtype), here((2 * rows, LANES), jnp.float32)),
        compiler_params=pltpu.CompilerParams(vmem_limit_bytes=8 * MIB),
        cost_estimate=pl.CostEstimate(flops=4 * rows * width, bytes_accessed=8 * rows * width, transcendentals=0),
    )(other, own)


def logits_kernel(count, first, aliased, *refs):
    blocks = refs[:count]
    cent_ref, bias_ref = refs[count : count + 2]
    logits_ref, group_ref, norm_ref, xsq_ref = refs[count + 2 + 3 * aliased :]
    rows, width = blocks[0].shape
    points = rows * count
    scale = SHARP / width * LOG2E
    columns = pl.ds(first, points)
    for at, ref in enumerate(blocks):
        block = ref[...]
        group_ref[pl.ds(first + at * rows, rows), :] = block
        wide = block.astype(jnp.float32)
        squares = jnp.sum(wide * wide, axis=1, keepdims=True) * scale
        xsq_ref[:, pl.ds(at * rows, rows)] = jnp.broadcast_to(squares, (rows, LANES)).T[:8]
    group = group_ref[columns, :]
    xsq = xsq_ref[:1, :]
    tiles = cent_ref.shape[0] // TILE
    high = None
    for t in range(tiles):
        here_rows = pl.ds(t * TILE, TILE)
        dots = lax.dot_general(
            cent_ref[here_rows, :], group, (((1,), (1,)), ((), ())), preferred_element_type=jnp.float32
        )
        bias = jnp.concatenate([bias_ref[here_rows, :]] * (points // LANES), axis=1)
        logits = 2.0 * scale * dots - (bias + xsq)
        logits_ref[here_rows, columns] = logits
        top = jnp.max(logits, axis=0, keepdims=True)
        high = top if high is None else jnp.maximum(high, top)
    total = None
    for t in range(tiles):
        part = jnp.sum(jnp.exp2(logits_ref[pl.ds(t * TILE, TILE), columns] - high), axis=0, keepdims=True)
        total = part if total is None else total + part
    norm_ref[:, columns] = high + jnp.log(total) * LOG2E


def logits_of(blocks, first, points, cents, bias, before):
    rows, width = blocks[0].shape
    count = cents.shape[0]
    more = rows * len(blocks)
    operands = [*blocks, cents, bias, *before]
    return pl.pallas_call(
        functools.partial(logits_kernel, len(blocks), first, len(before) > 0),
        in_specs=[IN_VMEM] * len(operands),
        out_specs=(IN_VMEM,) * 3,
        out_shape=(
            here((count, points), jnp.float32),
            here((points, width), blocks[0].dtype),
            here((1, points), jnp.float32),
        ),
        input_output_aliases={len(blocks) + 2 + k: k for k in range(len(before))},
        scratch_shapes=[pltpu.VMEM((8, more), jnp.float32)],
        compiler_params=pltpu.CompilerParams(vmem_limit_bytes=8 * MIB),
        cost_estimate=pl.CostEstimate(
            flops=2 * count * more * width, bytes_accessed=4 * count * more, transcendentals=count * more
        ),
    )(*pinned(*operands))


def row_of(offset, other):
    loop = lax.axis_index("loop")
    z, x_hi = loop // 4, (loop // 2) % 2
    plane = lax.rem(z + (offset % Z), Z)
    return 2 * plane + (1 - x_hi if other else x_hi)


def arrange_kernel(order, norm_ref, out_ref):
    for k, (offset, other) in enumerate(order):
        out_ref[pl.ds(row_of(offset, other), 1), :] = norm_ref[:, pl.ds(k * LANES, LANES)]


def arrange(order, norms):
    return pl.pallas_call(
        functools.partial(arrange_kernel, order),
        in_specs=[IN_VMEM],
        out_specs=IN_VMEM,
        out_shape=here((len(order), LANES), jnp.float32),
        compiler_params=pltpu.CompilerParams(vmem_limit_bytes=8 * MIB),
    )(*pinned(norms))


def sums_kernel(order, half, logits_ref, group_ref, norms_ref, cent_ref, out_ref, rows_ref, norm_ref):
    rows, width = cent_ref.shape
    points = group_ref.shape[0]
    rows_ref[...] = combine(norms_ref[...])
    for k, (offset, other) in enumerate(order):
        row = rows_ref[pl.ds(row_of(offset, other), 1), :]
        norm_ref[:, pl.ds(k * LANES, LANES)] = jnp.broadcast_to(row, (8, LANES))
    total, mass = None, None
    deep = 512
    for at in range(0, points, deep):
        columns = pl.ds(at, deep)
        logits = logits_ref[pl.ds(half * rows, rows), columns]
        resp = jnp.exp2(logits - norm_ref[:1, columns]).astype(jnp.bfloat16)
        part = jnp.dot(resp, group_ref[columns, :], preferred_element_type=jnp.float32)
        wide = resp.astype(jnp.float32)
        weight = sum(wide[:, k : k + LANES] for k in range(0, deep, LANES))
        total = part if total is None else total + part
        mass = weight if mass is None else mass + weight
    mass = jnp.sum(mass, axis=1, keepdims=True)
    if half == 1:
        total = total + PRIOR * cent_ref[...].astype(jnp.float32)
        mass = mass + PRIOR
    out_ref[:, pl.ds(0, width)] = total
    out_ref[:, pl.ds(width, LANES)] = jnp.broadcast_to(mass, (rows, LANES))


def sums_of(order, half, logits, blocks, norms, cents):
    rows, width = cents.shape
    points = blocks.shape[0]
    return pl.pallas_call(
        functools.partial(sums_kernel, order, half),
        in_specs=[IN_VMEM] * 4,
        out_specs=IN_VMEM,
        out_shape=here((rows, width + LANES), jnp.float32),
        scratch_shapes=[pltpu.VMEM((len(order), LANES), jnp.float32), pltpu.VMEM((8, points), jnp.float32)],
        compiler_params=pltpu.CompilerParams(vmem_limit_bytes=16 * MIB),
        cost_estimate=pl.CostEstimate(
            flops=2 * rows * points * width, bytes_accessed=4 * rows * points, transcendentals=rows * points
        ),
    )(*pinned(logits, blocks, norms, cents))


def finish_kernel(first_ref, second_ref, out_ref):
    rows, width = out_ref.shape
    here_rows = pl.ds(pl.multiple_of(pl.program_id(0) * rows, rows), rows)
    both = first_ref[here_rows, :] + second_ref[here_rows, :]
    weight = 1.0 / both[:, width:]
    out_ref[...] = both[:, :width] * jnp.concatenate([weight] * (width // LANES), axis=1)


def finish(first, second):
    rows, wide = first.shape
    width = wide - LANES
    return pl.pallas_call(
        finish_kernel,
        grid=(4,),
        in_specs=[IN_VMEM] * 2,
        out_specs=pl.BlockSpec((rows // 4, width), lambda i: (i, 0)),
        out_shape=jax.ShapeDtypeStruct((rows, width), jnp.float32),
        compiler_params=pltpu.CompilerParams(vmem_limit_bytes=8 * MIB),
        cost_estimate=pl.CostEstimate(flops=3 * rows * width, bytes_accessed=4 * rows * width, transcendentals=0),
    )(*pinned(first, second))


def after(arrays, *done):
    return lax.optimization_barrier((arrays, done))[0]


def shards(points, centroids):
    rows = points.shape[0]
    everything = rows * Z * 2

    across = send(points, lambda x, y, z, c: (3 - x, y, z, c))
    cents, bias = prepare(to_sibling(centroids), centroids)

    order, state = [], []

    def take(blocks, places):
        nonlocal state
        first = rows * len(order)
        order.extend(places)
        state = logits_of(blocks, first, everything, cents, bias, state)

    own, far = [points, points], [across, across]
    both_ways = lambda pair: [along_z(pair[0], 1), along_z(pair[1], -1)]
    own = both_ways(own)
    far = both_ways(far)
    take([points, across], [(0, 0), (0, 1)])
    for step in (1, 2, 3):
        if step < 3:
            next_own = both_ways(after(own, state[2]))
        else:
            next_own = [along_z(after(own[0], state[2]), 1)]
        take(own, [(-step, 0), (step, 0)])
        if step < 3:
            next_far = both_ways(after(far, state[2]))
        else:
            next_far = [along_z(after(far[1], state[2]), -1)]
        take(far, [(-step, 1), (step, 1)])
        own, far = next_own, next_far
    take([own[0], far[0]], [(4, 0), (4, 1)])
    logits, blocks, norms = state

    local = arrange(order, norms)
    local = combine(
        jnp.stack([local] + [send(local, lambda x, y, z, c, k=k: ((x + k) % X, y, z, c)) for k in (1, 2, 3)])
    )
    everywhere = jnp.broadcast_to(local[None], (Y * Z,) + local.shape)
    parts = lax.all_to_all(everywhere, AXES, 0, 0, axis_index_groups=groups_by(lambda x, y, z, c: (x, c)))

    other_sums = sums_of(order, 0, logits, blocks, parts, centroids)
    got = to_sibling(other_sums)
    own_sums = sums_of(order, 1, logits, blocks, parts, centroids)
    return finish(own_sums, got)


def solution(mesh):
    return jax.shard_map(
        shards,
        mesh=mesh,
        in_specs=(P("loop", None), P(("loop", "slab"), None)),
        out_specs=P(("loop", "slab"), None),
        check_vma=False,
    )
```

time: 609 us -> 86.4 us (0.14); the launches traced: 602 us -> 86.2 us
  waiting for transfers between devices: 242 us -> 13.7 us
  starting transfers between devices: 263 us -> 39 us
  matrix products: 49.1 us -> 0 us
  other arithmetic: 17.5 us -> 0.03 us
  Pallas kernels: 0 us -> 13 us
  blocking collectives: 25.7 us -> 18.2 us
    ppermute x160 -> x20, waiting for transfers between devices: 242 us -> 13.7 us  [send(): return lax.ppermute(block, AXES, route)]
    ppermute x160 -> x20, starting transfers between devices: 263 us -> 39 us  [send(): return lax.ppermute(block, AXES, route)]
    dot_general x96 -> x0, matrix products: 49.1 us -> none  [the longest x64 29.3 us: tile_logits(): dots = jnp.dot(xblock, cblock.T, preferred_element_type=jnp.float32)]
    all_gather x2 -> x0, blocking collectives: 25.7 us -> none  [combined_all(): everything = jax.tree.map(lambda part: lax.all_gather(part, axis), array)]
    all_to_all x0 -> x1, blocking collectives: none -> 18.2 us  [shards(): lax.all_to_all(everywhere, AXES, 0, 0, axis_index_groups=groups_by(lambda...]
    pallas_call x0 -> x13, Pallas kernels: none -> 13 us  [the longest x8 6.49 us: logits_of(): pl.pallas_call(functools.partial(logits_kernel, len(blocks), first, len(b...]
    dot_general x65 -> x0, other arithmetic: 9.07 us -> none  [row_squares(): jnp.einsum('pd,pd->p', block, block, preferred_element_type=jnp.float32)]
  transfers between devices with their start and end apart: 160 -> 20, of which waited for: 64 -> 10; matrix products, arithmetic and copies ran while one was open for 11% -> 0% of each run, Pallas kernels for 0% -> 10%
where the time goes in v2:
time: 86.4 us; the launch traced here: 86.2 us
  starting transfers between devices  39 us (45%)
  blocking collectives  18.2 us (21%)
  waiting for transfers between devices  13.7 us (16%)
  Pallas kernels  13 us (15%)
  local copies, waits for them, and re-layouts  2.08 us (2%)
    ppermute x20, starting transfers between devices, send(): return lax.ppermute(block, AXES, route)  39 us
    all_to_all x1, blocking collectives, shards(): lax.all_to_all(everywhere, AXES, 0, 0, axis_index_groups=groups_by(lambda...  18.2 us
    ppermute x20, waiting for transfers between devices, send(): return lax.ppermute(block, AXES, route)  13.7 us
    pallas_call x8, Pallas kernels, logits_of(): pl.pallas_call(functools.partial(logits_kernel, len(blocks), first, len(b...  6.49 us
    pallas_call x2, Pallas kernels, sums_of(): pl.pallas_call(functools.partial(sums_kernel, order, half), in_specs=[IN_...  4.29 us
    unnamed x6, local copies, waits for them, and re-layouts  2.06 us
    pallas_call x1, Pallas kernels, finish(): pl.pallas_call(finish_kernel, grid=(4,), in_specs=[IN_VMEM] * 2, out_spec...  1.75 us
  transfers between devices with their start and end apart: 20, of which 10 were waited for; matrix products, arithmetic and copies ran while one was open for 0% of the time, Pallas kernels for 10%

profile of v2, /device:TPU:1, one launch (start us, length us, event | category | flops | bytes accessed | tf_op | source)
XLA Modules:
  0.0 86.2 jit_solution(6663619658779618758)
XLA Ops:
  0.0 3.2 %collective-permute-start.3 = (bf16[512,768]{1,0:T(8,128)(2,1)}, bf16[512,768]{1,0:T(8,128)(2,1)S(1)}, u32[]{:S(2)}, u32[]{:S(2)}) collective-permute-start(bf16[512,768]{1,0:T(8,128)(2,1)} %cent_ref.3), channel_id=1, source_target_pairs={{0,8},{1,9},{2,10},{3,11},{4,12},{5,13},{6,14},{7,15},{8,0},{9,1},... | collective-permute-start | bytes 2359304 | tf_op jit(solution)/shard_map/ppermute | solution.py:33
  3.2 0.7 collective-permute-start.2
  4.0 1.6 %collective-permute-start = (bf16[128,768]{1,0:T(8,128)(2,1)}, bf16[128,768]{1,0:T(8,128)(2,1)S(1)}, u32[]{:S(2)}, u32[]{:S(2)}) collective-permute-start(bf16[128,768]{1,0:T(8,128)(2,1)} %refs_0_.1), channel_id=1, source_target_pairs={{0,32},{1,33},{2,34},{3,35},{4,36},{5,37},{6,38},{7,39},{8,40},{9,... | collective-permute-start | bytes 589832 | tf_op jit(solution)/shard_map/ppermute | solution.py:33
  5.6 3.9 %collective-permute-start.1 = (bf16[128,768]{1,0:T(8,128)(2,1)}, bf16[128,768]{1,0:T(8,128)(2,1)S(1)}, u32[]{:S(2)}, u32[]{:S(2)}) collective-permute-start(bf16[128,768]{1,0:T(8,128)(2,1)} %refs_0_.1), channel_id=1, source_target_pairs={{0,224},{1,225},{2,226},{3,227},{4,228},{5,229},{6,230},{7,231},{8... | collective-permute-start | bytes 589832 | tf_op jit(solution)/shard_map/ppermute | solution.py:33
  9.6 1.6 %collective-permute-done.2.refs_1_ = bf16[128,768]{1,0:T(8,128)(2,1)S(1)} collective-permute-done((bf16[128,768]{1,0:T(8,128)(2,1)}, bf16[128,768]{1,0:T(8,128)(2,1)S(1)}, u32[]{:S(2)}, u32[]{:S(2)}) %collective-permute-start.2) | collective-permute-done | bytes 196640 | tf_op jit(solution)/shard_map/ppermute | solution.py:33
  11.2 0.0 collective-permute-start.6
  11.2 3.8 %collective-permute-start.7 = (bf16[128,768]{1,0:T(8,128)(2,1)S(1)}, bf16[128,768]{1,0:T(8,128)(2,1)S(1)}, u32[]{:S(2)}, u32[]{:S(2)}) collective-permute-start(bf16[128,768]{1,0:T(8,128)(2,1)S(1)} %collective-permute-done.2.refs_1_), channel_id=1, source_target_pairs={{0,224},{1,225},{2,226},{3,227},{4,228},{5,229},{6,230},{7,231},{8... | collective-permute-start | bytes 589832 | tf_op jit(solution)/shard_map/ppermute | solution.py:33
  15.0 0.0 collective-permute-done.3.other_ref
  15.0 1.1 %copy-done = bf16[512,768]{1,0:T(8,128)(2,1)S(1)} copy-done((bf16[512,768]{1,0:T(8,128)(2,1)S(1)}, bf16[512,768]{1,0:T(8,128)(2,1)}, u32[]{:S(2)}) %copy-start) | copy-done | bytes 786456
  16.2 0.4 shard_map.28
  16.6 0.9 %copy-done.2 = bf16[128,768]{1,0:T(8,128)(2,1)S(1)} copy-done((bf16[128,768]{1,0:T(8,128)(2,1)S(1)}, bf16[128,768]{1,0:T(8,128)(2,1)}, u32[]{:S(2)}) %copy-start.2) | copy-done | bytes 196632
  17.5 0.8 shard_map.29
  18.3 0.0 collective-permute-done.refs_0_
  18.3 0.0 collective-permute-done.1.refs_1_
  18.3 0.1 collective-permute-start.4
  18.4 2.7 %collective-permute-start.5 = (bf16[128,768]{1,0:T(8,128)(2,1)S(1)}, bf16[128,768]{1,0:T(8,128)(2,1)S(1)}, u32[]{:S(2)}, u32[]{:S(2)}) collective-permute-start(bf16[128,768]{1,0:T(8,128)(2,1)S(1)} %collective-permute-done.1.refs_1_), channel_id=1, source_target_pairs={{0,224},{1,225},{2,226},{3,227},{4,228},{5,229},{6,230},{7,231},{8... | collective-permute-start | bytes 589832 | tf_op jit(solution)/shard_map/ppermute | solution.py:33
  21.1 0.8 shard_map.30
  21.9 0.0 collective-permute-done.7.refs_1_
  21.9 0.3 collective-permute-start.10
  22.2 1.3 %collective-permute-start.9 = (bf16[128,768]{1,0:T(8,128)(2,1)S(1)}, bf16[128,768]{1,0:T(8,128)(2,1)S(1)}, u32[]{:S(2)}, u32[]{:S(2)}) collective-permute-start(bf16[128,768]{1,0:T(8,128)(2,1)S(1)} %collective-permute-done.6.refs_0_), channel_id=1, source_target_pairs={{0,32},{1,33},{2,34},{3,35},{4,36},{5,37},{6,38},{7,39},{8,40},{9,... | collective-permute-start | bytes 589832 | tf_op jit(solution)/shard_map/ppermute | solution.py:33
  23.5 0.8 shard_map.31
  24.3 0.7 collective-permute-done.4.refs_0_
  25.0 0.0 collective-permute-done.5.refs_1_
  25.0 0.0 collective-permute-start.8
  25.0 2.7 %collective-permute-start.13 = (bf16[128,768]{1,0:T(8,128)(2,1)S(1)}, bf16[128,768]{1,0:T(8,128)(2,1)S(1)}, u32[]{:S(2)}, u32[]{:S(2)}) collective-permute-start(bf16[128,768]{1,0:T(8,128)(2,1)S(1)} %collective-permute-done.5.refs_1_), channel_id=1, source_target_pairs={{0,224},{1,225},{2,226},{3,227},{4,228},{5,229},{6,230},{7,231},{8... | collective-permute-start | bytes 589832 | tf_op jit(solution)/shard_map/ppermute | solution.py:33
  27.6 0.8 shard_map.32
  28.5 0.0 collective-permute-done.10.refs_1_
  28.5 3.1 %collective-permute-start.12 = (bf16[128,768]{1,0:T(8,128)(2,1)S(1)}, bf16[128,768]{1,0:T(8,128)(2,1)S(1)}, u32[]{:S(2)}, u32[]{:S(2)}) collective-permute-start(bf16[128,768]{1,0:T(8,128)(2,1)S(1)} %collective-permute-done.10.refs_1_), channel_id=1, source_target_pairs={{0,224},{1,225},{2,226},{3,227},{4,228},{5,229},{6,230},{7,231},{8... | collective-permute-start | bytes 589832 | tf_op jit(solution)/shard_map/ppermute | solution.py:33
  31.6 0.8 shard_map.33
  32.4 0.7 collective-permute-done.8.refs_0_
  33.1 0.8 shard_map.34
  33.9 2.1 %collective-permute-done.12.refs_1_ = bf16[128,768]{1,0:T(8,128)(2,1)S(1)} collective-permute-done((bf16[128,768]{1,0:T(8,128)(2,1)S(1)}, bf16[128,768]{1,0:T(8,128)(2,1)S(1)}, u32[]{:S(2)}, u32[]{:S(2)}) %collective-permute-start.12) | collective-permute-done | bytes 196640 | tf_op jit(solution)/shard_map/ppermute | solution.py:33
  36.0 3.4 %collective-permute-start.14 = (bf16[128,768]{1,0:T(8,128)(2,1)S(1)}, bf16[128,768]{1,0:T(8,128)(2,1)S(1)}, u32[]{:S(2)}, u32[]{:S(2)}) collective-permute-start(bf16[128,768]{1,0:T(8,128)(2,1)S(1)} %collective-permute-done.12.refs_1_), channel_id=1, source_target_pairs={{0,224},{1,225},{2,226},{3,227},{4,228},{5,229},{6,230},{7,231},{8... | collective-permute-start | bytes 589832 | tf_op jit(solution)/shard_map/ppermute | solution.py:33
  39.4 0.8 shard_map.35
  40.2 1.8 %collective-permute-done.14.refs_1_ = bf16[128,768]{1,0:T(8,128)(2,1)S(1)} collective-permute-done((bf16[128,768]{1,0:T(8,128)(2,1)S(1)}, bf16[128,768]{1,0:T(8,128)(2,1)S(1)}, u32[]{:S(2)}, u32[]{:S(2)}) %collective-permute-start.14) | collective-permute-done | bytes 196640 | tf_op jit(solution)/shard_map/ppermute | solution.py:33
  42.0 3.1 %collective-permute-done.11.refs_0_ = bf16[128,768]{1,0:T(8,128)(2,1)S(1)} collective-permute-done((bf16[128,768]{1,0:T(8,128)(2,1)S(1)}, bf16[128,768]{1,0:T(8,128)(2,1)S(1)}, u32[]{:S(2)}, u32[]{:S(2)}) %collective-permute-start.11) | collective-permute-done | bytes 196640 | tf_op jit(solution)/shard_map/ppermute | solution.py:33
  45.1 0.8 shard_map.36
  46.0 0.1 collective-permute-start.16
  46.1 3.6 %collective-permute-start.17 = (f32[16,128]{1,0:T(8,128)S(1)}, f32[16,128]{1,0:T(8,128)S(1)}, u32[]{:S(2)}, u32[]{:S(2)}) collective-permute-start(f32[16,128]{1,0:T(8,128)S(1)} %shard_map.37), channel_id=1, source_target_pairs={{0,16},{1,17},{2,18},{3,19},{4,20},{5,21},{6,22},{7,23},{8,24},{9,... | collective-permute-start | bytes 24584 | tf_op jit(solution)/shard_map/ppermute | solution.py:33
  49.7 0.1 collective-permute-done.16
  49.8 1.1 %collective-permute-done.17 = f32[16,128]{1,0:T(8,128)S(1)} collective-permute-done((f32[16,128]{1,0:T(8,128)S(1)}, f32[16,128]{1,0:T(8,128)S(1)}, u32[]{:S(2)}, u32[]{:S(2)}) %collective-permute-start.17) | collective-permute-done | bytes 8224 | tf_op jit(solution)/shard_map/ppermute | solution.py:33
  50.8 1.4 %collective-permute-done.18 = f32[16,128]{1,0:T(8,128)S(1)} collective-permute-done((f32[16,128]{1,0:T(8,128)S(1)}, f32[16,128]{1,0:T(8,128)S(1)}, u32[]{:S(2)}, u32[]{:S(2)}) %collective-permute-start.18) | collective-permute-done | bytes 8224 | tf_op jit(solution)/shard_map/ppermute | solution.py:33
  52.3 18.2 %all_to_all.5.norms_ref = f32[32,16,128]{2,1,0:T(8,128)S(1)} all-to-all(f32[32,16,128]{2,1,0:T(8,128)S(1)} %broadcast_in_dim.2), channel_id=1, replica_groups={{0,2,4,6,32,34,36,38,64,66,68,70,96,98,100,102,128,130,132,134,160,162,..., dimensions={0} | all-to-all | bytes 524288 | tf_op jit(solution)/shard_map/all_to_all | solution.py:277
  70.5 2.1 %shard_map.39 = f32[512,896]{1,0:T(8,128)S(1)} custom-call(f32[1024,2048]{1,0:T(8,128)S(1)} %get-tuple-element.74.logits_ref, bf16[2048,768]{1,0:T(8,128)(2,1)S(1)} %get-tuple-element.75.group_ref, f32[32,16,128]{2,1,0:T(8,128)S(1)} %all_to_all.5.norms_ref, bf16[512,768]{1,0:T(8,128)(2,1)S(1)} %copy-done.1), custom_call_target="tpu_custom_call" | custom-call | flops 1610612736 | bytes 4194304 | tf_op jit(solution)/shard_map/pallas_call | solution.py:198
  72.6 8.4 %collective-permute-start.19 = (f32[512,896]{1,0:T(8,128)S(1)}, f32[512,896]{1,0:T(8,128)S(1)}, u32[]{:S(2)}, u32[]{:S(2)}) collective-permute-start(f32[512,896]{1,0:T(8,128)S(1)} %shard_map.39), channel_id=1, source_target_pairs={{0,8},{1,9},{2,10},{3,11},{4,12},{5,13},{6,14},{7,15},{8,0},{9,1},... | collective-permute-start | bytes 5505032 | tf_op jit(solution)/shard_map/ppermute | solution.py:33
  81.0 2.2 %shard_map.38.first_ref = f32[512,896]{1,0:T(8,128)S(1)} custom-call(f32[1024,2048]{1,0:T(8,128)S(1)} %get-tuple-element.74.logits_ref, bf16[2048,768]{1,0:T(8,128)(2,1)S(1)} %get-tuple-element.75.group_ref, f32[32,16,128]{2,1,0:T(8,128)S(1)} %all_to_all.5.norms_ref, bf16[512,768]{1,0:T(8,128)(2,1)S(1)} %copy-done.1), custom_call_target="tpu_custom_call" | custom-call | flops 1610612736 | bytes 4194304 | tf_op jit(solution)/shard_map/pallas_call | solution.py:198
  83.2 1.2 %collective-permute-done.19.second_ref = f32[512,896]{1,0:T(8,128)S(1)} collective-permute-done((f32[512,896]{1,0:T(8,128)S(1)}, f32[512,896]{1,0:T(8,128)S(1)}, u32[]{:S(2)}, u32[]{:S(2)}) %collective-permute-start.19) | collective-permute-done | bytes 1835040 | tf_op jit(solution)/shard_map/ppermute | solution.py:33
  84.5 1.7 %shard_map.40 = f32[512,768]{1,0:T(8,128)} custom-call(f32[512,896]{1,0:T(8,128)S(1)} %shard_map.38.first_ref, f32[512,896]{1,0:T(8,128)S(1)} %collective-permute-done.19.second_ref), custom_call_target="tpu_custom_call" | custom-call | flops 1179648 | bytes 1572864 | tf_op jit(solution)/shard_map/pallas_call | solution.py:222
  (16 shorter events, 0.1 us)
Async XLA Ops:
  0.0 15.0 %collective-permute-start.3 = (bf16[512,768]{1,0:T(8,128)(2,1)}, bf16[512,768]{1,0:T(8,128)(2,1)S(1)}, u32[]{:S(2)}, u32[]{:S(2)}) collective-permute-start(bf16[512,768]{1,0:T(8,128)(2,1)} %cent_ref.3), channel_id=1, source_target_pairs={{0,8},{1,9},{2,10},{3,11},{4,12},{5,13},{6,14},{7,15},{8,0},{9,1},... | collective-permute-start | bytes 2359304 | tf_op jit(solution)/shard_map/ppermute | solution.py:33
  3.2 8.0 %collective-permute-start.2 = (bf16[128,768]{1,0:T(8,128)(2,1)}, bf16[128,768]{1,0:T(8,128)(2,1)S(1)}, u32[]{:S(2)}, u32[]{:S(2)}) collective-permute-start(bf16[128,768]{1,0:T(8,128)(2,1)} %refs_0_.1), channel_id=1, source_target_pairs={{0,17},{1,16},{2,19},{3,18},{4,21},{5,20},{6,23},{7,22},{8,25},{9,... | collective-permute-start | bytes 589832 | tf_op jit(solution)/shard_map/ppermute | solution.py:33
  4.0 14.3 %collective-permute-start = (bf16[128,768]{1,0:T(8,128)(2,1)}, bf16[128,768]{1,0:T(8,128)(2,1)S(1)}, u32[]{:S(2)}, u32[]{:S(2)}) collective-permute-start(bf16[128,768]{1,0:T(8,128)(2,1)} %refs_0_.1), channel_id=1, source_target_pairs={{0,32},{1,33},{2,34},{3,35},{4,36},{5,37},{6,38},{7,39},{8,40},{9,... | collective-permute-start | bytes 589832 | tf_op jit(solution)/shard_map/ppermute | solution.py:33
  5.6 12.7 %collective-permute-start.1 = (bf16[128,768]{1,0:T(8,128)(2,1)}, bf16[128,768]{1,0:T(8,128)(2,1)S(1)}, u32[]{:S(2)}, u32[]{:S(2)}) collective-permute-start(bf16[128,768]{1,0:T(8,128)(2,1)} %refs_0_.1), channel_id=1, source_target_pairs={{0,224},{1,225},{2,226},{3,227},{4,228},{5,229},{6,230},{7,231},{8... | collective-permute-start | bytes 589832 | tf_op jit(solution)/shard_map/ppermute | solution.py:33
  11.2 10.7 %collective-permute-start.6 = (bf16[128,768]{1,0:T(8,128)(2,1)S(1)}, bf16[128,768]{1,0:T(8,128)(2,1)S(1)}, u32[]{:S(2)}, u32[]{:S(2)}) collective-permute-start(bf16[128,768]{1,0:T(8,128)(2,1)S(1)} %collective-permute-done.2.refs_1_), channel_id=1, source_target_pairs={{0,32},{1,33},{2,34},{3,35},{4,36},{5,37},{6,38},{7,39},{8,40},{9,... | collective-permute-start | bytes 589832 | tf_op jit(solution)/shard_map/ppermute | solution.py:33
  11.2 10.7 %collective-permute-start.7 = (bf16[128,768]{1,0:T(8,128)(2,1)S(1)}, bf16[128,768]{1,0:T(8,128)(2,1)S(1)}, u32[]{:S(2)}, u32[]{:S(2)}) collective-permute-start(bf16[128,768]{1,0:T(8,128)(2,1)S(1)} %collective-permute-done.2.refs_1_), channel_id=1, source_target_pairs={{0,224},{1,225},{2,226},{3,227},{4,228},{5,229},{6,230},{7,231},{8... | collective-permute-start | bytes 589832 | tf_op jit(solution)/shard_map/ppermute | solution.py:33
  15.0 1.1 %copy-start = (bf16[512,768]{1,0:T(8,128)(2,1)S(1)}, bf16[512,768]{1,0:T(8,128)(2,1)}, u32[]{:S(2)}) copy-start(bf16[512,768]{1,0:T(8,128)(2,1)} %cent_ref.3) | copy-start | bytes 2359300
  16.6 0.9 %copy-start.2 = (bf16[128,768]{1,0:T(8,128)(2,1)S(1)}, bf16[128,768]{1,0:T(8,128)(2,1)}, u32[]{:S(2)}) copy-start(bf16[128,768]{1,0:T(8,128)(2,1)} %refs_0_.1) | copy-start | bytes 589828
  18.3 6.6 %collective-permute-start.4 = (bf16[128,768]{1,0:T(8,128)(2,1)S(1)}, bf16[128,768]{1,0:T(8,128)(2,1)S(1)}, u32[]{:S(2)}, u32[]{:S(2)}) collective-permute-start(bf16[128,768]{1,0:T(8,128)(2,1)S(1)} %collective-permute-done.refs_0_), channel_id=1, source_target_pairs={{0,32},{1,33},{2,34},{3,35},{4,36},{5,37},{6,38},{7,39},{8,40},{9,... | collective-permute-start | bytes 589832 | tf_op jit(solution)/shard_map/ppermute | solution.py:33
  18.4 6.5 %collective-permute-start.5 = (bf16[128,768]{1,0:T(8,128)(2,1)S(1)}, bf16[128,768]{1,0:T(8,128)(2,1)S(1)}, u32[]{:S(2)}, u32[]{:S(2)}) collective-permute-start(bf16[128,768]{1,0:T(8,128)(2,1)S(1)} %collective-permute-done.1.refs_1_), channel_id=1, source_target_pairs={{0,224},{1,225},{2,226},{3,227},{4,228},{5,229},{6,230},{7,231},{8... | collective-permute-start | bytes 589832 | tf_op jit(solution)/shard_map/ppermute | solution.py:33
  21.9 6.5 %collective-permute-start.10 = (bf16[128,768]{1,0:T(8,128)(2,1)S(1)}, bf16[128,768]{1,0:T(8,128)(2,1)S(1)}, u32[]{:S(2)}, u32[]{:S(2)}) collective-permute-start(bf16[128,768]{1,0:T(8,128)(2,1)S(1)} %collective-permute-done.7.refs_1_), channel_id=1, source_target_pairs={{0,224},{1,225},{2,226},{3,227},{4,228},{5,229},{6,230},{7,231},{8... | collective-permute-start | bytes 589832 | tf_op jit(solution)/shard_map/ppermute | solution.py:33
  22.2 6.2 %collective-permute-start.9 = (bf16[128,768]{1,0:T(8,128)(2,1)S(1)}, bf16[128,768]{1,0:T(8,128)(2,1)S(1)}, u32[]{:S(2)}, u32[]{:S(2)}) collective-permute-start(bf16[128,768]{1,0:T(8,128)(2,1)S(1)} %collective-permute-done.6.refs_0_), channel_id=1, source_target_pairs={{0,32},{1,33},{2,34},{3,35},{4,36},{5,37},{6,38},{7,39},{8,40},{9,... | collective-permute-start | bytes 589832 | tf_op jit(solution)/shard_map/ppermute | solution.py:33
  25.0 8.1 %collective-permute-start.8 = (bf16[128,768]{1,0:T(8,128)(2,1)S(1)}, bf16[128,768]{1,0:T(8,128)(2,1)S(1)}, u32[]{:S(2)}, u32[]{:S(2)}) collective-permute-start(bf16[128,768]{1,0:T(8,128)(2,1)S(1)} %collective-permute-done.4.refs_0_), channel_id=1, source_target_pairs={{0,32},{1,33},{2,34},{3,35},{4,36},{5,37},{6,38},{7,39},{8,40},{9,... | collective-permute-start | bytes 589832 | tf_op jit(solution)/shard_map/ppermute | solution.py:33
  25.0 8.1 %collective-permute-start.13 = (bf16[128,768]{1,0:T(8,128)(2,1)S(1)}, bf16[128,768]{1,0:T(8,128)(2,1)S(1)}, u32[]{:S(2)}, u32[]{:S(2)}) collective-permute-start(bf16[128,768]{1,0:T(8,128)(2,1)S(1)} %collective-permute-done.5.refs_1_), channel_id=1, source_target_pairs={{0,224},{1,225},{2,226},{3,227},{4,228},{5,229},{6,230},{7,231},{8... | collective-permute-start | bytes 589832 | tf_op jit(solution)/shard_map/ppermute | solution.py:33
  28.5 7.5 %collective-permute-start.12 = (bf16[128,768]{1,0:T(8,128)(2,1)S(1)}, bf16[128,768]{1,0:T(8,128)(2,1)S(1)}, u32[]{:S(2)}, u32[]{:S(2)}) collective-permute-start(bf16[128,768]{1,0:T(8,128)(2,1)S(1)} %collective-permute-done.10.refs_1_), channel_id=1, source_target_pairs={{0,224},{1,225},{2,226},{3,227},{4,228},{5,229},{6,230},{7,231},{8... | collective-permute-start | bytes 589832 | tf_op jit(solution)/shard_map/ppermute | solution.py:33
  31.6 7.8 %collective-permute-start.15 = (bf16[128,768]{1,0:T(8,128)(2,1)S(1)}, bf16[128,768]{1,0:T(8,128)(2,1)S(1)}, u32[]{:S(2)}, u32[]{:S(2)}) collective-permute-start(bf16[128,768]{1,0:T(8,128)(2,1)S(1)} %collective-permute-done.9.refs_0_), channel_id=1, source_target_pairs={{0,32},{1,33},{2,34},{3,35},{4,36},{5,37},{6,38},{7,39},{8,40},{9,... | collective-permute-start | bytes 589832 | tf_op jit(solution)/shard_map/ppermute | solution.py:33
  36.0 6.0 %collective-permute-start.14 = (bf16[128,768]{1,0:T(8,128)(2,1)S(1)}, bf16[128,768]{1,0:T(8,128)(2,1)S(1)}, u32[]{:S(2)}, u32[]{:S(2)}) collective-permute-start(bf16[128,768]{1,0:T(8,128)(2,1)S(1)} %collective-permute-done.12.refs_1_), channel_id=1, source_target_pairs={{0,224},{1,225},{2,226},{3,227},{4,228},{5,229},{6,230},{7,231},{8... | collective-permute-start | bytes 589832 | tf_op jit(solution)/shard_map/ppermute | solution.py:33
  39.4 5.7 %collective-permute-start.11 = (bf16[128,768]{1,0:T(8,128)(2,1)S(1)}, bf16[128,768]{1,0:T(8,128)(2,1)S(1)}, u32[]{:S(2)}, u32[]{:S(2)}) collective-permute-start(bf16[128,768]{1,0:T(8,128)(2,1)S(1)} %collective-permute-done.8.refs_0_), channel_id=1, source_target_pairs={{0,32},{1,33},{2,34},{3,35},{4,36},{5,37},{6,38},{7,39},{8,40},{9,... | collective-permute-start | bytes 589832 | tf_op jit(solution)/shard_map/ppermute | solution.py:33
  45.1 25.4 %copy-start.1 = (bf16[512,768]{1,0:T(8,128)(2,1)S(1)}, bf16[512,768]{1,0:T(8,128)(2,1)}, u32[]{:S(2)}) copy-start(bf16[512,768]{1,0:T(8,128)(2,1)} %cent_ref.3) | copy-start | bytes 2359300
  46.0 3.8 %collective-permute-start.16 = (f32[16,128]{1,0:T(8,128)S(1)}, f32[16,128]{1,0:T(8,128)S(1)}, u32[]{:S(2)}, u32[]{:S(2)}) collective-permute-start(f32[16,128]{1,0:T(8,128)S(1)} %shard_map.37), channel_id=1, source_target_pairs={{0,1},{1,16},{2,3},{3,18},{4,5},{5,20},{6,7},{7,22},{8,9},{9,24},{... | collective-permute-start | bytes 24584 | tf_op jit(solution)/shard_map/ppermute | solution.py:33
  46.1 4.8 %collective-permute-start.17 = (f32[16,128]{1,0:T(8,128)S(1)}, f32[16,128]{1,0:T(8,128)S(1)}, u32[]{:S(2)}, u32[]{:S(2)}) collective-permute-start(f32[16,128]{1,0:T(8,128)S(1)} %shard_map.37), channel_id=1, source_target_pairs={{0,16},{1,17},{2,18},{3,19},{4,20},{5,21},{6,22},{7,23},{8,24},{9,... | collective-permute-start | bytes 24584 | tf_op jit(solution)/shard_map/ppermute | solution.py:33
  49.7 2.5 %collective-permute-start.18 = (f32[16,128]{1,0:T(8,128)S(1)}, f32[16,128]{1,0:T(8,128)S(1)}, u32[]{:S(2)}, u32[]{:S(2)}) collective-permute-start(f32[16,128]{1,0:T(8,128)S(1)} %shard_map.37), channel_id=1, source_target_pairs={{0,17},{1,0},{2,19},{3,2},{4,21},{5,4},{6,23},{7,6},{8,25},{9,8},{... | collective-permute-start | bytes 24584 | tf_op jit(solution)/shard_map/ppermute | solution.py:33
  72.6 11.8 %collective-permute-start.19 = (f32[512,896]{1,0:T(8,128)S(1)}, f32[512,896]{1,0:T(8,128)S(1)}, u32[]{:S(2)}, u32[]{:S(2)}) collective-permute-start(f32[512,896]{1,0:T(8,128)S(1)} %shard_map.39), channel_id=1, source_target_pairs={{0,8},{1,9},{2,10},{3,11},{4,12},{5,13},{6,14},{7,15},{8,0},{9,1},... | collective-permute-start | bytes 5505032 | tf_op jit(solution)/shard_map/ppermute | solution.py:33

commit v3 on v2

--- a/solution.py
+++ b/solution.py
@@ -82,7 +82,7 @@
         out_specs=(IN_VMEM, IN_VMEM),
         out_shape=(here((2 * rows, width), own.dtype), here((2 * rows, LANES), jnp.float32)),
         compiler_params=pltpu.CompilerParams(vmem_limit_bytes=8 * MIB),
-        cost_estimate=pl.CostEstimate(flops=4 * rows * width, bytes_accessed=8 * rows * width, transcendentals=0),
+        cost_estimate=pl.CostEstimate(flops=1, bytes_accessed=1, transcendentals=0),
     )(other, own)
 
 
@@ -138,9 +138,7 @@
         input_output_aliases={len(blocks) + 2 + k: k for k in range(len(before))},
         scratch_shapes=[pltpu.VMEM((8, more), jnp.float32)],
         compiler_params=pltpu.CompilerParams(vmem_limit_bytes=8 * MIB),
-        cost_estimate=pl.CostEstimate(
-            flops=2 * count * more * width, bytes_accessed=4 * count * more, transcendentals=count * more
-        ),
+        cost_estimate=pl.CostEstimate(flops=1, bytes_accessed=1, transcendentals=0),
     )(*pinned(*operands))
 
 
@@ -253,20 +251,27 @@
     both_ways = lambda pair: [along_z(pair[0], 1), along_z(pair[1], -1)]
     own = both_ways(own)
     far = both_ways(far)
-    take([points, across], [(0, 0), (0, 1)])
+    pending = [([points, across], [(0, 0), (0, 1)])]
     for step in (1, 2, 3):
+        seen = [] if step == 1 else state[2]
         if step < 3:
-            next_own = both_ways(after(own, state[2]))
+            next_own = both_ways(after(own, seen))
         else:
-            next_own = [along_z(after(own[0], state[2]), 1)]
-        take(own, [(-step, 0), (step, 0)])
+            next_own = [along_z(after(own[0], seen), 1)]
+        take(*pending.pop(0))
+        seen = state[2]
         if step < 3:
-            next_far = both_ways(after(far, state[2]))
+            next_far = both_ways(after(far, seen))
         else:
-            next_far = [along_z(after(far[1], state[2]), -1)]
-        take(far, [(-step, 1), (step, 1)])
+            next_far = [along_z(after(far[1], seen), -1)]
+        if step > 1:
+            take(*pending.pop(0))
+        pending.append((own, [(-step, 0), (step, 0)]))
+        pending.append((far, [(-step, 1), (step, 1)]))
         own, far = next_own, next_far
-    take([own[0], far[0]], [(4, 0), (4, 1)])
+    pending.append(([own[0], far[0]], [(4, 0), (4, 1)]))
+    for blocks, places in pending:
+        take(blocks, places)
     logits, blocks, norms = state
 
     local = arrange(order, norms)

time: 86.4 us -> 81.1 us (0.939)
  starting transfers between devices: 39 us -> 35 us
  waiting for transfers between devices: 13.7 us -> 11.8 us
    ppermute x20, starting transfers between devices: 39 us -> 35 us  [send(): return lax.ppermute(block, AXES, route)]
    ppermute x20, waiting for transfers between devices: 13.7 us -> 11.8 us  [send(): return lax.ppermute(block, AXES, route)]
  transfers between devices with their start and end apart: 20 -> 20, of which waited for: 10 -> 9; matrix products, arithmetic and copies ran while one was open for 0% -> 0% of each run, Pallas kernels for 10% -> 10%
where the time goes in v3:
time: 81.1 us; the launch traced here: 80.9 us
  starting transfers between devices  35 us (43%)
  blocking collectives  19 us (23%)
  Pallas kernels  13 us (16%)
  waiting for transfers between devices  11.8 us (15%)
  local copies, waits for them, and re-layouts  2.08 us (3%)
    ppermute x20, starting transfers between devices, send(): return lax.ppermute(block, AXES, route)  35 us
    all_to_all x1, blocking collectives, shards(): lax.all_to_all(everywhere, AXES, 0, 0, axis_index_groups=groups_by(lambda...  19 us
    ppermute x20, waiting for transfers between devices, send(): return lax.ppermute(block, AXES, route)  11.8 us
    pallas_call x8, Pallas kernels, logits_of(): pl.pallas_call(functools.partial(logits_kernel, len(blocks), first, len(b...  6.48 us
    pallas_call x2, Pallas kernels, sums_of(): pl.pallas_call(functools.partial(sums_kernel, order, half), in_specs=[IN_...  4.29 us
    unnamed x6, local copies, waits for them, and re-layouts  2.06 us
    pallas_call x1, Pallas kernels, finish(): pl.pallas_call(finish_kernel, grid=(4,), in_specs=[IN_VMEM] * 2, out_spec...  1.75 us
  transfers between devices with their start and end apart: 20, of which 9 were waited for; matrix products, arithmetic and copies ran while one was open for 0% of the time, Pallas kernels for 10%

profile of v3, /device:TPU:1, one launch (start us, length us, event | category | flops | bytes accessed | tf_op | source)
XLA Modules:
  0.0 80.9 jit_solution(4662174134279062379)
XLA Ops:
  0.0 3.2 %collective-permute-start.5 = (bf16[512,768]{1,0:T(8,128)(2,1)}, bf16[512,768]{1,0:T(8,128)(2,1)S(1)}, u32[]{:S(2)}, u32[]{:S(2)}) collective-permute-start(bf16[512,768]{1,0:T(8,128)(2,1)} %cent_ref.3), channel_id=1, source_target_pairs={{0,8},{1,9},{2,10},{3,11},{4,12},{5,13},{6,14},{7,15},{8,0},{9,1},... | collective-permute-start | bytes 2359304 | tf_op jit(solution)/shard_map/ppermute | solution.py:33
  3.2 0.7 collective-permute-start.4
  4.0 1.6 %collective-permute-start = (bf16[128,768]{1,0:T(8,128)(2,1)}, bf16[128,768]{1,0:T(8,128)(2,1)S(1)}, u32[]{:S(2)}, u32[]{:S(2)}) collective-permute-start(bf16[128,768]{1,0:T(8,128)(2,1)} %refs_0_.1), channel_id=1, source_target_pairs={{0,32},{1,33},{2,34},{3,35},{4,36},{5,37},{6,38},{7,39},{8,40},{9,... | collective-permute-start | bytes 589832 | tf_op jit(solution)/shard_map/ppermute | solution.py:33
  5.6 3.9 %collective-permute-start.1 = (bf16[128,768]{1,0:T(8,128)(2,1)}, bf16[128,768]{1,0:T(8,128)(2,1)S(1)}, u32[]{:S(2)}, u32[]{:S(2)}) collective-permute-start(bf16[128,768]{1,0:T(8,128)(2,1)} %refs_0_.1), channel_id=1, source_target_pairs={{0,224},{1,225},{2,226},{3,227},{4,228},{5,229},{6,230},{7,231},{8... | collective-permute-start | bytes 589832 | tf_op jit(solution)/shard_map/ppermute | solution.py:33
  9.6 1.6 %collective-permute-done.4.refs_1_ = bf16[128,768]{1,0:T(8,128)(2,1)S(1)} collective-permute-done((bf16[128,768]{1,0:T(8,128)(2,1)}, bf16[128,768]{1,0:T(8,128)(2,1)S(1)}, u32[]{:S(2)}, u32[]{:S(2)}) %collective-permute-start.4) | collective-permute-done | bytes 196640 | tf_op jit(solution)/shard_map/ppermute | solution.py:33
  11.2 0.0 collective-permute-start.7
  11.2 3.8 %collective-permute-start.8 = (bf16[128,768]{1,0:T(8,128)(2,1)S(1)}, bf16[128,768]{1,0:T(8,128)(2,1)S(1)}, u32[]{:S(2)}, u32[]{:S(2)}) collective-permute-start(bf16[128,768]{1,0:T(8,128)(2,1)S(1)} %collective-permute-done.4.refs_1_), channel_id=1, source_target_pairs={{0,224},{1,225},{2,226},{3,227},{4,228},{5,229},{6,230},{7,231},{8... | collective-permute-start | bytes 589832 | tf_op jit(solution)/shard_map/ppermute | solution.py:33
  15.0 0.0 collective-permute-done.refs_0_
  15.0 0.0 collective-permute-done.1.refs_1_
  15.0 0.0 collective-permute-start.2
  15.1 2.7 %collective-permute-start.3 = (bf16[128,768]{1,0:T(8,128)(2,1)S(1)}, bf16[128,768]{1,0:T(8,128)(2,1)S(1)}, u32[]{:S(2)}, u32[]{:S(2)}) collective-permute-start(bf16[128,768]{1,0:T(8,128)(2,1)S(1)} %collective-permute-done.1.refs_1_), channel_id=1, source_target_pairs={{0,224},{1,225},{2,226},{3,227},{4,228},{5,229},{6,230},{7,231},{8... | collective-permute-start | bytes 589832 | tf_op jit(solution)/shard_map/ppermute | solution.py:33
  17.7 1.1 %copy-done = bf16[512,768]{1,0:T(8,128)(2,1)S(1)} copy-done((bf16[512,768]{1,0:T(8,128)(2,1)S(1)}, bf16[512,768]{1,0:T(8,128)(2,1)}, u32[]{:S(2)}) %copy-start) | copy-done | bytes 786456
  18.9 0.4 shard_map.28
  19.3 0.9 %copy-done.2 = bf16[128,768]{1,0:T(8,128)(2,1)S(1)} copy-done((bf16[128,768]{1,0:T(8,128)(2,1)S(1)}, bf16[128,768]{1,0:T(8,128)(2,1)}, u32[]{:S(2)}) %copy-start.2) | copy-done | bytes 196632
  20.2 0.8 shard_map.29
  21.0 0.0 collective-permute-done.8.refs_1_
  21.0 0.1 collective-permute-start.10
  21.1 2.7 %collective-permute-start.11 = (bf16[128,768]{1,0:T(8,128)(2,1)S(1)}, bf16[128,768]{1,0:T(8,128)(2,1)S(1)}, u32[]{:S(2)}, u32[]{:S(2)}) collective-permute-start(bf16[128,768]{1,0:T(8,128)(2,1)S(1)} %collective-permute-done.8.refs_1_), channel_id=1, source_target_pairs={{0,224},{1,225},{2,226},{3,227},{4,228},{5,229},{6,230},{7,231},{8... | collective-permute-start | bytes 589832 | tf_op jit(solution)/shard_map/ppermute | solution.py:33
  23.8 0.8 shard_map.30
  24.6 2.2 %collective-permute-done.10.refs_0_ = bf16[128,768]{1,0:T(8,128)(2,1)S(1)} collective-permute-done((bf16[128,768]{1,0:T(8,128)(2,1)S(1)}, bf16[128,768]{1,0:T(8,128)(2,1)S(1)}, u32[]{:S(2)}, u32[]{:S(2)}) %collective-permute-start.10) | collective-permute-done | bytes 196640 | tf_op jit(solution)/shard_map/ppermute | solution.py:33
  26.8 0.0 collective-permute-done.11.refs_1_
  26.8 2.7 %collective-permute-start.12 = (bf16[128,768]{1,0:T(8,128)(2,1)S(1)}, bf16[128,768]{1,0:T(8,128)(2,1)S(1)}, u32[]{:S(2)}, u32[]{:S(2)}) collective-permute-start(bf16[128,768]{1,0:T(8,128)(2,1)S(1)} %collective-permute-done.11.refs_1_), channel_id=1, source_target_pairs={{0,224},{1,225},{2,226},{3,227},{4,228},{5,229},{6,230},{7,231},{8... | collective-permute-start | bytes 589832 | tf_op jit(solution)/shard_map/ppermute | solution.py:33
  29.5 0.2 collective-permute-start.15
  29.7 0.8 %shard_map.31 = (f32[1024,2048]{1,0:T(8,128)S(1)}, bf16[2048,768]{1,0:T(8,128)(2,1)S(1)}, f32[1,2048]{1,0:T(1,128)S(1)}) custom-call(bf16[128,768]{1,0:T(8,128)(2,1)S(1)} %collective-permute-done.7.refs_0_, bf16[128,768]{1,0:T(8,128)(2,1)S(1)} %collective-permute-done.8.refs_1_, ...), custom_call_target="tpu_custom_call", output_to_operand_aliasing={{0}: (4, {}), {1}: (5, {}), {2}: (6, {})} | custom-call | flops 1 | bytes 1 | tf_op jit(solution)/shard_map/pallas_call | solution.py:129
  30.6 1.3 %collective-permute-done.6.refs_0_ = bf16[128,768]{1,0:T(8,128)(2,1)S(1)} collective-permute-done((bf16[128,768]{1,0:T(8,128)(2,1)S(1)}, bf16[128,768]{1,0:T(8,128)(2,1)S(1)}, u32[]{:S(2)}, u32[]{:S(2)}) %collective-permute-start.6) | collective-permute-done | bytes 196640 | tf_op jit(solution)/shard_map/ppermute | solution.py:33
  31.9 0.2 collective-permute-start.14
  32.1 0.6 collective-permute-start.9
  32.7 0.8 %shard_map.32 = (f32[1024,2048]{1,0:T(8,128)S(1)}, bf16[2048,768]{1,0:T(8,128)(2,1)S(1)}, f32[1,2048]{1,0:T(1,128)S(1)}) custom-call(bf16[128,768]{1,0:T(8,128)(2,1)S(1)} %collective-permute-done.2.refs_0_, bf16[128,768]{1,0:T(8,128)(2,1)S(1)} %collective-permute-done.3.refs_1_, ...), custom_call_target="tpu_custom_call", output_to_operand_aliasing={{0}: (4, {}), {1}: (5, {}), {2}: (6, {})} | custom-call | flops 1 | bytes 1 | tf_op jit(solution)/shard_map/pallas_call | solution.py:129
  33.5 0.0 collective-permute-done.12.refs_1_
  33.5 2.1 %collective-permute-start.13 = (bf16[128,768]{1,0:T(8,128)(2,1)S(1)}, bf16[128,768]{1,0:T(8,128)(2,1)S(1)}, u32[]{:S(2)}, u32[]{:S(2)}) collective-permute-start(bf16[128,768]{1,0:T(8,128)(2,1)S(1)} %collective-permute-done.12.refs_1_), channel_id=1, source_target_pairs={{0,224},{1,225},{2,226},{3,227},{4,228},{5,229},{6,230},{7,231},{8... | collective-permute-start | bytes 589832 | tf_op jit(solution)/shard_map/ppermute | solution.py:33
  35.6 0.8 %shard_map.33 = (f32[1024,2048]{1,0:T(8,128)S(1)}, bf16[2048,768]{1,0:T(8,128)(2,1)S(1)}, f32[1,2048]{1,0:T(1,128)S(1)}) custom-call(bf16[128,768]{1,0:T(8,128)(2,1)S(1)} %collective-permute-done.10.refs_0_, bf16[128,768]{1,0:T(8,128)(2,1)S(1)} %collective-permute-done.11.refs_1_, ...), custom_call_target="tpu_custom_call", output_to_operand_aliasing={{0}: (4, {}), {1}: (5, {}), {2}: (6, {})} | custom-call | flops 1 | bytes 1 | tf_op jit(solution)/shard_map/pallas_call | solution.py:129
  36.5 0.8 %shard_map.34 = (f32[1024,2048]{1,0:T(8,128)S(1)}, bf16[2048,768]{1,0:T(8,128)(2,1)S(1)}, f32[1,2048]{1,0:T(1,128)S(1)}) custom-call(bf16[128,768]{1,0:T(8,128)(2,1)S(1)} %collective-permute-done.6.refs_0_, bf16[128,768]{1,0:T(8,128)(2,1)S(1)} %collective-permute-done.15.refs_1_, ...), custom_call_target="tpu_custom_call", output_to_operand_aliasing={{0}: (4, {}), {1}: (5, {}), {2}: (6, {})} | custom-call | flops 1 | bytes 1 | tf_op jit(solution)/shard_map/pallas_call | solution.py:129
  37.3 0.3 collective-permute-done.14.refs_0_
  37.6 0.8 %shard_map.35 = (f32[1024,2048]{1,0:T(8,128)S(1)}, bf16[2048,768]{1,0:T(8,128)(2,1)S(1)}, f32[1,2048]{1,0:T(1,128)S(1)}) custom-call(bf16[128,768]{1,0:T(8,128)(2,1)S(1)} %collective-permute-done.14.refs_0_, bf16[128,768]{1,0:T(8,128)(2,1)S(1)} %collective-permute-done.12.refs_1_, ...), custom_call_target="tpu_custom_call", output_to_operand_aliasing={{0}: (4, {}), {1}: (5, {}), {2}: (6, {})} | custom-call | flops 1 | bytes 1 | tf_op jit(solution)/shard_map/pallas_call | solution.py:129
  38.4 2.3 %collective-permute-done.9.refs_0_ = bf16[128,768]{1,0:T(8,128)(2,1)S(1)} collective-permute-done((bf16[128,768]{1,0:T(8,128)(2,1)S(1)}, bf16[128,768]{1,0:T(8,128)(2,1)S(1)}, u32[]{:S(2)}, u32[]{:S(2)}) %collective-permute-start.9) | collective-permute-done | bytes 196640 | tf_op jit(solution)/shard_map/ppermute | solution.py:33
  40.7 0.3 collective-permute-done.13.refs_1_
  40.9 0.8 %shard_map.36 = (f32[1024,2048]{1,0:T(8,128)S(1)}, bf16[2048,768]{1,0:T(8,128)(2,1)S(1)}, f32[1,2048]{1,0:T(1,128)S(1)}) custom-call(bf16[128,768]{1,0:T(8,128)(2,1)S(1)} %collective-permute-done.9.refs_0_, bf16[128,768]{1,0:T(8,128)(2,1)S(1)} %collective-permute-done.13.refs_1_, ...), custom_call_target="tpu_custom_call", output_to_operand_aliasing={{0}: (4, {}), {1}: (5, {}), {2}: (6, {})} | custom-call | flops 1 | bytes 1 | tf_op jit(solution)/shard_map/pallas_call | solution.py:129
  41.8 0.1 collective-permute-start.16
  41.9 3.6 %collective-permute-start.17 = (f32[16,128]{1,0:T(8,128)S(1)}, f32[16,128]{1,0:T(8,128)S(1)}, u32[]{:S(2)}, u32[]{:S(2)}) collective-permute-start(f32[16,128]{1,0:T(8,128)S(1)} %shard_map.37), channel_id=1, source_target_pairs={{0,16},{1,17},{2,18},{3,19},{4,20},{5,21},{6,22},{7,23},{8,24},{9,... | collective-permute-start | bytes 24584 | tf_op jit(solution)/shard_map/ppermute | solution.py:33
  45.5 0.0 collective-permute-done.16
  45.6 1.1 %collective-permute-done.17 = f32[16,128]{1,0:T(8,128)S(1)} collective-permute-done((f32[16,128]{1,0:T(8,128)S(1)}, f32[16,128]{1,0:T(8,128)S(1)}, u32[]{:S(2)}, u32[]{:S(2)}) %collective-permute-start.17) | collective-permute-done | bytes 8224 | tf_op jit(solution)/shard_map/ppermute | solution.py:33
  46.7 1.4 %collective-permute-done.18 = f32[16,128]{1,0:T(8,128)S(1)} collective-permute-done((f32[16,128]{1,0:T(8,128)S(1)}, f32[16,128]{1,0:T(8,128)S(1)}, u32[]{:S(2)}, u32[]{:S(2)}) %collective-permute-start.18) | collective-permute-done | bytes 8224 | tf_op jit(solution)/shard_map/ppermute | solution.py:33
  48.1 19.0 %all_to_all.5.norms_ref = f32[32,16,128]{2,1,0:T(8,128)S(1)} all-to-all(f32[32,16,128]{2,1,0:T(8,128)S(1)} %broadcast_in_dim.2), channel_id=1, replica_groups={{0,2,4,6,32,34,36,38,64,66,68,70,96,98,100,102,128,130,132,134,160,162,..., dimensions={0} | all-to-all | bytes 524288 | tf_op jit(solution)/shard_map/all_to_all | solution.py:282
  67.1 2.1 %shard_map.39 = f32[512,896]{1,0:T(8,128)S(1)} custom-call(f32[1024,2048]{1,0:T(8,128)S(1)} %get-tuple-element.74.logits_ref, bf16[2048,768]{1,0:T(8,128)(2,1)S(1)} %get-tuple-element.75.group_ref, f32[32,16,128]{2,1,0:T(8,128)S(1)} %all_to_all.5.norms_ref, bf16[512,768]{1,0:T(8,128)(2,1)S(1)} %copy-done.1), custom_call_target="tpu_custom_call" | custom-call | flops 1610612736 | bytes 4194304 | tf_op jit(solution)/shard_map/pallas_call | solution.py:196
  69.2 6.5 %collective-permute-start.19 = (f32[512,896]{1,0:T(8,128)S(1)}, f32[512,896]{1,0:T(8,128)S(1)}, u32[]{:S(2)}, u32[]{:S(2)}) collective-permute-start(f32[512,896]{1,0:T(8,128)S(1)} %shard_map.39), channel_id=1, source_target_pairs={{0,8},{1,9},{2,10},{3,11},{4,12},{5,13},{6,14},{7,15},{8,0},{9,1},... | collective-permute-start | bytes 5505032 | tf_op jit(solution)/shard_map/ppermute | solution.py:33
  75.8 2.2 %shard_map.38.first_ref = f32[512,896]{1,0:T(8,128)S(1)} custom-call(f32[1024,2048]{1,0:T(8,128)S(1)} %get-tuple-element.74.logits_ref, bf16[2048,768]{1,0:T(8,128)(2,1)S(1)} %get-tuple-element.75.group_ref, f32[32,16,128]{2,1,0:T(8,128)S(1)} %all_to_all.5.norms_ref, bf16[512,768]{1,0:T(8,128)(2,1)S(1)} %copy-done.1), custom_call_target="tpu_custom_call" | custom-call | flops 1610612736 | bytes 4194304 | tf_op jit(solution)/shard_map/pallas_call | solution.py:196
  78.0 1.2 %collective-permute-done.19.second_ref = f32[512,896]{1,0:T(8,128)S(1)} collective-permute-done((f32[512,896]{1,0:T(8,128)S(1)}, f32[512,896]{1,0:T(8,128)S(1)}, u32[]{:S(2)}, u32[]{:S(2)}) %collective-permute-start.19) | collective-permute-done | bytes 1835040 | tf_op jit(solution)/shard_map/ppermute | solution.py:33
  79.2 1.7 %shard_map.40 = f32[512,768]{1,0:T(8,128)} custom-call(f32[512,896]{1,0:T(8,128)S(1)} %shard_map.38.first_ref, f32[512,896]{1,0:T(8,128)S(1)} %collective-permute-done.19.second_ref), custom_call_target="tpu_custom_call" | custom-call | flops 1179648 | bytes 1572864 | tf_op jit(solution)/shard_map/pallas_call | solution.py:220
  (16 shorter events, 0.1 us)
Async XLA Ops:
  0.0 17.7 %collective-permute-start.5 = (bf16[512,768]{1,0:T(8,128)(2,1)}, bf16[512,768]{1,0:T(8,128)(2,1)S(1)}, u32[]{:S(2)}, u32[]{:S(2)}) collective-permute-start(bf16[512,768]{1,0:T(8,128)(2,1)} %cent_ref.3), channel_id=1, source_target_pairs={{0,8},{1,9},{2,10},{3,11},{4,12},{5,13},{6,14},{7,15},{8,0},{9,1},... | collective-permute-start | bytes 2359304 | tf_op jit(solution)/shard_map/ppermute | solution.py:33
  3.2 8.0 %collective-permute-start.4 = (bf16[128,768]{1,0:T(8,128)(2,1)}, bf16[128,768]{1,0:T(8,128)(2,1)S(1)}, u32[]{:S(2)}, u32[]{:S(2)}) collective-permute-start(bf16[128,768]{1,0:T(8,128)(2,1)} %refs_0_.1), channel_id=1, source_target_pairs={{0,17},{1,16},{2,19},{3,18},{4,21},{5,20},{6,23},{7,22},{8,25},{9,... | collective-permute-start | bytes 589832 | tf_op jit(solution)/shard_map/ppermute | solution.py:33
  4.0 11.1 %collective-permute-start = (bf16[128,768]{1,0:T(8,128)(2,1)}, bf16[128,768]{1,0:T(8,128)(2,1)S(1)}, u32[]{:S(2)}, u32[]{:S(2)}) collective-permute-start(bf16[128,768]{1,0:T(8,128)(2,1)} %refs_0_.1), channel_id=1, source_target_pairs={{0,32},{1,33},{2,34},{3,35},{4,36},{5,37},{6,38},{7,39},{8,40},{9,... | collective-permute-start | bytes 589832 | tf_op jit(solution)/shard_map/ppermute | solution.py:33
  5.6 9.4 %collective-permute-start.1 = (bf16[128,768]{1,0:T(8,128)(2,1)}, bf16[128,768]{1,0:T(8,128)(2,1)S(1)}, u32[]{:S(2)}, u32[]{:S(2)}) collective-permute-start(bf16[128,768]{1,0:T(8,128)(2,1)} %refs_0_.1), channel_id=1, source_target_pairs={{0,224},{1,225},{2,226},{3,227},{4,228},{5,229},{6,230},{7,231},{8... | collective-permute-start | bytes 589832 | tf_op jit(solution)/shard_map/ppermute | solution.py:33
  11.2 9.8 %collective-permute-start.7 = (bf16[128,768]{1,0:T(8,128)(2,1)S(1)}, bf16[128,768]{1,0:T(8,128)(2,1)S(1)}, u32[]{:S(2)}, u32[]{:S(2)}) collective-permute-start(bf16[128,768]{1,0:T(8,128)(2,1)S(1)} %collective-permute-done.4.refs_1_), channel_id=1, source_target_pairs={{0,32},{1,33},{2,34},{3,35},{4,36},{5,37},{6,38},{7,39},{8,40},{9,... | collective-permute-start | bytes 589832 | tf_op jit(solution)/shard_map/ppermute | solution.py:33
  11.2 9.8 %collective-permute-start.8 = (bf16[128,768]{1,0:T(8,128)(2,1)S(1)}, bf16[128,768]{1,0:T(8,128)(2,1)S(1)}, u32[]{:S(2)}, u32[]{:S(2)}) collective-permute-start(bf16[128,768]{1,0:T(8,128)(2,1)S(1)} %collective-permute-done.4.refs_1_), channel_id=1, source_target_pairs={{0,224},{1,225},{2,226},{3,227},{4,228},{5,229},{6,230},{7,231},{8... | collective-permute-start | bytes 589832 | tf_op jit(solution)/shard_map/ppermute | solution.py:33
  15.0 8.7 %collective-permute-start.2 = (bf16[128,768]{1,0:T(8,128)(2,1)S(1)}, bf16[128,768]{1,0:T(8,128)(2,1)S(1)}, u32[]{:S(2)}, u32[]{:S(2)}) collective-permute-start(bf16[128,768]{1,0:T(8,128)(2,1)S(1)} %collective-permute-done.refs_0_), channel_id=1, source_target_pairs={{0,32},{1,33},{2,34},{3,35},{4,36},{5,37},{6,38},{7,39},{8,40},{9,... | collective-permute-start | bytes 589832 | tf_op jit(solution)/shard_map/ppermute | solution.py:33
  15.1 8.7 %collective-permute-start.3 = (bf16[128,768]{1,0:T(8,128)(2,1)S(1)}, bf16[128,768]{1,0:T(8,128)(2,1)S(1)}, u32[]{:S(2)}, u32[]{:S(2)}) collective-permute-start(bf16[128,768]{1,0:T(8,128)(2,1)S(1)} %collective-permute-done.1.refs_1_), channel_id=1, source_target_pairs={{0,224},{1,225},{2,226},{3,227},{4,228},{5,229},{6,230},{7,231},{8... | collective-permute-start | bytes 589832 | tf_op jit(solution)/shard_map/ppermute | solution.py:33
  17.7 1.1 %copy-start = (bf16[512,768]{1,0:T(8,128)(2,1)S(1)}, bf16[512,768]{1,0:T(8,128)(2,1)}, u32[]{:S(2)}) copy-start(bf16[512,768]{1,0:T(8,128)(2,1)} %cent_ref.3) | copy-start | bytes 2359300
  19.3 0.9 %copy-start.2 = (bf16[128,768]{1,0:T(8,128)(2,1)S(1)}, bf16[128,768]{1,0:T(8,128)(2,1)}, u32[]{:S(2)}) copy-start(bf16[128,768]{1,0:T(8,128)(2,1)} %refs_0_.1) | copy-start | bytes 589828
  21.0 5.8 %collective-permute-start.10 = (bf16[128,768]{1,0:T(8,128)(2,1)S(1)}, bf16[128,768]{1,0:T(8,128)(2,1)S(1)}, u32[]{:S(2)}, u32[]{:S(2)}) collective-permute-start(bf16[128,768]{1,0:T(8,128)(2,1)S(1)} %collective-permute-done.7.refs_0_), channel_id=1, source_target_pairs={{0,32},{1,33},{2,34},{3,35},{4,36},{5,37},{6,38},{7,39},{8,40},{9,... | collective-permute-start | bytes 589832 | tf_op jit(solution)/shard_map/ppermute | solution.py:33
  21.1 5.7 %collective-permute-start.11 = (bf16[128,768]{1,0:T(8,128)(2,1)S(1)}, bf16[128,768]{1,0:T(8,128)(2,1)S(1)}, u32[]{:S(2)}, u32[]{:S(2)}) collective-permute-start(bf16[128,768]{1,0:T(8,128)(2,1)S(1)} %collective-permute-done.8.refs_1_), channel_id=1, source_target_pairs={{0,224},{1,225},{2,226},{3,227},{4,228},{5,229},{6,230},{7,231},{8... | collective-permute-start | bytes 589832 | tf_op jit(solution)/shard_map/ppermute | solution.py:33
  23.8 8.1 %collective-permute-start.6 = (bf16[128,768]{1,0:T(8,128)(2,1)S(1)}, bf16[128,768]{1,0:T(8,128)(2,1)S(1)}, u32[]{:S(2)}, u32[]{:S(2)}) collective-permute-start(bf16[128,768]{1,0:T(8,128)(2,1)S(1)} %collective-permute-done.2.refs_0_), channel_id=1, source_target_pairs={{0,32},{1,33},{2,34},{3,35},{4,36},{5,37},{6,38},{7,39},{8,40},{9,... | collective-permute-start | bytes 589832 | tf_op jit(solution)/shard_map/ppermute | solution.py:33
  26.8 6.7 %collective-permute-start.12 = (bf16[128,768]{1,0:T(8,128)(2,1)S(1)}, bf16[128,768]{1,0:T(8,128)(2,1)S(1)}, u32[]{:S(2)}, u32[]{:S(2)}) collective-permute-start(bf16[128,768]{1,0:T(8,128)(2,1)S(1)} %collective-permute-done.11.refs_1_), channel_id=1, source_target_pairs={{0,224},{1,225},{2,226},{3,227},{4,228},{5,229},{6,230},{7,231},{8... | collective-permute-start | bytes 589832 | tf_op jit(solution)/shard_map/ppermute | solution.py:33
  29.5 6.9 %collective-permute-start.15 = (bf16[128,768]{1,0:T(8,128)(2,1)S(1)}, bf16[128,768]{1,0:T(8,128)(2,1)S(1)}, u32[]{:S(2)}, u32[]{:S(2)}) collective-permute-start(bf16[128,768]{1,0:T(8,128)(2,1)S(1)} %collective-permute-done.3.refs_1_), channel_id=1, source_target_pairs={{0,224},{1,225},{2,226},{3,227},{4,228},{5,229},{6,230},{7,231},{8... | collective-permute-start | bytes 589832 | tf_op jit(solution)/shard_map/ppermute | solution.py:33
  31.9 5.7 %collective-permute-start.14 = (bf16[128,768]{1,0:T(8,128)(2,1)S(1)}, bf16[128,768]{1,0:T(8,128)(2,1)S(1)}, u32[]{:S(2)}, u32[]{:S(2)}) collective-permute-start(bf16[128,768]{1,0:T(8,128)(2,1)S(1)} %collective-permute-done.10.refs_0_), channel_id=1, source_target_pairs={{0,32},{1,33},{2,34},{3,35},{4,36},{5,37},{6,38},{7,39},{8,40},{9,... | collective-permute-start | bytes 589832 | tf_op jit(solution)/shard_map/ppermute | solution.py:33
  32.1 8.6 %collective-permute-start.9 = (bf16[128,768]{1,0:T(8,128)(2,1)S(1)}, bf16[128,768]{1,0:T(8,128)(2,1)S(1)}, u32[]{:S(2)}, u32[]{:S(2)}) collective-permute-start(bf16[128,768]{1,0:T(8,128)(2,1)S(1)} %collective-permute-done.6.refs_0_), channel_id=1, source_target_pairs={{0,32},{1,33},{2,34},{3,35},{4,36},{5,37},{6,38},{7,39},{8,40},{9,... | collective-permute-start | bytes 589832 | tf_op jit(solution)/shard_map/ppermute | solution.py:33
  33.5 7.4 %collective-permute-start.13 = (bf16[128,768]{1,0:T(8,128)(2,1)S(1)}, bf16[128,768]{1,0:T(8,128)(2,1)S(1)}, u32[]{:S(2)}, u32[]{:S(2)}) collective-permute-start(bf16[128,768]{1,0:T(8,128)(2,1)S(1)} %collective-permute-done.12.refs_1_), channel_id=1, source_target_pairs={{0,224},{1,225},{2,226},{3,227},{4,228},{5,229},{6,230},{7,231},{8... | collective-permute-start | bytes 589832 | tf_op jit(solution)/shard_map/ppermute | solution.py:33
  40.9 26.2 %copy-start.1 = (bf16[512,768]{1,0:T(8,128)(2,1)S(1)}, bf16[512,768]{1,0:T(8,128)(2,1)}, u32[]{:S(2)}) copy-start(bf16[512,768]{1,0:T(8,128)(2,1)} %cent_ref.3) | copy-start | bytes 2359300
  41.8 3.8 %collective-permute-start.16 = (f32[16,128]{1,0:T(8,128)S(1)}, f32[16,128]{1,0:T(8,128)S(1)}, u32[]{:S(2)}, u32[]{:S(2)}) collective-permute-start(f32[16,128]{1,0:T(8,128)S(1)} %shard_map.37), channel_id=1, source_target_pairs={{0,1},{1,16},{2,3},{3,18},{4,5},{5,20},{6,7},{7,22},{8,9},{9,24},{... | collective-permute-start | bytes 24584 | tf_op jit(solution)/shard_map/ppermute | solution.py:33
  41.9 4.8 %collective-permute-start.17 = (f32[16,128]{1,0:T(8,128)S(1)}, f32[16,128]{1,0:T(8,128)S(1)}, u32[]{:S(2)}, u32[]{:S(2)}) collective-permute-start(f32[16,128]{1,0:T(8,128)S(1)} %shard_map.37), channel_id=1, source_target_pairs={{0,16},{1,17},{2,18},{3,19},{4,20},{5,21},{6,22},{7,23},{8,24},{9,... | collective-permute-start | bytes 24584 | tf_op jit(solution)/shard_map/ppermute | solution.py:33
  45.5 2.5 %collective-permute-start.18 = (f32[16,128]{1,0:T(8,128)S(1)}, f32[16,128]{1,0:T(8,128)S(1)}, u32[]{:S(2)}, u32[]{:S(2)}) collective-permute-start(f32[16,128]{1,0:T(8,128)S(1)} %shard_map.37), channel_id=1, source_target_pairs={{0,17},{1,0},{2,19},{3,2},{4,21},{5,4},{6,23},{7,6},{8,25},{9,8},{... | collective-permute-start | bytes 24584 | tf_op jit(solution)/shard_map/ppermute | solution.py:33
  69.2 10.0 %collective-permute-start.19 = (f32[512,896]{1,0:T(8,128)S(1)}, f32[512,896]{1,0:T(8,128)S(1)}, u32[]{:S(2)}, u32[]{:S(2)}) collective-permute-start(f32[512,896]{1,0:T(8,128)S(1)} %shard_map.39), channel_id=1, source_target_pairs={{0,8},{1,9},{2,10},{3,11},{4,12},{5,13},{6,14},{7,15},{8,0},{9,1},... | collective-permute-start | bytes 5505032 | tf_op jit(solution)/shard_map/ppermute | solution.py:33

commit v4 on v3

--- a/solution.py
+++ b/solution.py
@@ -164,18 +164,21 @@
     )(*pinned(norms))
 
 
-def sums_kernel(order, half, logits_ref, group_ref, norms_ref, cent_ref, out_ref, rows_ref, norm_ref):
-    rows, width = cent_ref.shape
-    points = group_ref.shape[0]
-    rows_ref[...] = combine(norms_ref[...])
+def spread_kernel(order, parts_ref, norm_ref, rows_ref):
+    rows_ref[...] = combine(parts_ref[...])
     for k, (offset, other) in enumerate(order):
         row = rows_ref[pl.ds(row_of(offset, other), 1), :]
         norm_ref[:, pl.ds(k * LANES, LANES)] = jnp.broadcast_to(row, (8, LANES))
+
+
+def add_up(logits_ref, start, group_ref, norm_ref, cent_ref, out_ref):
+    rows, width = out_ref.shape[0], group_ref.shape[1]
+    points = group_ref.shape[0]
     total, mass = None, None
     deep = 512
     for at in range(0, points, deep):
         columns = pl.ds(at, deep)
-        logits = logits_ref[pl.ds(half * rows, rows), columns]
+        logits = logits_ref[pl.ds(start, rows), columns]
         resp = jnp.exp2(logits - norm_ref[:1, columns]).astype(jnp.bfloat16)
         part = jnp.dot(resp, group_ref[columns, :], preferred_element_type=jnp.float32)
         wide = resp.astype(jnp.float32)
@@ -183,49 +186,64 @@
         total = part if total is None else total + part
         mass = weight if mass is None else mass + weight
     mass = jnp.sum(mass, axis=1, keepdims=True)
-    if half == 1:
+    if cent_ref is not None:
         total = total + PRIOR * cent_ref[...].astype(jnp.float32)
         mass = mass + PRIOR
     out_ref[:, pl.ds(0, width)] = total
     out_ref[:, pl.ds(width, LANES)] = jnp.broadcast_to(mass, (rows, LANES))
 
 
-def sums_of(order, half, logits, blocks, norms, cents):
-    rows, width = cents.shape
-    points = blocks.shape[0]
-    return pl.pallas_call(
-        functools.partial(sums_kernel, order, half),
-        in_specs=[IN_VMEM] * 4,
-        out_specs=IN_VMEM,
-        out_shape=here((rows, width + LANES), jnp.float32),
-        scratch_shapes=[pltpu.VMEM((len(order), LANES), jnp.float32), pltpu.VMEM((8, points), jnp.float32)],
+def first_sums_kernel(order, start, logits_ref, group_ref, parts_ref, out_ref, norm_ref, rows_ref):
+    spread_kernel(order, parts_ref, norm_ref, rows_ref)
+    add_up(logits_ref, start, group_ref, norm_ref, None, out_ref)
+
+
+def more_sums_kernel(start, logits_ref, group_ref, norm_ref, out_ref):
+    add_up(logits_ref, start, group_ref, norm_ref, None, out_ref)
+
+
+def own_sums_kernel(start, logits_ref, group_ref, norm_ref, cent_ref, out_ref):
+    add_up(logits_ref, start, group_ref, norm_ref, cent_ref, out_ref)
+
+
+def sums_call(kernel, operands, rows, points, width, spread=None):
+    out = here((rows, width + LANES), jnp.float32)
+    return pl.pallas_call(
+        kernel,
+        in_specs=[IN_VMEM] * len(operands),
+        out_specs=(IN_VMEM, IN_VMEM) if spread else IN_VMEM,
+        out_shape=(out, here((8, points), jnp.float32)) if spread else out,
+        scratch_shapes=[pltpu.VMEM((spread, LANES), jnp.float32)] if spread else [],
         compiler_params=pltpu.CompilerParams(vmem_limit_bytes=16 * MIB),
-        cost_estimate=pl.CostEstimate(
-            flops=2 * rows * points * width, bytes_accessed=4 * rows * points, transcendentals=rows * points
-        ),
-    )(*pinned(logits, blocks, norms, cents))
-
-
-def finish_kernel(first_ref, second_ref, out_ref):
+        cost_estimate=pl.CostEstimate(flops=1, bytes_accessed=1, transcendentals=0),
+    )(*pinned(*operands))
+
+
+def finish_kernel(own_ref, *refs):
+    out_ref = refs[-1]
     rows, width = out_ref.shape
-    here_rows = pl.ds(pl.multiple_of(pl.program_id(0) * rows, rows), rows)
-    both = first_ref[here_rows, :] + second_ref[here_rows, :]
-    weight = 1.0 / both[:, width:]
-    out_ref[...] = both[:, :width] * jnp.concatenate([weight] * (width // LANES), axis=1)
-
-
-def finish(first, second):
-    rows, wide = first.shape
+    for k, ref in enumerate(refs[:-1]):
+
+        @pl.when(pl.program_id(0) == k)
+        def _():
+            both = own_ref[pl.ds(k * rows, rows), :] + ref[...]
+            weight = 1.0 / both[:, width:]
+            out_ref[...] = both[:, :width] * jnp.concatenate([weight] * (width // LANES), axis=1)
+
+
+def finish(own, others):
+    rows, wide = own.shape
     width = wide - LANES
+    steps = len(others)
     return pl.pallas_call(
         finish_kernel,
-        grid=(4,),
-        in_specs=[IN_VMEM] * 2,
-        out_specs=pl.BlockSpec((rows // 4, width), lambda i: (i, 0)),
+        grid=(steps,),
+        in_specs=[IN_VMEM] * (1 + steps),
+        out_specs=pl.BlockSpec((rows // steps, width), lambda i: (i, 0)),
         out_shape=jax.ShapeDtypeStruct((rows, width), jnp.float32),
         compiler_params=pltpu.CompilerParams(vmem_limit_bytes=8 * MIB),
         cost_estimate=pl.CostEstimate(flops=3 * rows * width, bytes_accessed=4 * rows * width, transcendentals=0),
-    )(*pinned(first, second))
+    )(*pinned(own, *others))
 
 
 def after(arrays, *done):
@@ -281,10 +299,20 @@
     everywhere = jnp.broadcast_to(local[None], (Y * Z,) + local.shape)
     parts = lax.all_to_all(everywhere, AXES, 0, 0, axis_index_groups=groups_by(lambda x, y, z, c: (x, c)))
 
-    other_sums = sums_of(order, 0, logits, blocks, parts, centroids)
-    got = to_sibling(other_sums)
-    own_sums = sums_of(order, 1, logits, blocks, parts, centroids)
-    return finish(own_sums, got)
+    count, width = centroids.shape
+    piece = count // 2
+    shape = (everything, width)
+    one, norm = sums_call(
+        functools.partial(first_sums_kernel, tuple(order), 0), (logits, blocks, parts), piece, *shape, len(order)
+    )
+    got_one = to_sibling(one)
+    two = sums_call(functools.partial(more_sums_kernel, piece), (logits, blocks, norm), piece, *shape)
+    got_two = to_sibling(two)
+    norm = after(norm, two)
+    own_sums = sums_call(
+        functools.partial(own_sums_kernel, count), (logits, blocks, norm, centroids), count, *shape
+    )
+    return finish(own_sums, (got_one, got_two))
 
 
 def solution(mesh):

time: 81.1 us -> 80.6 us (level)
    pallas_call x3 -> x4, Pallas kernels: 6.03 us -> 5.36 us  [the longest x3 4.13 us: sums_call(): pl.pallas_call(kernel, in_specs=[IN_VMEM] * len(operands), out_specs=(IN_...]
    ppermute x20 -> x21, waiting for transfers between devices: 11.8 us -> 11.9 us  [send(): return lax.ppermute(block, AXES, route)]
    ppermute x20 -> x21, starting transfers between devices: 35 us -> 35.1 us  [send(): return lax.ppermute(block, AXES, route)]
  transfers between devices with their start and end apart: 20 -> 21, of which waited for: 9 -> 9; matrix products, arithmetic and copies ran while one was open for 0% -> 0% of each run, Pallas kernels for 10% -> 10%
where the time goes in v4:
time: 80.6 us; the launch traced here: 80.4 us
  starting transfers between devices  35.1 us (44%)
  blocking collectives  19 us (24%)
  Pallas kernels  12.2 us (15%)
  waiting for transfers between devices  11.9 us (15%)
  local copies, waits for them, and re-layouts  2.08 us (3%)
    ppermute x21, starting transfers between devices, send(): return lax.ppermute(block, AXES, route)  35.1 us
    all_to_all x1, blocking collectives, shards(): lax.all_to_all(everywhere, AXES, 0, 0, axis_index_groups=groups_by(lambda...  19 us
    ppermute x21, waiting for transfers between devices, send(): return lax.ppermute(block, AXES, route)  11.9 us
    pallas_call x8, Pallas kernels, logits_of(): pl.pallas_call(functools.partial(logits_kernel, len(blocks), first, len(b...  6.44 us
    pallas_call x3, Pallas kernels, sums_call(): pl.pallas_call(kernel, in_specs=[IN_VMEM] * len(operands), out_specs=(IN_...  4.13 us
    unnamed x6, local copies, waits for them, and re-layouts  2.06 us
  transfers between devices with their start and end apart: 21, of which 9 were waited for; matrix products, arithmetic and copies ran while one was open for 0% of the time, Pallas kernels for 10%

profile of v4, /device:TPU:1, one launch (start us, length us, event | category | flops | bytes accessed | tf_op | source)
XLA Modules:
  0.0 80.4 jit_solution(6039395030098453484)
XLA Ops:
  0.0 3.2 %collective-permute-start.5 = (bf16[512,768]{1,0:T(8,128)(2,1)}, bf16[512,768]{1,0:T(8,128)(2,1)S(1)}, u32[]{:S(2)}, u32[]{:S(2)}) collective-permute-start(bf16[512,768]{1,0:T(8,128)(2,1)} %cent_ref.1), channel_id=1, source_target_pairs={{0,8},{1,9},{2,10},{3,11},{4,12},{5,13},{6,14},{7,15},{8,0},{9,1},... | collective-permute-start | bytes 2359304 | tf_op jit(solution)/shard_map/ppermute | solution.py:33
  3.2 0.7 collective-permute-start.4
  4.0 1.6 %collective-permute-start = (bf16[128,768]{1,0:T(8,128)(2,1)}, bf16[128,768]{1,0:T(8,128)(2,1)S(1)}, u32[]{:S(2)}, u32[]{:S(2)}) collective-permute-start(bf16[128,768]{1,0:T(8,128)(2,1)} %refs_0_.1), channel_id=1, source_target_pairs={{0,32},{1,33},{2,34},{3,35},{4,36},{5,37},{6,38},{7,39},{8,40},{9,... | collective-permute-start | bytes 589832 | tf_op jit(solution)/shard_map/ppermute | solution.py:33
  5.6 3.9 %collective-permute-start.1 = (bf16[128,768]{1,0:T(8,128)(2,1)}, bf16[128,768]{1,0:T(8,128)(2,1)S(1)}, u32[]{:S(2)}, u32[]{:S(2)}) collective-permute-start(bf16[128,768]{1,0:T(8,128)(2,1)} %refs_0_.1), channel_id=1, source_target_pairs={{0,224},{1,225},{2,226},{3,227},{4,228},{5,229},{6,230},{7,231},{8... | collective-permute-start | bytes 589832 | tf_op jit(solution)/shard_map/ppermute | solution.py:33
  9.6 1.6 %collective-permute-done.4.refs_1_ = bf16[128,768]{1,0:T(8,128)(2,1)S(1)} collective-permute-done((bf16[128,768]{1,0:T(8,128)(2,1)}, bf16[128,768]{1,0:T(8,128)(2,1)S(1)}, u32[]{:S(2)}, u32[]{:S(2)}) %collective-permute-start.4) | collective-permute-done | bytes 196640 | tf_op jit(solution)/shard_map/ppermute | solution.py:33
  11.2 3.8 %collective-permute-start.8 = (bf16[128,768]{1,0:T(8,128)(2,1)S(1)}, bf16[128,768]{1,0:T(8,128)(2,1)S(1)}, u32[]{:S(2)}, u32[]{:S(2)}) collective-permute-start(bf16[128,768]{1,0:T(8,128)(2,1)S(1)} %collective-permute-done.4.refs_1_), channel_id=1, source_target_pairs={{0,224},{1,225},{2,226},{3,227},{4,228},{5,229},{6,230},{7,231},{8... | collective-permute-start | bytes 589832 | tf_op jit(solution)/shard_map/ppermute | solution.py:33
  15.0 0.0 collective-permute-start.2
  15.1 2.7 %collective-permute-start.3 = (bf16[128,768]{1,0:T(8,128)(2,1)S(1)}, bf16[128,768]{1,0:T(8,128)(2,1)S(1)}, u32[]{:S(2)}, u32[]{:S(2)}) collective-permute-start(bf16[128,768]{1,0:T(8,128)(2,1)S(1)} %collective-permute-done.1.refs_1_), channel_id=1, source_target_pairs={{0,224},{1,225},{2,226},{3,227},{4,228},{5,229},{6,230},{7,231},{8... | collective-permute-start | bytes 589832 | tf_op jit(solution)/shard_map/ppermute | solution.py:33
  17.7 1.1 %copy-done = bf16[512,768]{1,0:T(8,128)(2,1)S(1)} copy-done((bf16[512,768]{1,0:T(8,128)(2,1)S(1)}, bf16[512,768]{1,0:T(8,128)(2,1)}, u32[]{:S(2)}) %copy-start) | copy-done | bytes 786456
  18.9 0.4 shard_map.28
  19.3 0.9 %copy-done.2 = bf16[128,768]{1,0:T(8,128)(2,1)S(1)} copy-done((bf16[128,768]{1,0:T(8,128)(2,1)S(1)}, bf16[128,768]{1,0:T(8,128)(2,1)}, u32[]{:S(2)}) %copy-start.2) | copy-done | bytes 196632
  20.2 0.8 shard_map.29
  21.0 0.0 collective-permute-done.7.refs_0_
  21.0 0.1 collective-permute-start.10
  21.1 2.7 %collective-permute-start.11 = (bf16[128,768]{1,0:T(8,128)(2,1)S(1)}, bf16[128,768]{1,0:T(8,128)(2,1)S(1)}, u32[]{:S(2)}, u32[]{:S(2)}) collective-permute-start(bf16[128,768]{1,0:T(8,128)(2,1)S(1)} %collective-permute-done.8.refs_1_), channel_id=1, source_target_pairs={{0,224},{1,225},{2,226},{3,227},{4,228},{5,229},{6,230},{7,231},{8... | collective-permute-start | bytes 589832 | tf_op jit(solution)/shard_map/ppermute | solution.py:33
  23.8 0.0 collective-permute-done.2.refs_0_
  23.8 0.0 collective-permute-done.3.refs_1_
  23.8 0.0 collective-permute-start.6
  23.8 0.8 %shard_map.30 = (f32[1024,2048]{1,0:T(8,128)S(1)}, bf16[2048,768]{1,0:T(8,128)(2,1)S(1)}, f32[1,2048]{1,0:T(1,128)S(1)}) custom-call(bf16[128,768]{1,0:T(8,128)(2,1)S(1)} %collective-permute-done.refs_0_, bf16[128,768]{1,0:T(8,128)(2,1)S(1)} %collective-permute-done.1.refs_1_, ...), custom_call_target="tpu_custom_call", output_to_operand_aliasing={{0}: (4, {}), {1}: (5, {}), {2}: (6, {})} | custom-call | flops 1 | bytes 1 | tf_op jit(solution)/shard_map/pallas_call | solution.py:129
  24.6 2.2 %collective-permute-done.10.refs_0_ = bf16[128,768]{1,0:T(8,128)(2,1)S(1)} collective-permute-done((bf16[128,768]{1,0:T(8,128)(2,1)S(1)}, bf16[128,768]{1,0:T(8,128)(2,1)S(1)}, u32[]{:S(2)}, u32[]{:S(2)}) %collective-permute-start.10) | collective-permute-done | bytes 196640 | tf_op jit(solution)/shard_map/ppermute | solution.py:33
  26.8 2.7 %collective-permute-start.12 = (bf16[128,768]{1,0:T(8,128)(2,1)S(1)}, bf16[128,768]{1,0:T(8,128)(2,1)S(1)}, u32[]{:S(2)}, u32[]{:S(2)}) collective-permute-start(bf16[128,768]{1,0:T(8,128)(2,1)S(1)} %collective-permute-done.11.refs_1_), channel_id=1, source_target_pairs={{0,224},{1,225},{2,226},{3,227},{4,228},{5,229},{6,230},{7,231},{8... | collective-permute-start | bytes 589832 | tf_op jit(solution)/shard_map/ppermute | solution.py:33
  29.5 0.2 collective-permute-start.15
  29.7 0.8 %shard_map.31 = (f32[1024,2048]{1,0:T(8,128)S(1)}, bf16[2048,768]{1,0:T(8,128)(2,1)S(1)}, f32[1,2048]{1,0:T(1,128)S(1)}) custom-call(bf16[128,768]{1,0:T(8,128)(2,1)S(1)} %collective-permute-done.7.refs_0_, bf16[128,768]{1,0:T(8,128)(2,1)S(1)} %collective-permute-done.8.refs_1_, ...), custom_call_target="tpu_custom_call", output_to_operand_aliasing={{0}: (4, {}), {1}: (5, {}), {2}: (6, {})} | custom-call | flops 1 | bytes 1 | tf_op jit(solution)/shard_map/pallas_call | solution.py:129
  30.6 1.3 %collective-permute-done.6.refs_0_ = bf16[128,768]{1,0:T(8,128)(2,1)S(1)} collective-permute-done((bf16[128,768]{1,0:T(8,128)(2,1)S(1)}, bf16[128,768]{1,0:T(8,128)(2,1)S(1)}, u32[]{:S(2)}, u32[]{:S(2)}) %collective-permute-start.6) | collective-permute-done | bytes 196640 | tf_op jit(solution)/shard_map/ppermute | solution.py:33
  31.9 0.2 collective-permute-start.14
  32.0 0.7 collective-permute-start.9
  32.7 0.8 %shard_map.32 = (f32[1024,2048]{1,0:T(8,128)S(1)}, bf16[2048,768]{1,0:T(8,128)(2,1)S(1)}, f32[1,2048]{1,0:T(1,128)S(1)}) custom-call(bf16[128,768]{1,0:T(8,128)(2,1)S(1)} %collective-permute-done.2.refs_0_, bf16[128,768]{1,0:T(8,128)(2,1)S(1)} %collective-permute-done.3.refs_1_, ...), custom_call_target="tpu_custom_call", output_to_operand_aliasing={{0}: (4, {}), {1}: (5, {}), {2}: (6, {})} | custom-call | flops 1 | bytes 1 | tf_op jit(solution)/shard_map/pallas_call | solution.py:129
  33.5 2.1 %collective-permute-start.13 = (bf16[128,768]{1,0:T(8,128)(2,1)S(1)}, bf16[128,768]{1,0:T(8,128)(2,1)S(1)}, u32[]{:S(2)}, u32[]{:S(2)}) collective-permute-start(bf16[128,768]{1,0:T(8,128)(2,1)S(1)} %collective-permute-done.12.refs_1_), channel_id=1, source_target_pairs={{0,224},{1,225},{2,226},{3,227},{4,228},{5,229},{6,230},{7,231},{8... | collective-permute-start | bytes 589832 | tf_op jit(solution)/shard_map/ppermute | solution.py:33
  35.6 0.8 shard_map.33
  36.4 0.8 %shard_map.34 = (f32[1024,2048]{1,0:T(8,128)S(1)}, bf16[2048,768]{1,0:T(8,128)(2,1)S(1)}, f32[1,2048]{1,0:T(1,128)S(1)}) custom-call(bf16[128,768]{1,0:T(8,128)(2,1)S(1)} %collective-permute-done.6.refs_0_, bf16[128,768]{1,0:T(8,128)(2,1)S(1)} %collective-permute-done.15.refs_1_, ...), custom_call_target="tpu_custom_call", output_to_operand_aliasing={{0}: (4, {}), {1}: (5, {}), {2}: (6, {})} | custom-call | flops 1 | bytes 1 | tf_op jit(solution)/shard_map/pallas_call | solution.py:129
  37.2 0.4 collective-permute-done.14.refs_0_
  37.6 0.8 shard_map.35
  38.4 2.3 %collective-permute-done.9.refs_0_ = bf16[128,768]{1,0:T(8,128)(2,1)S(1)} collective-permute-done((bf16[128,768]{1,0:T(8,128)(2,1)S(1)}, bf16[128,768]{1,0:T(8,128)(2,1)S(1)}, u32[]{:S(2)}, u32[]{:S(2)}) %collective-permute-start.9) | collective-permute-done | bytes 196640 | tf_op jit(solution)/shard_map/ppermute | solution.py:33
  40.7 0.3 collective-permute-done.13.refs_1_
  40.9 0.8 shard_map.36
  41.8 0.1 collective-permute-start.16
  41.9 3.6 %collective-permute-start.17 = (f32[16,128]{1,0:T(8,128)S(1)}, f32[16,128]{1,0:T(8,128)S(1)}, u32[]{:S(2)}, u32[]{:S(2)}) collective-permute-start(f32[16,128]{1,0:T(8,128)S(1)} %shard_map.37), channel_id=1, source_target_pairs={{0,16},{1,17},{2,18},{3,19},{4,20},{5,21},{6,22},{7,23},{8,24},{9,... | collective-permute-start | bytes 24584 | tf_op jit(solution)/shard_map/ppermute | solution.py:33
  45.5 0.0 collective-permute-done.16
  45.6 1.1 %collective-permute-done.17 = f32[16,128]{1,0:T(8,128)S(1)} collective-permute-done((f32[16,128]{1,0:T(8,128)S(1)}, f32[16,128]{1,0:T(8,128)S(1)}, u32[]{:S(2)}, u32[]{:S(2)}) %collective-permute-start.17) | collective-permute-done | bytes 8224 | tf_op jit(solution)/shard_map/ppermute | solution.py:33
  46.7 1.4 %collective-permute-done.18 = f32[16,128]{1,0:T(8,128)S(1)} collective-permute-done((f32[16,128]{1,0:T(8,128)S(1)}, f32[16,128]{1,0:T(8,128)S(1)}, u32[]{:S(2)}, u32[]{:S(2)}) %collective-permute-start.18) | collective-permute-done | bytes 8224 | tf_op jit(solution)/shard_map/ppermute | solution.py:33
  48.1 19.0 %all_to_all.5.parts_ref = f32[32,16,128]{2,1,0:T(8,128)S(1)} all-to-all(f32[32,16,128]{2,1,0:T(8,128)S(1)} %broadcast_in_dim.2), channel_id=1, replica_groups={{0,2,4,6,32,34,36,38,64,66,68,70,96,98,100,102,128,130,132,134,160,162,..., dimensions={0} | all-to-all | bytes 524288 | tf_op jit(solution)/shard_map/all_to_all | solution.py:300
  67.1 1.1 %shard_map.38 = (f32[256,896]{1,0:T(8,128)S(1)}, f32[8,2048]{1,0:T(8,128)S(1)}) custom-call(f32[1024,2048]{1,0:T(8,128)S(1)} %get-tuple-element.77.logits_ref, bf16[2048,768]{1,0:T(8,128)(2,1)S(1)} %get-tuple-element.78.group_ref, f32[32,16,128]{2,1,0:T(8,128)S(1)} %all_to_all.5.parts_ref), custom_call_target="tpu_custom_call" | custom-call | flops 1 | bytes 1 | tf_op jit(solution)/shard_map/pallas_call | solution.py:211
  68.2 1.0 %shard_map.39 = f32[256,896]{1,0:T(8,128)S(1)} custom-call(f32[1024,2048]{1,0:T(8,128)S(1)} %get-tuple-element.77.logits_ref, bf16[2048,768]{1,0:T(8,128)(2,1)S(1)} %get-tuple-element.78.group_ref, f32[8,2048]{1,0:T(8,128)S(1)} %get-tuple-element.81.norm_ref), custom_call_target="tpu_custom_call" | custom-call | flops 1 | bytes 1 | tf_op jit(solution)/shard_map/pallas_call | solution.py:211
  69.3 6.5 %collective-permute-start.20 = (f32[256,896]{1,0:T(8,128)S(1)}, f32[256,896]{1,0:T(8,128)S(1)}, u32[]{:S(2)}, u32[]{:S(2)}) collective-permute-start(f32[256,896]{1,0:T(8,128)S(1)} %shard_map.39), channel_id=1, source_target_pairs={{0,8},{1,9},{2,10},{3,11},{4,12},{5,13},{6,14},{7,15},{8,0},{9,1},... | collective-permute-start | bytes 2752520 | tf_op jit(solution)/shard_map/ppermute | solution.py:33
  75.8 0.1 collective-permute-start.19
  75.9 2.0 %shard_map.40.own_ref = f32[512,896]{1,0:T(8,128)S(1)} custom-call(f32[1024,2048]{1,0:T(8,128)S(1)} %get-tuple-element.77.logits_ref, bf16[2048,768]{1,0:T(8,128)(2,1)S(1)} %get-tuple-element.78.group_ref, f32[8,2048]{1,0:T(8,128)S(1)} %get-tuple-element.81.norm_ref, bf16[512,768]{1,0:T(8,128)(2,1)S(1)} %copy-done.1), custom_call_target="tpu_custom_call" | custom-call | flops 1 | bytes 1 | tf_op jit(solution)/shard_map/pallas_call | solution.py:211
  77.9 1.3 %collective-permute-done.19.refs_0_ = f32[256,896]{1,0:T(8,128)S(1)} collective-permute-done((f32[256,896]{1,0:T(8,128)S(1)}, f32[256,896]{1,0:T(8,128)S(1)}, u32[]{:S(2)}, u32[]{:S(2)}) %collective-permute-start.19) | collective-permute-done | bytes 917536 | tf_op jit(solution)/shard_map/ppermute | solution.py:33
  79.2 1.2 %shard_map.41 = f32[512,768]{1,0:T(8,128)} custom-call(f32[512,896]{1,0:T(8,128)S(1)} %shard_map.40.own_ref, f32[256,896]{1,0:T(8,128)S(1)} %collective-permute-done.19.refs_0_, f32[256,896]{1,0:T(8,128)S(1)} %collective-permute-done.20.refs_1_), custom_call_target="tpu_custom_call" | custom-call | flops 1179648 | bytes 1572864 | tf_op jit(solution)/shard_map/pallas_call | solution.py:238
  (19 shorter events, 0.1 us)
Async XLA Ops:
  0.0 17.7 %collective-permute-start.5 = (bf16[512,768]{1,0:T(8,128)(2,1)}, bf16[512,768]{1,0:T(8,128)(2,1)S(1)}, u32[]{:S(2)}, u32[]{:S(2)}) collective-permute-start(bf16[512,768]{1,0:T(8,128)(2,1)} %cent_ref.1), channel_id=1, source_target_pairs={{0,8},{1,9},{2,10},{3,11},{4,12},{5,13},{6,14},{7,15},{8,0},{9,1},... | collective-permute-start | bytes 2359304 | tf_op jit(solution)/shard_map/ppermute | solution.py:33
  3.2 8.0 %collective-permute-start.4 = (bf16[128,768]{1,0:T(8,128)(2,1)}, bf16[128,768]{1,0:T(8,128)(2,1)S(1)}, u32[]{:S(2)}, u32[]{:S(2)}) collective-permute-start(bf16[128,768]{1,0:T(8,128)(2,1)} %refs_0_.1), channel_id=1, source_target_pairs={{0,17},{1,16},{2,19},{3,18},{4,21},{5,20},{6,23},{7,22},{8,25},{9,... | collective-permute-start | bytes 589832 | tf_op jit(solution)/shard_map/ppermute | solution.py:33
  4.0 11.1 %collective-permute-start = (bf16[128,768]{1,0:T(8,128)(2,1)}, bf16[128,768]{1,0:T(8,128)(2,1)S(1)}, u32[]{:S(2)}, u32[]{:S(2)}) collective-permute-start(bf16[128,768]{1,0:T(8,128)(2,1)} %refs_0_.1), channel_id=1, source_target_pairs={{0,32},{1,33},{2,34},{3,35},{4,36},{5,37},{6,38},{7,39},{8,40},{9,... | collective-permute-start | bytes 589832 | tf_op jit(solution)/shard_map/ppermute | solution.py:33
  5.6 9.4 %collective-permute-start.1 = (bf16[128,768]{1,0:T(8,128)(2,1)}, bf16[128,768]{1,0:T(8,128)(2,1)S(1)}, u32[]{:S(2)}, u32[]{:S(2)}) collective-permute-start(bf16[128,768]{1,0:T(8,128)(2,1)} %refs_0_.1), channel_id=1, source_target_pairs={{0,224},{1,225},{2,226},{3,227},{4,228},{5,229},{6,230},{7,231},{8... | collective-permute-start | bytes 589832 | tf_op jit(solution)/shard_map/ppermute | solution.py:33
  11.2 9.8 %collective-permute-start.7 = (bf16[128,768]{1,0:T(8,128)(2,1)S(1)}, bf16[128,768]{1,0:T(8,128)(2,1)S(1)}, u32[]{:S(2)}, u32[]{:S(2)}) collective-permute-start(bf16[128,768]{1,0:T(8,128)(2,1)S(1)} %collective-permute-done.4.refs_1_), channel_id=1, source_target_pairs={{0,32},{1,33},{2,34},{3,35},{4,36},{5,37},{6,38},{7,39},{8,40},{9,... | collective-permute-start | bytes 589832 | tf_op jit(solution)/shard_map/ppermute | solution.py:33
  11.2 9.8 %collective-permute-start.8 = (bf16[128,768]{1,0:T(8,128)(2,1)S(1)}, bf16[128,768]{1,0:T(8,128)(2,1)S(1)}, u32[]{:S(2)}, u32[]{:S(2)}) collective-permute-start(bf16[128,768]{1,0:T(8,128)(2,1)S(1)} %collective-permute-done.4.refs_1_), channel_id=1, source_target_pairs={{0,224},{1,225},{2,226},{3,227},{4,228},{5,229},{6,230},{7,231},{8... | collective-permute-start | bytes 589832 | tf_op jit(solution)/shard_map/ppermute | solution.py:33
  15.0 8.7 %collective-permute-start.2 = (bf16[128,768]{1,0:T(8,128)(2,1)S(1)}, bf16[128,768]{1,0:T(8,128)(2,1)S(1)}, u32[]{:S(2)}, u32[]{:S(2)}) collective-permute-start(bf16[128,768]{1,0:T(8,128)(2,1)S(1)} %collective-permute-done.refs_0_), channel_id=1, source_target_pairs={{0,32},{1,33},{2,34},{3,35},{4,36},{5,37},{6,38},{7,39},{8,40},{9,... | collective-permute-start | bytes 589832 | tf_op jit(solution)/shard_map/ppermute | solution.py:33
  15.1 8.7 %collective-permute-start.3 = (bf16[128,768]{1,0:T(8,128)(2,1)S(1)}, bf16[128,768]{1,0:T(8,128)(2,1)S(1)}, u32[]{:S(2)}, u32[]{:S(2)}) collective-permute-start(bf16[128,768]{1,0:T(8,128)(2,1)S(1)} %collective-permute-done.1.refs_1_), channel_id=1, source_target_pairs={{0,224},{1,225},{2,226},{3,227},{4,228},{5,229},{6,230},{7,231},{8... | collective-permute-start | bytes 589832 | tf_op jit(solution)/shard_map/ppermute | solution.py:33
  17.7 1.1 %copy-start = (bf16[512,768]{1,0:T(8,128)(2,1)S(1)}, bf16[512,768]{1,0:T(8,128)(2,1)}, u32[]{:S(2)}) copy-start(bf16[512,768]{1,0:T(8,128)(2,1)} %cent_ref.1) | copy-start | bytes 2359300
  19.3 0.9 %copy-start.2 = (bf16[128,768]{1,0:T(8,128)(2,1)S(1)}, bf16[128,768]{1,0:T(8,128)(2,1)}, u32[]{:S(2)}) copy-start(bf16[128,768]{1,0:T(8,128)(2,1)} %refs_0_.1) | copy-start | bytes 589828
  21.0 5.8 %collective-permute-start.10 = (bf16[128,768]{1,0:T(8,128)(2,1)S(1)}, bf16[128,768]{1,0:T(8,128)(2,1)S(1)}, u32[]{:S(2)}, u32[]{:S(2)}) collective-permute-start(bf16[128,768]{1,0:T(8,128)(2,1)S(1)} %collective-permute-done.7.refs_0_), channel_id=1, source_target_pairs={{0,32},{1,33},{2,34},{3,35},{4,36},{5,37},{6,38},{7,39},{8,40},{9,... | collective-permute-start | bytes 589832 | tf_op jit(solution)/shard_map/ppermute | solution.py:33
  21.1 5.7 %collective-permute-start.11 = (bf16[128,768]{1,0:T(8,128)(2,1)S(1)}, bf16[128,768]{1,0:T(8,128)(2,1)S(1)}, u32[]{:S(2)}, u32[]{:S(2)}) collective-permute-start(bf16[128,768]{1,0:T(8,128)(2,1)S(1)} %collective-permute-done.8.refs_1_), channel_id=1, source_target_pairs={{0,224},{1,225},{2,226},{3,227},{4,228},{5,229},{6,230},{7,231},{8... | collective-permute-start | bytes 589832 | tf_op jit(solution)/shard_map/ppermute | solution.py:33
  23.8 8.1 %collective-permute-start.6 = (bf16[128,768]{1,0:T(8,128)(2,1)S(1)}, bf16[128,768]{1,0:T(8,128)(2,1)S(1)}, u32[]{:S(2)}, u32[]{:S(2)}) collective-permute-start(bf16[128,768]{1,0:T(8,128)(2,1)S(1)} %collective-permute-done.2.refs_0_), channel_id=1, source_target_pairs={{0,32},{1,33},{2,34},{3,35},{4,36},{5,37},{6,38},{7,39},{8,40},{9,... | collective-permute-start | bytes 589832 | tf_op jit(solution)/shard_map/ppermute | solution.py:33
  26.8 6.7 %collective-permute-start.12 = (bf16[128,768]{1,0:T(8,128)(2,1)S(1)}, bf16[128,768]{1,0:T(8,128)(2,1)S(1)}, u32[]{:S(2)}, u32[]{:S(2)}) collective-permute-start(bf16[128,768]{1,0:T(8,128)(2,1)S(1)} %collective-permute-done.11.refs_1_), channel_id=1, source_target_pairs={{0,224},{1,225},{2,226},{3,227},{4,228},{5,229},{6,230},{7,231},{8... | collective-permute-start | bytes 589832 | tf_op jit(solution)/shard_map/ppermute | solution.py:33
  29.5 6.9 %collective-permute-start.15 = (bf16[128,768]{1,0:T(8,128)(2,1)S(1)}, bf16[128,768]{1,0:T(8,128)(2,1)S(1)}, u32[]{:S(2)}, u32[]{:S(2)}) collective-permute-start(bf16[128,768]{1,0:T(8,128)(2,1)S(1)} %collective-permute-done.3.refs_1_), channel_id=1, source_target_pairs={{0,224},{1,225},{2,226},{3,227},{4,228},{5,229},{6,230},{7,231},{8... | collective-permute-start | bytes 589832 | tf_op jit(solution)/shard_map/ppermute | solution.py:33
  31.9 5.7 %collective-permute-start.14 = (bf16[128,768]{1,0:T(8,128)(2,1)S(1)}, bf16[128,768]{1,0:T(8,128)(2,1)S(1)}, u32[]{:S(2)}, u32[]{:S(2)}) collective-permute-start(bf16[128,768]{1,0:T(8,128)(2,1)S(1)} %collective-permute-done.10.refs_0_), channel_id=1, source_target_pairs={{0,32},{1,33},{2,34},{3,35},{4,36},{5,37},{6,38},{7,39},{8,40},{9,... | collective-permute-start | bytes 589832 | tf_op jit(solution)/shard_map/ppermute | solution.py:33
  32.0 8.6 %collective-permute-start.9 = (bf16[128,768]{1,0:T(8,128)(2,1)S(1)}, bf16[128,768]{1,0:T(8,128)(2,1)S(1)}, u32[]{:S(2)}, u32[]{:S(2)}) collective-permute-start(bf16[128,768]{1,0:T(8,128)(2,1)S(1)} %collective-permute-done.6.refs_0_), channel_id=1, source_target_pairs={{0,32},{1,33},{2,34},{3,35},{4,36},{5,37},{6,38},{7,39},{8,40},{9,... | collective-permute-start | bytes 589832 | tf_op jit(solution)/shard_map/ppermute | solution.py:33
  33.5 7.4 %collective-permute-start.13 = (bf16[128,768]{1,0:T(8,128)(2,1)S(1)}, bf16[128,768]{1,0:T(8,128)(2,1)S(1)}, u32[]{:S(2)}, u32[]{:S(2)}) collective-permute-start(bf16[128,768]{1,0:T(8,128)(2,1)S(1)} %collective-permute-done.12.refs_1_), channel_id=1, source_target_pairs={{0,224},{1,225},{2,226},{3,227},{4,228},{5,229},{6,230},{7,231},{8... | collective-permute-start | bytes 589832 | tf_op jit(solution)/shard_map/ppermute | solution.py:33
  41.8 3.8 %collective-permute-start.16 = (f32[16,128]{1,0:T(8,128)S(1)}, f32[16,128]{1,0:T(8,128)S(1)}, u32[]{:S(2)}, u32[]{:S(2)}) collective-permute-start(f32[16,128]{1,0:T(8,128)S(1)} %shard_map.37), channel_id=1, source_target_pairs={{0,1},{1,16},{2,3},{3,18},{4,5},{5,20},{6,7},{7,22},{8,9},{9,24},{... | collective-permute-start | bytes 24584 | tf_op jit(solution)/shard_map/ppermute | solution.py:33
  41.9 4.8 %collective-permute-start.17 = (f32[16,128]{1,0:T(8,128)S(1)}, f32[16,128]{1,0:T(8,128)S(1)}, u32[]{:S(2)}, u32[]{:S(2)}) collective-permute-start(f32[16,128]{1,0:T(8,128)S(1)} %shard_map.37), channel_id=1, source_target_pairs={{0,16},{1,17},{2,18},{3,19},{4,20},{5,21},{6,22},{7,23},{8,24},{9,... | collective-permute-start | bytes 24584 | tf_op jit(solution)/shard_map/ppermute | solution.py:33
  45.5 2.5 %collective-permute-start.18 = (f32[16,128]{1,0:T(8,128)S(1)}, f32[16,128]{1,0:T(8,128)S(1)}, u32[]{:S(2)}, u32[]{:S(2)}) collective-permute-start(f32[16,128]{1,0:T(8,128)S(1)} %shard_map.37), channel_id=1, source_target_pairs={{0,17},{1,0},{2,19},{3,2},{4,21},{5,4},{6,23},{7,6},{8,25},{9,8},{... | collective-permute-start | bytes 24584 | tf_op jit(solution)/shard_map/ppermute | solution.py:33
  68.2 7.7 %copy-start.1 = (bf16[512,768]{1,0:T(8,128)(2,1)S(1)}, bf16[512,768]{1,0:T(8,128)(2,1)}, u32[]{:S(2)}) copy-start(bf16[512,768]{1,0:T(8,128)(2,1)} %cent_ref.1) | copy-start | bytes 2359300
  69.3 8.6 %collective-permute-start.20 = (f32[256,896]{1,0:T(8,128)S(1)}, f32[256,896]{1,0:T(8,128)S(1)}, u32[]{:S(2)}, u32[]{:S(2)}) collective-permute-start(f32[256,896]{1,0:T(8,128)S(1)} %shard_map.39), channel_id=1, source_target_pairs={{0,8},{1,9},{2,10},{3,11},{4,12},{5,13},{6,14},{7,15},{8,0},{9,1},... | collective-permute-start | bytes 2752520 | tf_op jit(solution)/shard_map/ppermute | solution.py:33
  75.8 3.4 %collective-permute-start.19 = (f32[256,896]{1,0:T(8,128)S(1)}, f32[256,896]{1,0:T(8,128)S(1)}, u32[]{:S(2)}, u32[]{:S(2)}) collective-permute-start(f32[256,896]{1,0:T(8,128)S(1)} %get-tuple-element.82), channel_id=1, source_target_pairs={{0,8},{1,9},{2,10},{3,11},{4,12},{5,13},{6,14},{7,15},{8,0},{9,1},... | collective-permute-start | bytes 2752520 | tf_op jit(solution)/shard_map/ppermute | solution.py:33

commit v5 on v4

--- a/solution.py
+++ b/solution.py
@@ -222,23 +222,33 @@
 def finish_kernel(own_ref, *refs):
     out_ref = refs[-1]
     rows, width = out_ref.shape
-    for k, ref in enumerate(refs[:-1]):
-
-        @pl.when(pl.program_id(0) == k)
-        def _():
-            both = own_ref[pl.ds(k * rows, rows), :] + ref[...]
-            weight = 1.0 / both[:, width:]
-            out_ref[...] = both[:, :width] * jnp.concatenate([weight] * (width // LANES), axis=1)
+    first = 0
+    for ref in refs[:-1]:
+        last = first + ref.shape[0]
+        for step in range(own_ref.shape[0] // rows):
+            start, stop = max(first, step * rows), min(last, (step + 1) * rows)
+            if start >= stop:
+                continue
+
+            @pl.when(pl.program_id(0) == step)
+            def _():
+                both = own_ref[pl.ds(start, stop - start), :] + ref[pl.ds(start - first, stop - start), :]
+                weight = 1.0 / both[:, width:]
+                out_ref[pl.ds(start - step * rows, stop - start), :] = both[:, :width] * jnp.concatenate(
+                    [weight] * (width // LANES), axis=1
+                )
+
+        first = last
 
 
 def finish(own, others):
     rows, wide = own.shape
     width = wide - LANES
-    steps = len(others)
+    steps = 2
     return pl.pallas_call(
         finish_kernel,
         grid=(steps,),
-        in_specs=[IN_VMEM] * (1 + steps),
+        in_specs=[IN_VMEM] * (1 + len(others)),
         out_specs=pl.BlockSpec((rows // steps, width), lambda i: (i, 0)),
         out_shape=jax.ShapeDtypeStruct((rows, width), jnp.float32),
         compiler_params=pltpu.CompilerParams(vmem_limit_bytes=8 * MIB),
@@ -294,19 +304,19 @@
 
     local = arrange(order, norms)
     local = combine(
-        jnp.stack([local] + [send(local, lambda x, y, z, c, k=k: ((x + k) % X, y, z, c)) for k in (1, 2, 3)])
+        jnp.stack([local] + [send(local, lambda x, y, z, c, k=k: ((x + k) % X, y, z, c)) for k in (2, 1, 3)])
     )
     everywhere = jnp.broadcast_to(local[None], (Y * Z,) + local.shape)
     parts = lax.all_to_all(everywhere, AXES, 0, 0, axis_index_groups=groups_by(lambda x, y, z, c: (x, c)))
 
     count, width = centroids.shape
-    piece = count // 2
+    piece = count * 5 // 8
     shape = (everything, width)
     one, norm = sums_call(
         functools.partial(first_sums_kernel, tuple(order), 0), (logits, blocks, parts), piece, *shape, len(order)
     )
     got_one = to_sibling(one)
-    two = sums_call(functools.partial(more_sums_kernel, piece), (logits, blocks, norm), piece, *shape)
+    two = sums_call(functools.partial(more_sums_kernel, piece), (logits, blocks, norm), count - piece, *shape)
     got_two = to_sibling(two)
     norm = after(norm, two)
     own_sums = sums_call(

time: 80.6 us -> 79.2 us (0.983)
  waiting for transfers between devices: 11.9 us -> 9.72 us
    ppermute x21, waiting for transfers between devices: 11.9 us -> 9.72 us  [send(): return lax.ppermute(block, AXES, route)]
  transfers between devices with their start and end apart: 21 -> 21, of which waited for: 9 -> 9; matrix products, arithmetic and copies ran while one was open for 0% -> 0% of each run, Pallas kernels for 10% -> 11%
where the time goes in v5:
time: 79.2 us; the launch traced here: 79 us
  starting transfers between devices  35.6 us (45%)
  blocking collectives  19 us (24%)
  Pallas kernels  12.2 us (15%)
  waiting for transfers between devices  9.72 us (12%)
  local copies, waits for them, and re-layouts  2.3 us (3%)
    ppermute x21, starting transfers between devices, send(): return lax.ppermute(block, AXES, route)  35.6 us
    all_to_all x1, blocking collectives, shards(): lax.all_to_all(everywhere, AXES, 0, 0, axis_index_groups=groups_by(lambda...  19 us
    ppermute x21, waiting for transfers between devices, send(): return lax.ppermute(block, AXES, route)  9.72 us
    pallas_call x8, Pallas kernels, logits_of(): pl.pallas_call(functools.partial(logits_kernel, len(blocks), first, len(b...  6.44 us
    pallas_call x3, Pallas kernels, sums_call(): pl.pallas_call(kernel, in_specs=[IN_VMEM] * len(operands), out_specs=(IN_...  4.12 us
    unnamed x6, local copies, waits for them, and re-layouts  2.28 us
  transfers between devices with their start and end apart: 21, of which 9 were waited for; matrix products, arithmetic and copies ran while one was open for 0% of the time, Pallas kernels for 11%

profile of v5, /device:TPU:1, one launch (start us, length us, event | category | flops | bytes accessed | tf_op | source)
XLA Modules:
  0.0 79.0 jit_solution(6874936339556902062)
XLA Ops:
  0.0 3.2 %collective-permute-start.5 = (bf16[512,768]{1,0:T(8,128)(2,1)}, bf16[512,768]{1,0:T(8,128)(2,1)S(1)}, u32[]{:S(2)}, u32[]{:S(2)}) collective-permute-start(bf16[512,768]{1,0:T(8,128)(2,1)} %cent_ref.1), channel_id=1, source_target_pairs={{0,8},{1,9},{2,10},{3,11},{4,12},{5,13},{6,14},{7,15},{8,0},{9,1},... | collective-permute-start | bytes 2359304 | tf_op jit(solution)/shard_map/ppermute | solution.py:33
  3.2 0.7 collective-permute-start.4
  4.0 1.6 %collective-permute-start = (bf16[128,768]{1,0:T(8,128)(2,1)}, bf16[128,768]{1,0:T(8,128)(2,1)S(1)}, u32[]{:S(2)}, u32[]{:S(2)}) collective-permute-start(bf16[128,768]{1,0:T(8,128)(2,1)} %refs_0_.1), channel_id=1, source_target_pairs={{0,32},{1,33},{2,34},{3,35},{4,36},{5,37},{6,38},{7,39},{8,40},{9,... | collective-permute-start | bytes 589832 | tf_op jit(solution)/shard_map/ppermute | solution.py:33
  5.6 3.9 %collective-permute-start.1 = (bf16[128,768]{1,0:T(8,128)(2,1)}, bf16[128,768]{1,0:T(8,128)(2,1)S(1)}, u32[]{:S(2)}, u32[]{:S(2)}) collective-permute-start(bf16[128,768]{1,0:T(8,128)(2,1)} %refs_0_.1), channel_id=1, source_target_pairs={{0,224},{1,225},{2,226},{3,227},{4,228},{5,229},{6,230},{7,231},{8... | collective-permute-start | bytes 589832 | tf_op jit(solution)/shard_map/ppermute | solution.py:33
  9.6 1.6 %collective-permute-done.4.refs_1_ = bf16[128,768]{1,0:T(8,128)(2,1)S(1)} collective-permute-done((bf16[128,768]{1,0:T(8,128)(2,1)}, bf16[128,768]{1,0:T(8,128)(2,1)S(1)}, u32[]{:S(2)}, u32[]{:S(2)}) %collective-permute-start.4) | collective-permute-done | bytes 196640 | tf_op jit(solution)/shard_map/ppermute | solution.py:33
  11.2 3.8 %collective-permute-start.8 = (bf16[128,768]{1,0:T(8,128)(2,1)S(1)}, bf16[128,768]{1,0:T(8,128)(2,1)S(1)}, u32[]{:S(2)}, u32[]{:S(2)}) collective-permute-start(bf16[128,768]{1,0:T(8,128)(2,1)S(1)} %collective-permute-done.4.refs_1_), channel_id=1, source_target_pairs={{0,224},{1,225},{2,226},{3,227},{4,228},{5,229},{6,230},{7,231},{8... | collective-permute-start | bytes 589832 | tf_op jit(solution)/shard_map/ppermute | solution.py:33
  15.0 0.0 collective-permute-done.refs_0_
  15.0 0.0 collective-permute-done.1.refs_1_
  15.0 0.0 collective-permute-start.2
  15.1 2.7 %collective-permute-start.3 = (bf16[128,768]{1,0:T(8,128)(2,1)S(1)}, bf16[128,768]{1,0:T(8,128)(2,1)S(1)}, u32[]{:S(2)}, u32[]{:S(2)}) collective-permute-start(bf16[128,768]{1,0:T(8,128)(2,1)S(1)} %collective-permute-done.1.refs_1_), channel_id=1, source_target_pairs={{0,224},{1,225},{2,226},{3,227},{4,228},{5,229},{6,230},{7,231},{8... | collective-permute-start | bytes 589832 | tf_op jit(solution)/shard_map/ppermute | solution.py:33
  17.7 1.1 %copy-done = bf16[512,768]{1,0:T(8,128)(2,1)S(1)} copy-done((bf16[512,768]{1,0:T(8,128)(2,1)S(1)}, bf16[512,768]{1,0:T(8,128)(2,1)}, u32[]{:S(2)}) %copy-start) | copy-done | bytes 786456
  18.9 0.4 shard_map.28
  19.3 0.9 %copy-done.2 = bf16[128,768]{1,0:T(8,128)(2,1)S(1)} copy-done((bf16[128,768]{1,0:T(8,128)(2,1)S(1)}, bf16[128,768]{1,0:T(8,128)(2,1)}, u32[]{:S(2)}) %copy-start.2) | copy-done | bytes 196632
  20.2 0.8 %shard_map.29 = (f32[1024,2048]{1,0:T(8,128)S(1)}, bf16[2048,768]{1,0:T(8,128)(2,1)S(1)}, f32[1,2048]{1,0:T(1,128)S(1)}) custom-call(bf16[128,768]{1,0:T(8,128)(2,1)S(1)} %copy-done.2, bf16[128,768]{1,0:T(8,128)(2,1)S(1)} %collective-permute-done.4.refs_1_, bf16[1024,768]{1,0:T(8,128)(2,1)S(1)} %get-tuple-element.46.refs_2_, ...), custom_call_target="tpu_custom_call" | custom-call | flops 1 | bytes 1 | tf_op jit(solution)/shard_map/pallas_call | solution.py:129
  21.0 0.0 collective-permute-done.8.refs_1_
  21.0 0.1 collective-permute-start.10
  21.1 2.7 %collective-permute-start.11 = (bf16[128,768]{1,0:T(8,128)(2,1)S(1)}, bf16[128,768]{1,0:T(8,128)(2,1)S(1)}, u32[]{:S(2)}, u32[]{:S(2)}) collective-permute-start(bf16[128,768]{1,0:T(8,128)(2,1)S(1)} %collective-permute-done.8.refs_1_), channel_id=1, source_target_pairs={{0,224},{1,225},{2,226},{3,227},{4,228},{5,229},{6,230},{7,231},{8... | collective-permute-start | bytes 589832 | tf_op jit(solution)/shard_map/ppermute | solution.py:33
  23.8 0.8 %shard_map.30 = (f32[1024,2048]{1,0:T(8,128)S(1)}, bf16[2048,768]{1,0:T(8,128)(2,1)S(1)}, f32[1,2048]{1,0:T(1,128)S(1)}) custom-call(bf16[128,768]{1,0:T(8,128)(2,1)S(1)} %collective-permute-done.refs_0_, bf16[128,768]{1,0:T(8,128)(2,1)S(1)} %collective-permute-done.1.refs_1_, ...), custom_call_target="tpu_custom_call", output_to_operand_aliasing={{0}: (4, {}), {1}: (5, {}), {2}: (6, {})} | custom-call | flops 1 | bytes 1 | tf_op jit(solution)/shard_map/pallas_call | solution.py:129
  24.6 2.2 %collective-permute-done.10.refs_0_ = bf16[128,768]{1,0:T(8,128)(2,1)S(1)} collective-permute-done((bf16[128,768]{1,0:T(8,128)(2,1)S(1)}, bf16[128,768]{1,0:T(8,128)(2,1)S(1)}, u32[]{:S(2)}, u32[]{:S(2)}) %collective-permute-start.10) | collective-permute-done | bytes 196640 | tf_op jit(solution)/shard_map/ppermute | solution.py:33
  26.8 2.7 %collective-permute-start.12 = (bf16[128,768]{1,0:T(8,128)(2,1)S(1)}, bf16[128,768]{1,0:T(8,128)(2,1)S(1)}, u32[]{:S(2)}, u32[]{:S(2)}) collective-permute-start(bf16[128,768]{1,0:T(8,128)(2,1)S(1)} %collective-permute-done.11.refs_1_), channel_id=1, source_target_pairs={{0,224},{1,225},{2,226},{3,227},{4,228},{5,229},{6,230},{7,231},{8... | collective-permute-start | bytes 589832 | tf_op jit(solution)/shard_map/ppermute | solution.py:33
  29.5 0.2 collective-permute-start.15
  29.7 0.8 %shard_map.31 = (f32[1024,2048]{1,0:T(8,128)S(1)}, bf16[2048,768]{1,0:T(8,128)(2,1)S(1)}, f32[1,2048]{1,0:T(1,128)S(1)}) custom-call(bf16[128,768]{1,0:T(8,128)(2,1)S(1)} %collective-permute-done.7.refs_0_, bf16[128,768]{1,0:T(8,128)(2,1)S(1)} %collective-permute-done.8.refs_1_, ...), custom_call_target="tpu_custom_call", output_to_operand_aliasing={{0}: (4, {}), {1}: (5, {}), {2}: (6, {})} | custom-call | flops 1 | bytes 1 | tf_op jit(solution)/shard_map/pallas_call | solution.py:129
  30.6 1.3 %collective-permute-done.6.refs_0_ = bf16[128,768]{1,0:T(8,128)(2,1)S(1)} collective-permute-done((bf16[128,768]{1,0:T(8,128)(2,1)S(1)}, bf16[128,768]{1,0:T(8,128)(2,1)S(1)}, u32[]{:S(2)}, u32[]{:S(2)}) %collective-permute-start.6) | collective-permute-done | bytes 196640 | tf_op jit(solution)/shard_map/ppermute | solution.py:33
  31.9 0.2 collective-permute-start.14
  32.0 0.7 collective-permute-start.9
  32.7 0.8 %shard_map.32 = (f32[1024,2048]{1,0:T(8,128)S(1)}, bf16[2048,768]{1,0:T(8,128)(2,1)S(1)}, f32[1,2048]{1,0:T(1,128)S(1)}) custom-call(bf16[128,768]{1,0:T(8,128)(2,1)S(1)} %collective-permute-done.2.refs_0_, bf16[128,768]{1,0:T(8,128)(2,1)S(1)} %collective-permute-done.3.refs_1_, ...), custom_call_target="tpu_custom_call", output_to_operand_aliasing={{0}: (4, {}), {1}: (5, {}), {2}: (6, {})} | custom-call | flops 1 | bytes 1 | tf_op jit(solution)/shard_map/pallas_call | solution.py:129
  33.5 2.1 %collective-permute-start.13 = (bf16[128,768]{1,0:T(8,128)(2,1)S(1)}, bf16[128,768]{1,0:T(8,128)(2,1)S(1)}, u32[]{:S(2)}, u32[]{:S(2)}) collective-permute-start(bf16[128,768]{1,0:T(8,128)(2,1)S(1)} %collective-permute-done.12.refs_1_), channel_id=1, source_target_pairs={{0,224},{1,225},{2,226},{3,227},{4,228},{5,229},{6,230},{7,231},{8... | collective-permute-start | bytes 589832 | tf_op jit(solution)/shard_map/ppermute | solution.py:33
  35.6 0.8 %shard_map.33 = (f32[1024,2048]{1,0:T(8,128)S(1)}, bf16[2048,768]{1,0:T(8,128)(2,1)S(1)}, f32[1,2048]{1,0:T(1,128)S(1)}) custom-call(bf16[128,768]{1,0:T(8,128)(2,1)S(1)} %collective-permute-done.10.refs_0_, bf16[128,768]{1,0:T(8,128)(2,1)S(1)} %collective-permute-done.11.refs_1_, ...), custom_call_target="tpu_custom_call", output_to_operand_aliasing={{0}: (4, {}), {1}: (5, {}), {2}: (6, {})} | custom-call | flops 1 | bytes 1 | tf_op jit(solution)/shard_map/pallas_call | solution.py:129
  36.4 0.8 %shard_map.34 = (f32[1024,2048]{1,0:T(8,128)S(1)}, bf16[2048,768]{1,0:T(8,128)(2,1)S(1)}, f32[1,2048]{1,0:T(1,128)S(1)}) custom-call(bf16[128,768]{1,0:T(8,128)(2,1)S(1)} %collective-permute-done.6.refs_0_, bf16[128,768]{1,0:T(8,128)(2,1)S(1)} %collective-permute-done.15.refs_1_, ...), custom_call_target="tpu_custom_call", output_to_operand_aliasing={{0}: (4, {}), {1}: (5, {}), {2}: (6, {})} | custom-call | flops 1 | bytes 1 | tf_op jit(solution)/shard_map/pallas_call | solution.py:129
  37.2 0.4 collective-permute-done.14.refs_0_
  37.6 0.8 %shard_map.35 = (f32[1024,2048]{1,0:T(8,128)S(1)}, bf16[2048,768]{1,0:T(8,128)(2,1)S(1)}, f32[1,2048]{1,0:T(1,128)S(1)}) custom-call(bf16[128,768]{1,0:T(8,128)(2,1)S(1)} %collective-permute-done.14.refs_0_, bf16[128,768]{1,0:T(8,128)(2,1)S(1)} %collective-permute-done.12.refs_1_, ...), custom_call_target="tpu_custom_call", output_to_operand_aliasing={{0}: (4, {}), {1}: (5, {}), {2}: (6, {})} | custom-call | flops 1 | bytes 1 | tf_op jit(solution)/shard_map/pallas_call | solution.py:129
  38.4 2.3 %collective-permute-done.9.refs_0_ = bf16[128,768]{1,0:T(8,128)(2,1)S(1)} collective-permute-done((bf16[128,768]{1,0:T(8,128)(2,1)S(1)}, bf16[128,768]{1,0:T(8,128)(2,1)S(1)}, u32[]{:S(2)}, u32[]{:S(2)}) %collective-permute-start.9) | collective-permute-done | bytes 196640 | tf_op jit(solution)/shard_map/ppermute | solution.py:33
  40.7 0.3 collective-permute-done.13.refs_1_
  40.9 0.8 %shard_map.36 = (f32[1024,2048]{1,0:T(8,128)S(1)}, bf16[2048,768]{1,0:T(8,128)(2,1)S(1)}, f32[1,2048]{1,0:T(1,128)S(1)}) custom-call(bf16[128,768]{1,0:T(8,128)(2,1)S(1)} %collective-permute-done.9.refs_0_, bf16[128,768]{1,0:T(8,128)(2,1)S(1)} %collective-permute-done.13.refs_1_, ...), custom_call_target="tpu_custom_call", output_to_operand_aliasing={{0}: (4, {}), {1}: (5, {}), {2}: (6, {})} | custom-call | flops 1 | bytes 1 | tf_op jit(solution)/shard_map/pallas_call | solution.py:129
  41.8 1.6 %collective-permute-start.16 = (f32[16,128]{1,0:T(8,128)S(1)}, f32[16,128]{1,0:T(8,128)S(1)}, u32[]{:S(2)}, u32[]{:S(2)}) collective-permute-start(f32[16,128]{1,0:T(8,128)S(1)} %shard_map.37), channel_id=1, source_target_pairs={{0,16},{1,17},{2,18},{3,19},{4,20},{5,21},{6,22},{7,23},{8,24},{9,... | collective-permute-start | bytes 24584 | tf_op jit(solution)/shard_map/ppermute | solution.py:33
  43.4 1.5 %collective-permute-start.17 = (f32[16,128]{1,0:T(8,128)S(1)}, f32[16,128]{1,0:T(8,128)S(1)}, u32[]{:S(2)}, u32[]{:S(2)}) collective-permute-start(f32[16,128]{1,0:T(8,128)S(1)} %shard_map.37), channel_id=1, source_target_pairs={{0,1},{1,16},{2,3},{3,18},{4,5},{5,20},{6,7},{7,22},{8,9},{9,24},{... | collective-permute-start | bytes 24584 | tf_op jit(solution)/shard_map/ppermute | solution.py:33
  44.9 1.1 %collective-permute-start.18 = (f32[16,128]{1,0:T(8,128)S(1)}, f32[16,128]{1,0:T(8,128)S(1)}, u32[]{:S(2)}, u32[]{:S(2)}) collective-permute-start(f32[16,128]{1,0:T(8,128)S(1)} %shard_map.37), channel_id=1, source_target_pairs={{0,17},{1,0},{2,19},{3,2},{4,21},{5,4},{6,23},{7,6},{8,25},{9,8},{... | collective-permute-start | bytes 24584 | tf_op jit(solution)/shard_map/ppermute | solution.py:33
  46.1 1.0 %collective-permute-done.17 = f32[16,128]{1,0:T(8,128)S(1)} collective-permute-done((f32[16,128]{1,0:T(8,128)S(1)}, f32[16,128]{1,0:T(8,128)S(1)}, u32[]{:S(2)}, u32[]{:S(2)}) %collective-permute-start.17) | collective-permute-done | bytes 8224 | tf_op jit(solution)/shard_map/ppermute | solution.py:33
  47.1 0.3 collective-permute-done.18
  47.5 19.0 %all_to_all.5.parts_ref = f32[32,16,128]{2,1,0:T(8,128)S(1)} all-to-all(f32[32,16,128]{2,1,0:T(8,128)S(1)} %broadcast_in_dim.2), channel_id=1, replica_groups={{0,2,4,6,32,34,36,38,64,66,68,70,96,98,100,102,128,130,132,134,160,162,..., dimensions={0} | all-to-all | bytes 524288 | tf_op jit(solution)/shard_map/all_to_all | solution.py:310
  66.5 1.3 %shard_map.38 = (f32[320,896]{1,0:T(8,128)S(1)}, f32[8,2048]{1,0:T(8,128)S(1)}) custom-call(f32[1024,2048]{1,0:T(8,128)S(1)} %get-tuple-element.77.logits_ref, bf16[2048,768]{1,0:T(8,128)(2,1)S(1)} %get-tuple-element.78.group_ref, f32[32,16,128]{2,1,0:T(8,128)S(1)} %all_to_all.5.parts_ref), custom_call_target="tpu_custom_call" | custom-call | flops 1 | bytes 1 | tf_op jit(solution)/shard_map/pallas_call | solution.py:211
  67.9 6.5 %collective-permute-start.19 = (f32[320,896]{1,0:T(8,128)S(1)}, f32[320,896]{1,0:T(8,128)S(1)}, u32[]{:S(2)}, u32[]{:S(2)}) collective-permute-start(f32[320,896]{1,0:T(8,128)S(1)} %get-tuple-element.82), channel_id=1, source_target_pairs={{0,8},{1,9},{2,10},{3,11},{4,12},{5,13},{6,14},{7,15},{8,0},{9,1},... | collective-permute-start | bytes 3440648 | tf_op jit(solution)/shard_map/ppermute | solution.py:33
  74.4 0.8 shard_map.39
  75.2 0.1 collective-permute-start.20
  75.3 0.2 copy-done.1
  75.5 2.0 %shard_map.40.own_ref = f32[512,896]{1,0:T(8,128)S(1)} custom-call(f32[1024,2048]{1,0:T(8,128)S(1)} %get-tuple-element.77.logits_ref, bf16[2048,768]{1,0:T(8,128)(2,1)S(1)} %get-tuple-element.78.group_ref, f32[8,2048]{1,0:T(8,128)S(1)} %get-tuple-element.81.norm_ref, bf16[512,768]{1,0:T(8,128)(2,1)S(1)} %copy-done.1), custom_call_target="tpu_custom_call" | custom-call | flops 1 | bytes 1 | tf_op jit(solution)/shard_map/pallas_call | solution.py:211
  77.5 0.3 collective-permute-done.20.refs_1_
  77.8 1.2 %shard_map.41 = f32[512,768]{1,0:T(8,128)} custom-call(f32[512,896]{1,0:T(8,128)S(1)} %shard_map.40.own_ref, f32[320,896]{1,0:T(8,128)S(1)} %collective-permute-done.19.refs_0_, f32[192,896]{1,0:T(8,128)S(1)} %collective-permute-done.20.refs_1_), custom_call_target="tpu_custom_call" | custom-call | flops 1179648 | bytes 1572864 | tf_op jit(solution)/shard_map/pallas_call | solution.py:248
  (19 shorter events, 0.1 us)
Async XLA Ops:
  0.0 17.7 %collective-permute-start.5 = (bf16[512,768]{1,0:T(8,128)(2,1)}, bf16[512,768]{1,0:T(8,128)(2,1)S(1)}, u32[]{:S(2)}, u32[]{:S(2)}) collective-permute-start(bf16[512,768]{1,0:T(8,128)(2,1)} %cent_ref.1), channel_id=1, source_target_pairs={{0,8},{1,9},{2,10},{3,11},{4,12},{5,13},{6,14},{7,15},{8,0},{9,1},... | collective-permute-start | bytes 2359304 | tf_op jit(solution)/shard_map/ppermute | solution.py:33
  3.2 8.0 %collective-permute-start.4 = (bf16[128,768]{1,0:T(8,128)(2,1)}, bf16[128,768]{1,0:T(8,128)(2,1)S(1)}, u32[]{:S(2)}, u32[]{:S(2)}) collective-permute-start(bf16[128,768]{1,0:T(8,128)(2,1)} %refs_0_.1), channel_id=1, source_target_pairs={{0,17},{1,16},{2,19},{3,18},{4,21},{5,20},{6,23},{7,22},{8,25},{9,... | collective-permute-start | bytes 589832 | tf_op jit(solution)/shard_map/ppermute | solution.py:33
  4.0 11.1 %collective-permute-start = (bf16[128,768]{1,0:T(8,128)(2,1)}, bf16[128,768]{1,0:T(8,128)(2,1)S(1)}, u32[]{:S(2)}, u32[]{:S(2)}) collective-permute-start(bf16[128,768]{1,0:T(8,128)(2,1)} %refs_0_.1), channel_id=1, source_target_pairs={{0,32},{1,33},{2,34},{3,35},{4,36},{5,37},{6,38},{7,39},{8,40},{9,... | collective-permute-start | bytes 589832 | tf_op jit(solution)/shard_map/ppermute | solution.py:33
  5.6 9.4 %collective-permute-start.1 = (bf16[128,768]{1,0:T(8,128)(2,1)}, bf16[128,768]{1,0:T(8,128)(2,1)S(1)}, u32[]{:S(2)}, u32[]{:S(2)}) collective-permute-start(bf16[128,768]{1,0:T(8,128)(2,1)} %refs_0_.1), channel_id=1, source_target_pairs={{0,224},{1,225},{2,226},{3,227},{4,228},{5,229},{6,230},{7,231},{8... | collective-permute-start | bytes 589832 | tf_op jit(solution)/shard_map/ppermute | solution.py:33
  11.2 9.8 %collective-permute-start.7 = (bf16[128,768]{1,0:T(8,128)(2,1)S(1)}, bf16[128,768]{1,0:T(8,128)(2,1)S(1)}, u32[]{:S(2)}, u32[]{:S(2)}) collective-permute-start(bf16[128,768]{1,0:T(8,128)(2,1)S(1)} %collective-permute-done.4.refs_1_), channel_id=1, source_target_pairs={{0,32},{1,33},{2,34},{3,35},{4,36},{5,37},{6,38},{7,39},{8,40},{9,... | collective-permute-start | bytes 589832 | tf_op jit(solution)/shard_map/ppermute | solution.py:33
  11.2 9.8 %collective-permute-start.8 = (bf16[128,768]{1,0:T(8,128)(2,1)S(1)}, bf16[128,768]{1,0:T(8,128)(2,1)S(1)}, u32[]{:S(2)}, u32[]{:S(2)}) collective-permute-start(bf16[128,768]{1,0:T(8,128)(2,1)S(1)} %collective-permute-done.4.refs_1_), channel_id=1, source_target_pairs={{0,224},{1,225},{2,226},{3,227},{4,228},{5,229},{6,230},{7,231},{8... | collective-permute-start | bytes 589832 | tf_op jit(solution)/shard_map/ppermute | solution.py:33
  15.0 8.7 %collective-permute-start.2 = (bf16[128,768]{1,0:T(8,128)(2,1)S(1)}, bf16[128,768]{1,0:T(8,128)(2,1)S(1)}, u32[]{:S(2)}, u32[]{:S(2)}) collective-permute-start(bf16[128,768]{1,0:T(8,128)(2,1)S(1)} %collective-permute-done.refs_0_), channel_id=1, source_target_pairs={{0,32},{1,33},{2,34},{3,35},{4,36},{5,37},{6,38},{7,39},{8,40},{9,... | collective-permute-start | bytes 589832 | tf_op jit(solution)/shard_map/ppermute | solution.py:33
  15.1 8.7 %collective-permute-start.3 = (bf16[128,768]{1,0:T(8,128)(2,1)S(1)}, bf16[128,768]{1,0:T(8,128)(2,1)S(1)}, u32[]{:S(2)}, u32[]{:S(2)}) collective-permute-start(bf16[128,768]{1,0:T(8,128)(2,1)S(1)} %collective-permute-done.1.refs_1_), channel_id=1, source_target_pairs={{0,224},{1,225},{2,226},{3,227},{4,228},{5,229},{6,230},{7,231},{8... | collective-permute-start | bytes 589832 | tf_op jit(solution)/shard_map/ppermute | solution.py:33
  17.7 1.1 %copy-start = (bf16[512,768]{1,0:T(8,128)(2,1)S(1)}, bf16[512,768]{1,0:T(8,128)(2,1)}, u32[]{:S(2)}) copy-start(bf16[512,768]{1,0:T(8,128)(2,1)} %cent_ref.1) | copy-start | bytes 2359300
  19.3 0.9 %copy-start.2 = (bf16[128,768]{1,0:T(8,128)(2,1)S(1)}, bf16[128,768]{1,0:T(8,128)(2,1)}, u32[]{:S(2)}) copy-start(bf16[128,768]{1,0:T(8,128)(2,1)} %refs_0_.1) | copy-start | bytes 589828
  21.0 5.8 %collective-permute-start.10 = (bf16[128,768]{1,0:T(8,128)(2,1)S(1)}, bf16[128,768]{1,0:T(8,128)(2,1)S(1)}, u32[]{:S(2)}, u32[]{:S(2)}) collective-permute-start(bf16[128,768]{1,0:T(8,128)(2,1)S(1)} %collective-permute-done.7.refs_0_), channel_id=1, source_target_pairs={{0,32},{1,33},{2,34},{3,35},{4,36},{5,37},{6,38},{7,39},{8,40},{9,... | collective-permute-start | bytes 589832 | tf_op jit(solution)/shard_map/ppermute | solution.py:33
  21.1 5.7 %collective-permute-start.11 = (bf16[128,768]{1,0:T(8,128)(2,1)S(1)}, bf16[128,768]{1,0:T(8,128)(2,1)S(1)}, u32[]{:S(2)}, u32[]{:S(2)}) collective-permute-start(bf16[128,768]{1,0:T(8,128)(2,1)S(1)} %collective-permute-done.8.refs_1_), channel_id=1, source_target_pairs={{0,224},{1,225},{2,226},{3,227},{4,228},{5,229},{6,230},{7,231},{8... | collective-permute-start | bytes 589832 | tf_op jit(solution)/shard_map/ppermute | solution.py:33
  23.8 8.1 %collective-permute-start.6 = (bf16[128,768]{1,0:T(8,128)(2,1)S(1)}, bf16[128,768]{1,0:T(8,128)(2,1)S(1)}, u32[]{:S(2)}, u32[]{:S(2)}) collective-permute-start(bf16[128,768]{1,0:T(8,128)(2,1)S(1)} %collective-permute-done.2.refs_0_), channel_id=1, source_target_pairs={{0,32},{1,33},{2,34},{3,35},{4,36},{5,37},{6,38},{7,39},{8,40},{9,... | collective-permute-start | bytes 589832 | tf_op jit(solution)/shard_map/ppermute | solution.py:33
  26.8 6.7 %collective-permute-start.12 = (bf16[128,768]{1,0:T(8,128)(2,1)S(1)}, bf16[128,768]{1,0:T(8,128)(2,1)S(1)}, u32[]{:S(2)}, u32[]{:S(2)}) collective-permute-start(bf16[128,768]{1,0:T(8,128)(2,1)S(1)} %collective-permute-done.11.refs_1_), channel_id=1, source_target_pairs={{0,224},{1,225},{2,226},{3,227},{4,228},{5,229},{6,230},{7,231},{8... | collective-permute-start | bytes 589832 | tf_op jit(solution)/shard_map/ppermute | solution.py:33
  29.5 6.9 %collective-permute-start.15 = (bf16[128,768]{1,0:T(8,128)(2,1)S(1)}, bf16[128,768]{1,0:T(8,128)(2,1)S(1)}, u32[]{:S(2)}, u32[]{:S(2)}) collective-permute-start(bf16[128,768]{1,0:T(8,128)(2,1)S(1)} %collective-permute-done.3.refs_1_), channel_id=1, source_target_pairs={{0,224},{1,225},{2,226},{3,227},{4,228},{5,229},{6,230},{7,231},{8... | collective-permute-start | bytes 589832 | tf_op jit(solution)/shard_map/ppermute | solution.py:33
  31.9 5.7 %collective-permute-start.14 = (bf16[128,768]{1,0:T(8,128)(2,1)S(1)}, bf16[128,768]{1,0:T(8,128)(2,1)S(1)}, u32[]{:S(2)}, u32[]{:S(2)}) collective-permute-start(bf16[128,768]{1,0:T(8,128)(2,1)S(1)} %collective-permute-done.10.refs_0_), channel_id=1, source_target_pairs={{0,32},{1,33},{2,34},{3,35},{4,36},{5,37},{6,38},{7,39},{8,40},{9,... | collective-permute-start | bytes 589832 | tf_op jit(solution)/shard_map/ppermute | solution.py:33
  32.0 8.6 %collective-permute-start.9 = (bf16[128,768]{1,0:T(8,128)(2,1)S(1)}, bf16[128,768]{1,0:T(8,128)(2,1)S(1)}, u32[]{:S(2)}, u32[]{:S(2)}) collective-permute-start(bf16[128,768]{1,0:T(8,128)(2,1)S(1)} %collective-permute-done.6.refs_0_), channel_id=1, source_target_pairs={{0,32},{1,33},{2,34},{3,35},{4,36},{5,37},{6,38},{7,39},{8,40},{9,... | collective-permute-start | bytes 589832 | tf_op jit(solution)/shard_map/ppermute | solution.py:33
  33.5 7.4 %collective-permute-start.13 = (bf16[128,768]{1,0:T(8,128)(2,1)S(1)}, bf16[128,768]{1,0:T(8,128)(2,1)S(1)}, u32[]{:S(2)}, u32[]{:S(2)}) collective-permute-start(bf16[128,768]{1,0:T(8,128)(2,1)S(1)} %collective-permute-done.12.refs_1_), channel_id=1, source_target_pairs={{0,224},{1,225},{2,226},{3,227},{4,228},{5,229},{6,230},{7,231},{8... | collective-permute-start | bytes 589832 | tf_op jit(solution)/shard_map/ppermute | solution.py:33
  41.8 4.3 %collective-permute-start.16 = (f32[16,128]{1,0:T(8,128)S(1)}, f32[16,128]{1,0:T(8,128)S(1)}, u32[]{:S(2)}, u32[]{:S(2)}) collective-permute-start(f32[16,128]{1,0:T(8,128)S(1)} %shard_map.37), channel_id=1, source_target_pairs={{0,16},{1,17},{2,18},{3,19},{4,20},{5,21},{6,22},{7,23},{8,24},{9,... | collective-permute-start | bytes 24584 | tf_op jit(solution)/shard_map/ppermute | solution.py:33
  43.4 3.7 %collective-permute-start.17 = (f32[16,128]{1,0:T(8,128)S(1)}, f32[16,128]{1,0:T(8,128)S(1)}, u32[]{:S(2)}, u32[]{:S(2)}) collective-permute-start(f32[16,128]{1,0:T(8,128)S(1)} %shard_map.37), channel_id=1, source_target_pairs={{0,1},{1,16},{2,3},{3,18},{4,5},{5,20},{6,7},{7,22},{8,9},{9,24},{... | collective-permute-start | bytes 24584 | tf_op jit(solution)/shard_map/ppermute | solution.py:33
  44.9 2.5 %collective-permute-start.18 = (f32[16,128]{1,0:T(8,128)S(1)}, f32[16,128]{1,0:T(8,128)S(1)}, u32[]{:S(2)}, u32[]{:S(2)}) collective-permute-start(f32[16,128]{1,0:T(8,128)S(1)} %shard_map.37), channel_id=1, source_target_pairs={{0,17},{1,0},{2,19},{3,2},{4,21},{5,4},{6,23},{7,6},{8,25},{9,8},{... | collective-permute-start | bytes 24584 | tf_op jit(solution)/shard_map/ppermute | solution.py:33
  67.9 9.9 %collective-permute-start.19 = (f32[320,896]{1,0:T(8,128)S(1)}, f32[320,896]{1,0:T(8,128)S(1)}, u32[]{:S(2)}, u32[]{:S(2)}) collective-permute-start(f32[320,896]{1,0:T(8,128)S(1)} %get-tuple-element.82), channel_id=1, source_target_pairs={{0,8},{1,9},{2,10},{3,11},{4,12},{5,13},{6,14},{7,15},{8,0},{9,1},... | collective-permute-start | bytes 3440648 | tf_op jit(solution)/shard_map/ppermute | solution.py:33
  74.4 1.1 %copy-start.1 = (bf16[512,768]{1,0:T(8,128)(2,1)S(1)}, bf16[512,768]{1,0:T(8,128)(2,1)}, u32[]{:S(2)}) copy-start(bf16[512,768]{1,0:T(8,128)(2,1)} %cent_ref.1) | copy-start | bytes 2359300
  75.2 2.6 %collective-permute-start.20 = (f32[192,896]{1,0:T(8,128)S(1)}, f32[192,896]{1,0:T(8,128)S(1)}, u32[]{:S(2)}, u32[]{:S(2)}) collective-permute-start(f32[192,896]{1,0:T(8,128)S(1)} %shard_map.39), channel_id=1, source_target_pairs={{0,8},{1,9},{2,10},{3,11},{4,12},{5,13},{6,14},{7,15},{8,0},{9,1},... | collective-permute-start | bytes 2064392 | tf_op jit(solution)/shard_map/ppermute | solution.py:33

commit v6 on v5

--- a/solution.py
+++ b/solution.py
@@ -64,32 +64,52 @@
     return top + jnp.log(jnp.sum(jnp.exp2(parts - top), axis=0)) * LOG2E
 
 
-def prepare_kernel(other_ref, own_ref, both_ref, bias_ref):
-    half, width = own_ref.shape
-    for at, ref in enumerate((other_ref, own_ref)):
-        block = ref[...]
-        both_ref[pl.ds(at * half, half), :] = block
-        wide = block.astype(jnp.float32)
-        squares = jnp.sum(wide * wide, axis=1, keepdims=True)
-        bias_ref[pl.ds(at * half, half), :] = jnp.broadcast_to(squares * (SHARP / width * LOG2E), (half, LANES))
-
-
-def prepare(other, own):
-    rows, width = own.shape
-    return pl.pallas_call(
-        prepare_kernel,
+def squares_of(block):
+    wide = block.astype(jnp.float32)
+    return jnp.sum(wide * wide, axis=1, keepdims=True) * (SHARP / block.shape[1] * LOG2E)
+
+
+def bias_kernel(cent_ref, bias_ref):
+    bias_ref[...] = jnp.broadcast_to(squares_of(cent_ref[...]), bias_ref.shape)
+
+
+def bias_of(cents):
+    return pl.pallas_call(
+        bias_kernel,
+        in_specs=[IN_VMEM],
+        out_specs=IN_VMEM,
+        out_shape=here((cents.shape[0], LANES), jnp.float32),
+        compiler_params=pltpu.CompilerParams(vmem_limit_bytes=8 * MIB),
+        cost_estimate=pl.CostEstimate(flops=1, bytes_accessed=1, transcendentals=0),
+    )(*pinned(cents))
+
+
+def begin_kernel(point_ref, cent_ref, point_out, cent_out, bias_ref):
+    point_out[...] = point_ref[...]
+    cents = cent_ref[...]
+    cent_out[...] = cents
+    bias_ref[...] = jnp.broadcast_to(squares_of(cents), bias_ref.shape)
+
+
+def begin(points, cents):
+    return pl.pallas_call(
+        begin_kernel,
         in_specs=[IN_VMEM, IN_VMEM],
-        out_specs=(IN_VMEM, IN_VMEM),
-        out_shape=(here((2 * rows, width), own.dtype), here((2 * rows, LANES), jnp.float32)),
+        out_specs=(IN_VMEM,) * 3,
+        out_shape=(
+            here(points.shape, points.dtype),
+            here(cents.shape, cents.dtype),
+            here((cents.shape[0], LANES), jnp.float32),
+        ),
         compiler_params=pltpu.CompilerParams(vmem_limit_bytes=8 * MIB),
         cost_estimate=pl.CostEstimate(flops=1, bytes_accessed=1, transcendentals=0),
-    )(other, own)
+    )(points, cents)
 
 
 def logits_kernel(count, first, aliased, *refs):
     blocks = refs[:count]
-    cent_ref, bias_ref = refs[count : count + 2]
-    logits_ref, group_ref, norm_ref, xsq_ref = refs[count + 2 + 3 * aliased :]
+    cent_refs, bias_refs = refs[count : count + 2], refs[count + 2 : count + 4]
+    logits_ref, group_ref, norm_ref, xsq_ref = refs[count + 4 + 3 * aliased :]
     rows, width = blocks[0].shape
     points = rows * count
     scale = SHARP / width * LOG2E
@@ -97,19 +117,18 @@
     for at, ref in enumerate(blocks):
         block = ref[...]
         group_ref[pl.ds(first + at * rows, rows), :] = block
-        wide = block.astype(jnp.float32)
-        squares = jnp.sum(wide * wide, axis=1, keepdims=True) * scale
-        xsq_ref[:, pl.ds(at * rows, rows)] = jnp.broadcast_to(squares, (rows, LANES)).T[:8]
+        xsq_ref[:, pl.ds(at * rows, rows)] = jnp.broadcast_to(squares_of(block), (rows, LANES)).T[:8]
     group = group_ref[columns, :]
     xsq = xsq_ref[:1, :]
-    tiles = cent_ref.shape[0] // TILE
+    half = cent_refs[0].shape[0] // TILE
+    tiles = 2 * half
     high = None
     for t in range(tiles):
-        here_rows = pl.ds(t * TILE, TILE)
+        here_rows, within = pl.ds(t * TILE, TILE), pl.ds(t % half * TILE, TILE)
         dots = lax.dot_general(
-            cent_ref[here_rows, :], group, (((1,), (1,)), ((), ())), preferred_element_type=jnp.float32
+            cent_refs[t // half][within, :], group, (((1,), (1,)), ((), ())), preferred_element_type=jnp.float32
         )
-        bias = jnp.concatenate([bias_ref[here_rows, :]] * (points // LANES), axis=1)
+        bias = jnp.concatenate([bias_refs[t // half][within, :]] * (points // LANES), axis=1)
         logits = 2.0 * scale * dots - (bias + xsq)
         logits_ref[here_rows, columns] = logits
         top = jnp.max(logits, axis=0, keepdims=True)
@@ -123,9 +142,9 @@
 
 def logits_of(blocks, first, points, cents, bias, before):
     rows, width = blocks[0].shape
-    count = cents.shape[0]
+    count = 2 * cents[0].shape[0]
     more = rows * len(blocks)
-    operands = [*blocks, cents, bias, *before]
+    operands = [*blocks, *cents, *bias, *before]
     return pl.pallas_call(
         functools.partial(logits_kernel, len(blocks), first, len(before) > 0),
         in_specs=[IN_VMEM] * len(operands),
@@ -135,10 +154,10 @@
             here((points, width), blocks[0].dtype),
             here((1, points), jnp.float32),
         ),
-        input_output_aliases={len(blocks) + 2 + k: k for k in range(len(before))},
+        input_output_aliases={len(blocks) + 4 + k: k for k in range(len(before))},
         scratch_shapes=[pltpu.VMEM((8, more), jnp.float32)],
         compiler_params=pltpu.CompilerParams(vmem_limit_bytes=8 * MIB),
-        cost_estimate=pl.CostEstimate(flops=1, bytes_accessed=1, transcendentals=0),
+        cost_estimate=pl.CostEstimate(flops=2 * count * more * width, bytes_accessed=1, transcendentals=0),
     )(*pinned(*operands))
 
 
@@ -265,7 +284,9 @@
     everything = rows * Z * 2
 
     across = send(points, lambda x, y, z, c: (3 - x, y, z, c))
-    cents, bias = prepare(to_sibling(centroids), centroids)
+    other_cents = to_sibling(centroids)
+    held, own_cents, own_bias = begin(points, centroids)
+    cents, bias = (other_cents, own_cents), (bias_of(other_cents), own_bias)
 
     order, state = [], []
 
@@ -278,14 +299,14 @@
     own, far = [points, points], [across, across]
     both_ways = lambda pair: [along_z(pair[0], 1), along_z(pair[1], -1)]
     own = both_ways(own)
-    far = both_ways(far)
-    pending = [([points, across], [(0, 0), (0, 1)])]
+    far = both_ways(after(far, held))
+    pending = [([held, across], [(0, 0), (0, 1)])]
     for step in (1, 2, 3):
         seen = [] if step == 1 else state[2]
         if step < 3:
             next_own = both_ways(after(own, seen))
         else:
-            next_own = [along_z(after(own[0], seen), 1)]
+            next_own = [along_z(own[0], 1)]
         take(*pending.pop(0))
         seen = state[2]
         if step < 3:
@@ -320,7 +341,7 @@
     got_two = to_sibling(two)
     norm = after(norm, two)
     own_sums = sums_call(
-        functools.partial(own_sums_kernel, count), (logits, blocks, norm, centroids), count, *shape
+        functools.partial(own_sums_kernel, count), (logits, blocks, norm, own_cents), count, *shape
     )
     return finish(own_sums, (got_one, got_two))
 

time: 79.2 us -> 78.8 us (level)
    unnamed x6 -> x4, local copies, waits for them, and re-layouts: 2.28 us -> 2.06 us
  transfers between devices with their start and end apart: 21 -> 21, of which waited for: 9 -> 8; matrix products, arithmetic and copies ran while one was open for 0% -> 0% of each run, Pallas kernels for 11% -> 11%
where the time goes in v6:
time: 78.8 us; the launch traced here: 78.6 us
  starting transfers between devices  35.5 us (45%)
  blocking collectives  18.9 us (24%)
  Pallas kernels  12.3 us (16%)
  waiting for transfers between devices  9.68 us (12%)
  local copies, waits for them, and re-layouts  2.08 us (3%)
    ppermute x21, starting transfers between devices, send(): return lax.ppermute(block, AXES, route)  35.5 us
    all_to_all x1, blocking collectives, shards(): lax.all_to_all(everywhere, AXES, 0, 0, axis_index_groups=groups_by(lambda...  18.9 us
    ppermute x21, waiting for transfers between devices, send(): return lax.ppermute(block, AXES, route)  9.68 us
    pallas_call x8, Pallas kernels, logits_of(): pl.pallas_call(functools.partial(logits_kernel, len(blocks), first, len(b...  6.45 us
    pallas_call x3, Pallas kernels, sums_call(): pl.pallas_call(kernel, in_specs=[IN_VMEM] * len(operands), out_specs=(IN_...  4.11 us
    unnamed x4, local copies, waits for them, and re-layouts  2.06 us
  transfers between devices with their start and end apart: 21, of which 8 were waited for; matrix products, arithmetic and copies ran while one was open for 0% of the time, Pallas kernels for 11%

profile of v6, /device:TPU:1, one launch (start us, length us, event | category | flops | bytes accessed | tf_op | source)
XLA Modules:
  0.0 78.6 jit_solution(14736088495920148452)
XLA Ops:
  0.0 3.2 %collective-permute-start.5 = (bf16[512,768]{1,0:T(8,128)(2,1)}, bf16[512,768]{1,0:T(8,128)(2,1)S(1)}, u32[]{:S(2)}, u32[]{:S(2)}) collective-permute-start(bf16[512,768]{1,0:T(8,128)(2,1)} %cent_ref.1), channel_id=1, source_target_pairs={{0,8},{1,9},{2,10},{3,11},{4,12},{5,13},{6,14},{7,15},{8,0},{9,1},... | collective-permute-start | bytes 2359304 | tf_op jit(solution)/shard_map/ppermute | solution.py:33
  3.2 0.7 collective-permute-start.4
  4.0 1.6 %collective-permute-start = (bf16[128,768]{1,0:T(8,128)(2,1)}, bf16[128,768]{1,0:T(8,128)(2,1)S(1)}, u32[]{:S(2)}, u32[]{:S(2)}) collective-permute-start(bf16[128,768]{1,0:T(8,128)(2,1)} %point_ref.1), channel_id=1, source_target_pairs={{0,32},{1,33},{2,34},{3,35},{4,36},{5,37},{6,38},{7,39},{8,40},{9,... | collective-permute-start | bytes 589832 | tf_op jit(solution)/shard_map/ppermute | solution.py:33
  5.6 3.9 %collective-permute-start.1 = (bf16[128,768]{1,0:T(8,128)(2,1)}, bf16[128,768]{1,0:T(8,128)(2,1)S(1)}, u32[]{:S(2)}, u32[]{:S(2)}) collective-permute-start(bf16[128,768]{1,0:T(8,128)(2,1)} %point_ref.1), channel_id=1, source_target_pairs={{0,224},{1,225},{2,226},{3,227},{4,228},{5,229},{6,230},{7,231},{8... | collective-permute-start | bytes 589832 | tf_op jit(solution)/shard_map/ppermute | solution.py:33
  9.6 1.1 %copy-done = bf16[512,768]{1,0:T(8,128)(2,1)S(1)} copy-done((bf16[512,768]{1,0:T(8,128)(2,1)S(1)}, bf16[512,768]{1,0:T(8,128)(2,1)}, u32[]{:S(2)}) %copy-start) | copy-done | bytes 786456
  10.7 0.9 %copy-done.1 = bf16[128,768]{1,0:T(8,128)(2,1)S(1)} copy-done((bf16[128,768]{1,0:T(8,128)(2,1)S(1)}, bf16[128,768]{1,0:T(8,128)(2,1)}, u32[]{:S(2)}) %copy-start.1) | copy-done | bytes 196632
  11.6 0.2 shard_map.28
  11.9 0.1 collective-permute-start.8
  12.0 3.1 %collective-permute-start.9 = (bf16[128,768]{1,0:T(8,128)(2,1)S(1)}, bf16[128,768]{1,0:T(8,128)(2,1)S(1)}, u32[]{:S(2)}, u32[]{:S(2)}) collective-permute-start(bf16[128,768]{1,0:T(8,128)(2,1)S(1)} %collective-permute-done.4.refs_1_), channel_id=1, source_target_pairs={{0,224},{1,225},{2,226},{3,227},{4,228},{5,229},{6,230},{7,231},{8... | collective-permute-start | bytes 589832 | tf_op jit(solution)/shard_map/ppermute | solution.py:33
  15.0 0.0 collective-permute-done.refs_0_
  15.1 2.7 %collective-permute-start.3 = (bf16[128,768]{1,0:T(8,128)(2,1)S(1)}, bf16[128,768]{1,0:T(8,128)(2,1)S(1)}, u32[]{:S(2)}, u32[]{:S(2)}) collective-permute-start(bf16[128,768]{1,0:T(8,128)(2,1)S(1)} %collective-permute-done.1.refs_1_), channel_id=1, source_target_pairs={{0,224},{1,225},{2,226},{3,227},{4,228},{5,229},{6,230},{7,231},{8... | collective-permute-start | bytes 589832 | tf_op jit(solution)/shard_map/ppermute | solution.py:33
  17.7 0.0 collective-permute-done.5.cent_ref.refs_2_
  17.7 0.2 shard_map.29.refs_4_
  18.0 0.8 %shard_map.30 = (f32[1024,2048]{1,0:T(8,128)S(1)}, bf16[2048,768]{1,0:T(8,128)(2,1)S(1)}, f32[1,2048]{1,0:T(1,128)S(1)}) custom-call(bf16[128,768]{1,0:T(8,128)(2,1)S(1)} %get-tuple-element.48.refs_0_, bf16[128,768]{1,0:T(8,128)(2,1)S(1)} %collective-permute-done.4.refs_1_, bf16[512,768]{1,0:T(8,128)(2,1)S(1)} %collective-permute-done.5.cent_ref.refs_2_, ...), custom_call_target="tpu_custom_call" | custom-call | flops 402653184 | bytes 1 | tf_op jit(solution)/shard_map/pallas_call | solution.py:148
  18.8 0.8 collective-permute-done.8.refs_0_
  19.5 0.0 collective-permute-done.9.refs_1_
  19.5 0.0 collective-permute-start.10
  19.5 2.7 %collective-permute-start.11 = (bf16[128,768]{1,0:T(8,128)(2,1)S(1)}, bf16[128,768]{1,0:T(8,128)(2,1)S(1)}, u32[]{:S(2)}, u32[]{:S(2)}) collective-permute-start(bf16[128,768]{1,0:T(8,128)(2,1)S(1)} %collective-permute-done.9.refs_1_), channel_id=1, source_target_pairs={{0,224},{1,225},{2,226},{3,227},{4,228},{5,229},{6,230},{7,231},{8... | collective-permute-start | bytes 589832 | tf_op jit(solution)/shard_map/ppermute | solution.py:33
  22.2 1.5 %collective-permute-done.2.refs_0_ = bf16[128,768]{1,0:T(8,128)(2,1)S(1)} collective-permute-done((bf16[128,768]{1,0:T(8,128)(2,1)S(1)}, bf16[128,768]{1,0:T(8,128)(2,1)S(1)}, u32[]{:S(2)}, u32[]{:S(2)}) %collective-permute-start.2) | collective-permute-done | bytes 196640 | tf_op jit(solution)/shard_map/ppermute | solution.py:33
  23.7 0.0 collective-permute-done.3.refs_1_
  23.8 0.8 %shard_map.31 = (f32[1024,2048]{1,0:T(8,128)S(1)}, bf16[2048,768]{1,0:T(8,128)(2,1)S(1)}, f32[1,2048]{1,0:T(1,128)S(1)}) custom-call(bf16[128,768]{1,0:T(8,128)(2,1)S(1)} %collective-permute-done.refs_0_, bf16[128,768]{1,0:T(8,128)(2,1)S(1)} %collective-permute-done.1.refs_1_, ...), custom_call_target="tpu_custom_call", output_to_operand_aliasing={{0}: (6, {}), {1}: (7, {}), {2}: (8, {})} | custom-call | flops 402653184 | bytes 1 | tf_op jit(solution)/shard_map/pallas_call | solution.py:148
  24.6 2.7 %collective-permute-done.10.refs_0_ = bf16[128,768]{1,0:T(8,128)(2,1)S(1)} collective-permute-done((bf16[128,768]{1,0:T(8,128)(2,1)S(1)}, bf16[128,768]{1,0:T(8,128)(2,1)S(1)}, u32[]{:S(2)}, u32[]{:S(2)}) %collective-permute-start.10) | collective-permute-done | bytes 196640 | tf_op jit(solution)/shard_map/ppermute | solution.py:33
  27.3 2.4 %collective-permute-start.12 = (bf16[128,768]{1,0:T(8,128)(2,1)S(1)}, bf16[128,768]{1,0:T(8,128)(2,1)S(1)}, u32[]{:S(2)}, u32[]{:S(2)}) collective-permute-start(bf16[128,768]{1,0:T(8,128)(2,1)S(1)} %collective-permute-done.11.refs_1_), channel_id=1, source_target_pairs={{0,224},{1,225},{2,226},{3,227},{4,228},{5,229},{6,230},{7,231},{8... | collective-permute-start | bytes 589832 | tf_op jit(solution)/shard_map/ppermute | solution.py:33
  29.7 0.0 collective-permute-start.15
  29.7 1.4 %collective-permute-start.14 = (bf16[128,768]{1,0:T(8,128)(2,1)S(1)}, bf16[128,768]{1,0:T(8,128)(2,1)S(1)}, u32[]{:S(2)}, u32[]{:S(2)}) collective-permute-start(bf16[128,768]{1,0:T(8,128)(2,1)S(1)} %collective-permute-done.10.refs_0_), channel_id=1, source_target_pairs={{0,32},{1,33},{2,34},{3,35},{4,36},{5,37},{6,38},{7,39},{8,40},{9,... | collective-permute-start | bytes 589832 | tf_op jit(solution)/shard_map/ppermute | solution.py:33
  31.2 0.4 collective-permute-done.6.refs_0_
  31.5 0.0 collective-permute-start.7
  31.5 0.8 %shard_map.32 = (f32[1024,2048]{1,0:T(8,128)S(1)}, bf16[2048,768]{1,0:T(8,128)(2,1)S(1)}, f32[1,2048]{1,0:T(1,128)S(1)}) custom-call(bf16[128,768]{1,0:T(8,128)(2,1)S(1)} %collective-permute-done.8.refs_0_, bf16[128,768]{1,0:T(8,128)(2,1)S(1)} %collective-permute-done.9.refs_1_, ...), custom_call_target="tpu_custom_call", output_to_operand_aliasing={{0}: (6, {}), {1}: (7, {}), {2}: (8, {})} | custom-call | flops 402653184 | bytes 1 | tf_op jit(solution)/shard_map/pallas_call | solution.py:148
  32.4 0.8 %shard_map.33 = (f32[1024,2048]{1,0:T(8,128)S(1)}, bf16[2048,768]{1,0:T(8,128)(2,1)S(1)}, f32[1,2048]{1,0:T(1,128)S(1)}) custom-call(bf16[128,768]{1,0:T(8,128)(2,1)S(1)} %collective-permute-done.2.refs_0_, bf16[128,768]{1,0:T(8,128)(2,1)S(1)} %collective-permute-done.3.refs_1_, ...), custom_call_target="tpu_custom_call", output_to_operand_aliasing={{0}: (6, {}), {1}: (7, {}), {2}: (8, {})} | custom-call | flops 402653184 | bytes 1 | tf_op jit(solution)/shard_map/pallas_call | solution.py:148
  33.2 2.7 %collective-permute-start.13 = (bf16[128,768]{1,0:T(8,128)(2,1)S(1)}, bf16[128,768]{1,0:T(8,128)(2,1)S(1)}, u32[]{:S(2)}, u32[]{:S(2)}) collective-permute-start(bf16[128,768]{1,0:T(8,128)(2,1)S(1)} %collective-permute-done.12.refs_1_), channel_id=1, source_target_pairs={{0,224},{1,225},{2,226},{3,227},{4,228},{5,229},{6,230},{7,231},{8... | collective-permute-start | bytes 589832 | tf_op jit(solution)/shard_map/ppermute | solution.py:33
  35.9 0.8 %shard_map.34 = (f32[1024,2048]{1,0:T(8,128)S(1)}, bf16[2048,768]{1,0:T(8,128)(2,1)S(1)}, f32[1,2048]{1,0:T(1,128)S(1)}) custom-call(bf16[128,768]{1,0:T(8,128)(2,1)S(1)} %collective-permute-done.10.refs_0_, bf16[128,768]{1,0:T(8,128)(2,1)S(1)} %collective-permute-done.11.refs_1_, ...), custom_call_target="tpu_custom_call", output_to_operand_aliasing={{0}: (6, {}), {1}: (7, {}), {2}: (8, {})} | custom-call | flops 402653184 | bytes 1 | tf_op jit(solution)/shard_map/pallas_call | solution.py:148
  36.7 0.8 %shard_map.35 = (f32[1024,2048]{1,0:T(8,128)S(1)}, bf16[2048,768]{1,0:T(8,128)(2,1)S(1)}, f32[1,2048]{1,0:T(1,128)S(1)}) custom-call(bf16[128,768]{1,0:T(8,128)(2,1)S(1)} %collective-permute-done.6.refs_0_, bf16[128,768]{1,0:T(8,128)(2,1)S(1)} %collective-permute-done.15.refs_1_, ...), custom_call_target="tpu_custom_call", output_to_operand_aliasing={{0}: (6, {}), {1}: (7, {}), {2}: (8, {})} | custom-call | flops 402653184 | bytes 1 | tf_op jit(solution)/shard_map/pallas_call | solution.py:148
  37.5 0.8 %shard_map.36 = (f32[1024,2048]{1,0:T(8,128)S(1)}, bf16[2048,768]{1,0:T(8,128)(2,1)S(1)}, f32[1,2048]{1,0:T(1,128)S(1)}) custom-call(bf16[128,768]{1,0:T(8,128)(2,1)S(1)} %collective-permute-done.14.refs_0_, bf16[128,768]{1,0:T(8,128)(2,1)S(1)} %collective-permute-done.12.refs_1_, ...), custom_call_target="tpu_custom_call", output_to_operand_aliasing={{0}: (6, {}), {1}: (7, {}), {2}: (8, {})} | custom-call | flops 402653184 | bytes 1 | tf_op jit(solution)/shard_map/pallas_call | solution.py:148
  38.3 2.4 %collective-permute-done.13.refs_1_ = bf16[128,768]{1,0:T(8,128)(2,1)S(1)} collective-permute-done((bf16[128,768]{1,0:T(8,128)(2,1)S(1)}, bf16[128,768]{1,0:T(8,128)(2,1)S(1)}, u32[]{:S(2)}, u32[]{:S(2)}) %collective-permute-start.13) | collective-permute-done | bytes 196640 | tf_op jit(solution)/shard_map/ppermute | solution.py:33
  40.7 0.8 %shard_map.37 = (f32[1024,2048]{1,0:T(8,128)S(1)}, bf16[2048,768]{1,0:T(8,128)(2,1)S(1)}, f32[1,2048]{1,0:T(1,128)S(1)}) custom-call(bf16[128,768]{1,0:T(8,128)(2,1)S(1)} %collective-permute-done.7.refs_0_, bf16[128,768]{1,0:T(8,128)(2,1)S(1)} %collective-permute-done.13.refs_1_, ...), custom_call_target="tpu_custom_call", output_to_operand_aliasing={{0}: (6, {}), {1}: (7, {}), {2}: (8, {})} | custom-call | flops 402653184 | bytes 1 | tf_op jit(solution)/shard_map/pallas_call | solution.py:148
  41.5 1.6 %collective-permute-start.16 = (f32[16,128]{1,0:T(8,128)S(1)}, f32[16,128]{1,0:T(8,128)S(1)}, u32[]{:S(2)}, u32[]{:S(2)}) collective-permute-start(f32[16,128]{1,0:T(8,128)S(1)} %shard_map.38), channel_id=1, source_target_pairs={{0,16},{1,17},{2,18},{3,19},{4,20},{5,21},{6,22},{7,23},{8,24},{9,... | collective-permute-start | bytes 24584 | tf_op jit(solution)/shard_map/ppermute | solution.py:33
  43.2 1.5 %collective-permute-start.17 = (f32[16,128]{1,0:T(8,128)S(1)}, f32[16,128]{1,0:T(8,128)S(1)}, u32[]{:S(2)}, u32[]{:S(2)}) collective-permute-start(f32[16,128]{1,0:T(8,128)S(1)} %shard_map.38), channel_id=1, source_target_pairs={{0,1},{1,16},{2,3},{3,18},{4,5},{5,20},{6,7},{7,22},{8,9},{9,24},{... | collective-permute-start | bytes 24584 | tf_op jit(solution)/shard_map/ppermute | solution.py:33
  44.7 1.1 %collective-permute-start.18 = (f32[16,128]{1,0:T(8,128)S(1)}, f32[16,128]{1,0:T(8,128)S(1)}, u32[]{:S(2)}, u32[]{:S(2)}) collective-permute-start(f32[16,128]{1,0:T(8,128)S(1)} %shard_map.38), channel_id=1, source_target_pairs={{0,17},{1,0},{2,19},{3,2},{4,21},{5,4},{6,23},{7,6},{8,25},{9,8},{... | collective-permute-start | bytes 24584 | tf_op jit(solution)/shard_map/ppermute | solution.py:33
  45.8 1.0 %collective-permute-done.17 = f32[16,128]{1,0:T(8,128)S(1)} collective-permute-done((f32[16,128]{1,0:T(8,128)S(1)}, f32[16,128]{1,0:T(8,128)S(1)}, u32[]{:S(2)}, u32[]{:S(2)}) %collective-permute-start.17) | collective-permute-done | bytes 8224 | tf_op jit(solution)/shard_map/ppermute | solution.py:33
  46.9 0.3 collective-permute-done.18
  47.3 18.9 %all_to_all.5.parts_ref = f32[32,16,128]{2,1,0:T(8,128)S(1)} all-to-all(f32[32,16,128]{2,1,0:T(8,128)S(1)} %broadcast_in_dim.2), channel_id=1, replica_groups={{0,2,4,6,32,34,36,38,64,66,68,70,96,98,100,102,128,130,132,134,160,162,..., dimensions={0} | all-to-all | bytes 524288 | tf_op jit(solution)/shard_map/all_to_all | solution.py:331
  66.2 1.3 %shard_map.39 = (f32[320,896]{1,0:T(8,128)S(1)}, f32[8,2048]{1,0:T(8,128)S(1)}) custom-call(f32[1024,2048]{1,0:T(8,128)S(1)} %get-tuple-element.81.logits_ref, bf16[2048,768]{1,0:T(8,128)(2,1)S(1)} %get-tuple-element.82.group_ref, f32[32,16,128]{2,1,0:T(8,128)S(1)} %all_to_all.5.parts_ref), custom_call_target="tpu_custom_call" | custom-call | flops 1 | bytes 1 | tf_op jit(solution)/shard_map/pallas_call | solution.py:230
  67.5 6.4 %collective-permute-start.19 = (f32[320,896]{1,0:T(8,128)S(1)}, f32[320,896]{1,0:T(8,128)S(1)}, u32[]{:S(2)}, u32[]{:S(2)}) collective-permute-start(f32[320,896]{1,0:T(8,128)S(1)} %get-tuple-element.86), channel_id=1, source_target_pairs={{0,8},{1,9},{2,10},{3,11},{4,12},{5,13},{6,14},{7,15},{8,0},{9,1},... | collective-permute-start | bytes 3440648 | tf_op jit(solution)/shard_map/ppermute | solution.py:33
  73.9 0.8 shard_map.40
  74.7 0.1 collective-permute-start.20
  74.8 2.0 %shard_map.41.own_ref = f32[512,896]{1,0:T(8,128)S(1)} custom-call(f32[1024,2048]{1,0:T(8,128)S(1)} %get-tuple-element.81.logits_ref, bf16[2048,768]{1,0:T(8,128)(2,1)S(1)} %get-tuple-element.82.group_ref, f32[8,2048]{1,0:T(8,128)S(1)} %get-tuple-element.85.norm_ref, bf16[512,768]{1,0:T(8,128)(2,1)S(1)} %get-tuple-element.49.refs_3_.cent_ref), custom_call_target="tpu_custom_call" | custom-call | flops 1 | bytes 1 | tf_op jit(solution)/shard_map/pallas_call | solution.py:230
  76.8 0.5 collective-permute-done.20.refs_1_
  77.3 1.2 %shard_map.42 = f32[512,768]{1,0:T(8,128)} custom-call(f32[512,896]{1,0:T(8,128)S(1)} %shard_map.41.own_ref, f32[320,896]{1,0:T(8,128)S(1)} %collective-permute-done.19.refs_0_, f32[192,896]{1,0:T(8,128)S(1)} %collective-permute-done.20.refs_1_), custom_call_target="tpu_custom_call" | custom-call | flops 1179648 | bytes 1572864 | tf_op jit(solution)/shard_map/pallas_call | solution.py:267
  (18 shorter events, 0.1 us)
Async XLA Ops:
  0.0 17.7 %collective-permute-start.5 = (bf16[512,768]{1,0:T(8,128)(2,1)}, bf16[512,768]{1,0:T(8,128)(2,1)S(1)}, u32[]{:S(2)}, u32[]{:S(2)}) collective-permute-start(bf16[512,768]{1,0:T(8,128)(2,1)} %cent_ref.1), channel_id=1, source_target_pairs={{0,8},{1,9},{2,10},{3,11},{4,12},{5,13},{6,14},{7,15},{8,0},{9,1},... | collective-permute-start | bytes 2359304 | tf_op jit(solution)/shard_map/ppermute | solution.py:33
  3.2 8.6 %collective-permute-start.4 = (bf16[128,768]{1,0:T(8,128)(2,1)}, bf16[128,768]{1,0:T(8,128)(2,1)S(1)}, u32[]{:S(2)}, u32[]{:S(2)}) collective-permute-start(bf16[128,768]{1,0:T(8,128)(2,1)} %point_ref.1), channel_id=1, source_target_pairs={{0,17},{1,16},{2,19},{3,18},{4,21},{5,20},{6,23},{7,22},{8,25},{9,... | collective-permute-start | bytes 589832 | tf_op jit(solution)/shard_map/ppermute | solution.py:33
  4.0 11.1 %collective-permute-start = (bf16[128,768]{1,0:T(8,128)(2,1)}, bf16[128,768]{1,0:T(8,128)(2,1)S(1)}, u32[]{:S(2)}, u32[]{:S(2)}) collective-permute-start(bf16[128,768]{1,0:T(8,128)(2,1)} %point_ref.1), channel_id=1, source_target_pairs={{0,32},{1,33},{2,34},{3,35},{4,36},{5,37},{6,38},{7,39},{8,40},{9,... | collective-permute-start | bytes 589832 | tf_op jit(solution)/shard_map/ppermute | solution.py:33
  5.6 9.4 %collective-permute-start.1 = (bf16[128,768]{1,0:T(8,128)(2,1)}, bf16[128,768]{1,0:T(8,128)(2,1)S(1)}, u32[]{:S(2)}, u32[]{:S(2)}) collective-permute-start(bf16[128,768]{1,0:T(8,128)(2,1)} %point_ref.1), channel_id=1, source_target_pairs={{0,224},{1,225},{2,226},{3,227},{4,228},{5,229},{6,230},{7,231},{8... | collective-permute-start | bytes 589832 | tf_op jit(solution)/shard_map/ppermute | solution.py:33
  9.6 1.1 %copy-start = (bf16[512,768]{1,0:T(8,128)(2,1)S(1)}, bf16[512,768]{1,0:T(8,128)(2,1)}, u32[]{:S(2)}) copy-start(bf16[512,768]{1,0:T(8,128)(2,1)} %cent_ref.1) | copy-start | bytes 2359300
  10.7 0.9 %copy-start.1 = (bf16[128,768]{1,0:T(8,128)(2,1)S(1)}, bf16[128,768]{1,0:T(8,128)(2,1)}, u32[]{:S(2)}) copy-start(bf16[128,768]{1,0:T(8,128)(2,1)} %point_ref.1) | copy-start | bytes 589828
  11.9 7.7 %collective-permute-start.8 = (bf16[128,768]{1,0:T(8,128)(2,1)S(1)}, bf16[128,768]{1,0:T(8,128)(2,1)S(1)}, u32[]{:S(2)}, u32[]{:S(2)}) collective-permute-start(bf16[128,768]{1,0:T(8,128)(2,1)S(1)} %collective-permute-done.4.refs_1_), channel_id=1, source_target_pairs={{0,32},{1,33},{2,34},{3,35},{4,36},{5,37},{6,38},{7,39},{8,40},{9,... | collective-permute-start | bytes 589832 | tf_op jit(solution)/shard_map/ppermute | solution.py:33
  12.0 7.6 %collective-permute-start.9 = (bf16[128,768]{1,0:T(8,128)(2,1)S(1)}, bf16[128,768]{1,0:T(8,128)(2,1)S(1)}, u32[]{:S(2)}, u32[]{:S(2)}) collective-permute-start(bf16[128,768]{1,0:T(8,128)(2,1)S(1)} %collective-permute-done.4.refs_1_), channel_id=1, source_target_pairs={{0,224},{1,225},{2,226},{3,227},{4,228},{5,229},{6,230},{7,231},{8... | collective-permute-start | bytes 589832 | tf_op jit(solution)/shard_map/ppermute | solution.py:33
  15.0 8.7 %collective-permute-start.2 = (bf16[128,768]{1,0:T(8,128)(2,1)S(1)}, bf16[128,768]{1,0:T(8,128)(2,1)S(1)}, u32[]{:S(2)}, u32[]{:S(2)}) collective-permute-start(bf16[128,768]{1,0:T(8,128)(2,1)S(1)} %collective-permute-done.refs_0_), channel_id=1, source_target_pairs={{0,32},{1,33},{2,34},{3,35},{4,36},{5,37},{6,38},{7,39},{8,40},{9,... | collective-permute-start | bytes 589832 | tf_op jit(solution)/shard_map/ppermute | solution.py:33
  15.1 8.7 %collective-permute-start.3 = (bf16[128,768]{1,0:T(8,128)(2,1)S(1)}, bf16[128,768]{1,0:T(8,128)(2,1)S(1)}, u32[]{:S(2)}, u32[]{:S(2)}) collective-permute-start(bf16[128,768]{1,0:T(8,128)(2,1)S(1)} %collective-permute-done.1.refs_1_), channel_id=1, source_target_pairs={{0,224},{1,225},{2,226},{3,227},{4,228},{5,229},{6,230},{7,231},{8... | collective-permute-start | bytes 589832 | tf_op jit(solution)/shard_map/ppermute | solution.py:33
  19.5 7.8 %collective-permute-start.10 = (bf16[128,768]{1,0:T(8,128)(2,1)S(1)}, bf16[128,768]{1,0:T(8,128)(2,1)S(1)}, u32[]{:S(2)}, u32[]{:S(2)}) collective-permute-start(bf16[128,768]{1,0:T(8,128)(2,1)S(1)} %collective-permute-done.8.refs_0_), channel_id=1, source_target_pairs={{0,32},{1,33},{2,34},{3,35},{4,36},{5,37},{6,38},{7,39},{8,40},{9,... | collective-permute-start | bytes 589832 | tf_op jit(solution)/shard_map/ppermute | solution.py:33
  19.5 7.8 %collective-permute-start.11 = (bf16[128,768]{1,0:T(8,128)(2,1)S(1)}, bf16[128,768]{1,0:T(8,128)(2,1)S(1)}, u32[]{:S(2)}, u32[]{:S(2)}) collective-permute-start(bf16[128,768]{1,0:T(8,128)(2,1)S(1)} %collective-permute-done.9.refs_1_), channel_id=1, source_target_pairs={{0,224},{1,225},{2,226},{3,227},{4,228},{5,229},{6,230},{7,231},{8... | collective-permute-start | bytes 589832 | tf_op jit(solution)/shard_map/ppermute | solution.py:33
  23.8 7.8 %collective-permute-start.6 = (bf16[128,768]{1,0:T(8,128)(2,1)S(1)}, bf16[128,768]{1,0:T(8,128)(2,1)S(1)}, u32[]{:S(2)}, u32[]{:S(2)}) collective-permute-start(bf16[128,768]{1,0:T(8,128)(2,1)S(1)} %collective-permute-done.2.refs_0_), channel_id=1, source_target_pairs={{0,32},{1,33},{2,34},{3,35},{4,36},{5,37},{6,38},{7,39},{8,40},{9,... | collective-permute-start | bytes 589832 | tf_op jit(solution)/shard_map/ppermute | solution.py:33
  27.3 5.9 %collective-permute-start.12 = (bf16[128,768]{1,0:T(8,128)(2,1)S(1)}, bf16[128,768]{1,0:T(8,128)(2,1)S(1)}, u32[]{:S(2)}, u32[]{:S(2)}) collective-permute-start(bf16[128,768]{1,0:T(8,128)(2,1)S(1)} %collective-permute-done.11.refs_1_), channel_id=1, source_target_pairs={{0,224},{1,225},{2,226},{3,227},{4,228},{5,229},{6,230},{7,231},{8... | collective-permute-start | bytes 589832 | tf_op jit(solution)/shard_map/ppermute | solution.py:33
  29.7 7.0 %collective-permute-start.15 = (bf16[128,768]{1,0:T(8,128)(2,1)S(1)}, bf16[128,768]{1,0:T(8,128)(2,1)S(1)}, u32[]{:S(2)}, u32[]{:S(2)}) collective-permute-start(bf16[128,768]{1,0:T(8,128)(2,1)S(1)} %collective-permute-done.3.refs_1_), channel_id=1, source_target_pairs={{0,224},{1,225},{2,226},{3,227},{4,228},{5,229},{6,230},{7,231},{8... | collective-permute-start | bytes 589832 | tf_op jit(solution)/shard_map/ppermute | solution.py:33
  29.7 7.8 %collective-permute-start.14 = (bf16[128,768]{1,0:T(8,128)(2,1)S(1)}, bf16[128,768]{1,0:T(8,128)(2,1)S(1)}, u32[]{:S(2)}, u32[]{:S(2)}) collective-permute-start(bf16[128,768]{1,0:T(8,128)(2,1)S(1)} %collective-permute-done.10.refs_0_), channel_id=1, source_target_pairs={{0,32},{1,33},{2,34},{3,35},{4,36},{5,37},{6,38},{7,39},{8,40},{9,... | collective-permute-start | bytes 589832 | tf_op jit(solution)/shard_map/ppermute | solution.py:33
  31.5 6.8 %collective-permute-start.7 = (bf16[128,768]{1,0:T(8,128)(2,1)S(1)}, bf16[128,768]{1,0:T(8,128)(2,1)S(1)}, u32[]{:S(2)}, u32[]{:S(2)}) collective-permute-start(bf16[128,768]{1,0:T(8,128)(2,1)S(1)} %collective-permute-done.6.refs_0_), channel_id=1, source_target_pairs={{0,32},{1,33},{2,34},{3,35},{4,36},{5,37},{6,38},{7,39},{8,40},{9,... | collective-permute-start | bytes 589832 | tf_op jit(solution)/shard_map/ppermute | solution.py:33
  33.2 7.5 %collective-permute-start.13 = (bf16[128,768]{1,0:T(8,128)(2,1)S(1)}, bf16[128,768]{1,0:T(8,128)(2,1)S(1)}, u32[]{:S(2)}, u32[]{:S(2)}) collective-permute-start(bf16[128,768]{1,0:T(8,128)(2,1)S(1)} %collective-permute-done.12.refs_1_), channel_id=1, source_target_pairs={{0,224},{1,225},{2,226},{3,227},{4,228},{5,229},{6,230},{7,231},{8... | collective-permute-start | bytes 589832 | tf_op jit(solution)/shard_map/ppermute | solution.py:33
  41.5 4.3 %collective-permute-start.16 = (f32[16,128]{1,0:T(8,128)S(1)}, f32[16,128]{1,0:T(8,128)S(1)}, u32[]{:S(2)}, u32[]{:S(2)}) collective-permute-start(f32[16,128]{1,0:T(8,128)S(1)} %shard_map.38), channel_id=1, source_target_pairs={{0,16},{1,17},{2,18},{3,19},{4,20},{5,21},{6,22},{7,23},{8,24},{9,... | collective-permute-start | bytes 24584 | tf_op jit(solution)/shard_map/ppermute | solution.py:33
  43.2 3.7 %collective-permute-start.17 = (f32[16,128]{1,0:T(8,128)S(1)}, f32[16,128]{1,0:T(8,128)S(1)}, u32[]{:S(2)}, u32[]{:S(2)}) collective-permute-start(f32[16,128]{1,0:T(8,128)S(1)} %shard_map.38), channel_id=1, source_target_pairs={{0,1},{1,16},{2,3},{3,18},{4,5},{5,20},{6,7},{7,22},{8,9},{9,24},{... | collective-permute-start | bytes 24584 | tf_op jit(solution)/shard_map/ppermute | solution.py:33
  44.7 2.5 %collective-permute-start.18 = (f32[16,128]{1,0:T(8,128)S(1)}, f32[16,128]{1,0:T(8,128)S(1)}, u32[]{:S(2)}, u32[]{:S(2)}) collective-permute-start(f32[16,128]{1,0:T(8,128)S(1)} %shard_map.38), channel_id=1, source_target_pairs={{0,17},{1,0},{2,19},{3,2},{4,21},{5,4},{6,23},{7,6},{8,25},{9,8},{... | collective-permute-start | bytes 24584 | tf_op jit(solution)/shard_map/ppermute | solution.py:33
  67.5 9.8 %collective-permute-start.19 = (f32[320,896]{1,0:T(8,128)S(1)}, f32[320,896]{1,0:T(8,128)S(1)}, u32[]{:S(2)}, u32[]{:S(2)}) collective-permute-start(f32[320,896]{1,0:T(8,128)S(1)} %get-tuple-element.86), channel_id=1, source_target_pairs={{0,8},{1,9},{2,10},{3,11},{4,12},{5,13},{6,14},{7,15},{8,0},{9,1},... | collective-permute-start | bytes 3440648 | tf_op jit(solution)/shard_map/ppermute | solution.py:33
  74.7 2.6 %collective-permute-start.20 = (f32[192,896]{1,0:T(8,128)S(1)}, f32[192,896]{1,0:T(8,128)S(1)}, u32[]{:S(2)}, u32[]{:S(2)}) collective-permute-start(f32[192,896]{1,0:T(8,128)S(1)} %shard_map.40), channel_id=1, source_target_pairs={{0,8},{1,9},{2,10},{3,11},{4,12},{5,13},{6,14},{7,15},{8,0},{9,1},... | collective-permute-start | bytes 2064392 | tf_op jit(solution)/shard_map/ppermute | solution.py:33

commit v7 on v6

--- a/solution.py
+++ b/solution.py
@@ -193,23 +193,26 @@
 def add_up(logits_ref, start, group_ref, norm_ref, cent_ref, out_ref):
     rows, width = out_ref.shape[0], group_ref.shape[1]
     points = group_ref.shape[0]
-    total, mass = None, None
-    deep = 512
-    for at in range(0, points, deep):
-        columns = pl.ds(at, deep)
-        logits = logits_ref[pl.ds(start, rows), columns]
-        resp = jnp.exp2(logits - norm_ref[:1, columns]).astype(jnp.bfloat16)
-        part = jnp.dot(resp, group_ref[columns, :], preferred_element_type=jnp.float32)
-        wide = resp.astype(jnp.float32)
-        weight = sum(wide[:, k : k + LANES] for k in range(0, deep, LANES))
-        total = part if total is None else total + part
-        mass = weight if mass is None else mass + weight
-    mass = jnp.sum(mass, axis=1, keepdims=True)
-    if cent_ref is not None:
-        total = total + PRIOR * cent_ref[...].astype(jnp.float32)
-        mass = mass + PRIOR
-    out_ref[:, pl.ds(0, width)] = total
-    out_ref[:, pl.ds(width, LANES)] = jnp.broadcast_to(mass, (rows, LANES))
+    some = TILE if rows % TILE == 0 else rows
+    deep = points if rows % TILE == 0 else 512
+    for first in range(0, rows, some):
+        within = pl.ds(first, some)
+        total, mass = None, None
+        for at in range(0, points, deep):
+            columns = pl.ds(at, deep)
+            logits = logits_ref[pl.ds(start + first, some), columns]
+            resp = jnp.exp2(logits - norm_ref[:1, columns]).astype(jnp.bfloat16)
+            part = jnp.dot(resp, group_ref[columns, :], preferred_element_type=jnp.float32)
+            wide = resp.astype(jnp.float32)
+            weight = sum(wide[:, k : k + LANES] for k in range(0, deep, LANES))
+            total = part if total is None else total + part
+            mass = weight if mass is None else mass + weight
+        mass = jnp.sum(mass, axis=1, keepdims=True)
+        if cent_ref is not None:
+            total = total + PRIOR * cent_ref[within, :].astype(jnp.float32)
+            mass = mass + PRIOR
+        out_ref[within, pl.ds(0, width)] = total
+        out_ref[within, pl.ds(width, LANES)] = jnp.broadcast_to(mass, (some, LANES))
 
 
 def first_sums_kernel(order, start, logits_ref, group_ref, parts_ref, out_ref, norm_ref, rows_ref):

time: 78.8 us -> 78.8 us (level)
  no operation moved by 1% of the time
where the time goes in v7:
time: 78.8 us; the launch traced here: 78.6 us
  starting transfers between devices  35.5 us (45%)
  blocking collectives  18.9 us (24%)
  Pallas kernels  12.2 us (15%)
  waiting for transfers between devices  9.8 us (12%)
  local copies, waits for them, and re-layouts  2.08 us (3%)
    ppermute x21, starting transfers between devices, send(): return lax.ppermute(block, AXES, route)  35.5 us
    all_to_all x1, blocking collectives, shards(): lax.all_to_all(everywhere, AXES, 0, 0, axis_index_groups=groups_by(lambda...  18.9 us
    ppermute x21, waiting for transfers between devices, send(): return lax.ppermute(block, AXES, route)  9.8 us
    pallas_call x8, Pallas kernels, logits_of(): pl.pallas_call(functools.partial(logits_kernel, len(blocks), first, len(b...  6.45 us
    pallas_call x3, Pallas kernels, sums_call(): pl.pallas_call(kernel, in_specs=[IN_VMEM] * len(operands), out_specs=(IN_...  4 us
    unnamed x4, local copies, waits for them, and re-layouts  2.06 us
  transfers between devices with their start and end apart: 21, of which 8 were waited for; matrix products, arithmetic and copies ran while one was open for 0% of the time, Pallas kernels for 11%

profile of v7, /device:TPU:1, one launch (start us, length us, event | category | flops | bytes accessed | tf_op | source)
XLA Modules:
  0.0 78.6 jit_solution(4146162419758020022)
XLA Ops:
  0.0 3.2 %collective-permute-start.5 = (bf16[512,768]{1,0:T(8,128)(2,1)}, bf16[512,768]{1,0:T(8,128)(2,1)S(1)}, u32[]{:S(2)}, u32[]{:S(2)}) collective-permute-start(bf16[512,768]{1,0:T(8,128)(2,1)} %cent_ref.1), channel_id=1, source_target_pairs={{0,8},{1,9},{2,10},{3,11},{4,12},{5,13},{6,14},{7,15},{8,0},{9,1},... | collective-permute-start | bytes 2359304 | tf_op jit(solution)/shard_map/ppermute | solution.py:33
  3.2 0.7 collective-permute-start.4
  4.0 1.6 %collective-permute-start = (bf16[128,768]{1,0:T(8,128)(2,1)}, bf16[128,768]{1,0:T(8,128)(2,1)S(1)}, u32[]{:S(2)}, u32[]{:S(2)}) collective-permute-start(bf16[128,768]{1,0:T(8,128)(2,1)} %point_ref.1), channel_id=1, source_target_pairs={{0,32},{1,33},{2,34},{3,35},{4,36},{5,37},{6,38},{7,39},{8,40},{9,... | collective-permute-start | bytes 589832 | tf_op jit(solution)/shard_map/ppermute | solution.py:33
  5.6 3.9 %collective-permute-start.1 = (bf16[128,768]{1,0:T(8,128)(2,1)}, bf16[128,768]{1,0:T(8,128)(2,1)S(1)}, u32[]{:S(2)}, u32[]{:S(2)}) collective-permute-start(bf16[128,768]{1,0:T(8,128)(2,1)} %point_ref.1), channel_id=1, source_target_pairs={{0,224},{1,225},{2,226},{3,227},{4,228},{5,229},{6,230},{7,231},{8... | collective-permute-start | bytes 589832 | tf_op jit(solution)/shard_map/ppermute | solution.py:33
  9.6 1.1 %copy-done = bf16[512,768]{1,0:T(8,128)(2,1)S(1)} copy-done((bf16[512,768]{1,0:T(8,128)(2,1)S(1)}, bf16[512,768]{1,0:T(8,128)(2,1)}, u32[]{:S(2)}) %copy-start) | copy-done | bytes 786456
  10.7 0.9 %copy-done.1 = bf16[128,768]{1,0:T(8,128)(2,1)S(1)} copy-done((bf16[128,768]{1,0:T(8,128)(2,1)S(1)}, bf16[128,768]{1,0:T(8,128)(2,1)}, u32[]{:S(2)}) %copy-start.1) | copy-done | bytes 196632
  11.6 0.2 shard_map.28
  11.9 0.1 collective-permute-start.8
  12.0 3.1 %collective-permute-start.9 = (bf16[128,768]{1,0:T(8,128)(2,1)S(1)}, bf16[128,768]{1,0:T(8,128)(2,1)S(1)}, u32[]{:S(2)}, u32[]{:S(2)}) collective-permute-start(bf16[128,768]{1,0:T(8,128)(2,1)S(1)} %collective-permute-done.4.refs_1_), channel_id=1, source_target_pairs={{0,224},{1,225},{2,226},{3,227},{4,228},{5,229},{6,230},{7,231},{8... | collective-permute-start | bytes 589832 | tf_op jit(solution)/shard_map/ppermute | solution.py:33
  15.0 0.0 collective-permute-done.refs_0_
  15.1 2.7 %collective-permute-start.3 = (bf16[128,768]{1,0:T(8,128)(2,1)S(1)}, bf16[128,768]{1,0:T(8,128)(2,1)S(1)}, u32[]{:S(2)}, u32[]{:S(2)}) collective-permute-start(bf16[128,768]{1,0:T(8,128)(2,1)S(1)} %collective-permute-done.1.refs_1_), channel_id=1, source_target_pairs={{0,224},{1,225},{2,226},{3,227},{4,228},{5,229},{6,230},{7,231},{8... | collective-permute-start | bytes 589832 | tf_op jit(solution)/shard_map/ppermute | solution.py:33
  17.7 0.0 collective-permute-done.5.cent_ref.refs_2_
  17.7 0.2 shard_map.29.refs_4_
  18.0 0.8 %shard_map.30 = (f32[1024,2048]{1,0:T(8,128)S(1)}, bf16[2048,768]{1,0:T(8,128)(2,1)S(1)}, f32[1,2048]{1,0:T(1,128)S(1)}) custom-call(bf16[128,768]{1,0:T(8,128)(2,1)S(1)} %get-tuple-element.48.refs_0_, bf16[128,768]{1,0:T(8,128)(2,1)S(1)} %collective-permute-done.4.refs_1_, bf16[512,768]{1,0:T(8,128)(2,1)S(1)} %collective-permute-done.5.cent_ref.refs_2_, ...), custom_call_target="tpu_custom_call" | custom-call | flops 402653184 | bytes 1 | tf_op jit(solution)/shard_map/pallas_call | solution.py:148
  18.8 0.8 collective-permute-done.8.refs_0_
  19.5 0.0 collective-permute-done.9.refs_1_
  19.5 0.0 collective-permute-start.10
  19.5 2.7 %collective-permute-start.11 = (bf16[128,768]{1,0:T(8,128)(2,1)S(1)}, bf16[128,768]{1,0:T(8,128)(2,1)S(1)}, u32[]{:S(2)}, u32[]{:S(2)}) collective-permute-start(bf16[128,768]{1,0:T(8,128)(2,1)S(1)} %collective-permute-done.9.refs_1_), channel_id=1, source_target_pairs={{0,224},{1,225},{2,226},{3,227},{4,228},{5,229},{6,230},{7,231},{8... | collective-permute-start | bytes 589832 | tf_op jit(solution)/shard_map/ppermute | solution.py:33
  22.2 1.5 %collective-permute-done.2.refs_0_ = bf16[128,768]{1,0:T(8,128)(2,1)S(1)} collective-permute-done((bf16[128,768]{1,0:T(8,128)(2,1)S(1)}, bf16[128,768]{1,0:T(8,128)(2,1)S(1)}, u32[]{:S(2)}, u32[]{:S(2)}) %collective-permute-start.2) | collective-permute-done | bytes 196640 | tf_op jit(solution)/shard_map/ppermute | solution.py:33
  23.7 0.0 collective-permute-done.3.refs_1_
  23.8 0.8 %shard_map.31 = (f32[1024,2048]{1,0:T(8,128)S(1)}, bf16[2048,768]{1,0:T(8,128)(2,1)S(1)}, f32[1,2048]{1,0:T(1,128)S(1)}) custom-call(bf16[128,768]{1,0:T(8,128)(2,1)S(1)} %collective-permute-done.refs_0_, bf16[128,768]{1,0:T(8,128)(2,1)S(1)} %collective-permute-done.1.refs_1_, ...), custom_call_target="tpu_custom_call", output_to_operand_aliasing={{0}: (6, {}), {1}: (7, {}), {2}: (8, {})} | custom-call | flops 402653184 | bytes 1 | tf_op jit(solution)/shard_map/pallas_call | solution.py:148
  24.6 2.7 %collective-permute-done.10.refs_0_ = bf16[128,768]{1,0:T(8,128)(2,1)S(1)} collective-permute-done((bf16[128,768]{1,0:T(8,128)(2,1)S(1)}, bf16[128,768]{1,0:T(8,128)(2,1)S(1)}, u32[]{:S(2)}, u32[]{:S(2)}) %collective-permute-start.10) | collective-permute-done | bytes 196640 | tf_op jit(solution)/shard_map/ppermute | solution.py:33
  27.3 2.4 %collective-permute-start.12 = (bf16[128,768]{1,0:T(8,128)(2,1)S(1)}, bf16[128,768]{1,0:T(8,128)(2,1)S(1)}, u32[]{:S(2)}, u32[]{:S(2)}) collective-permute-start(bf16[128,768]{1,0:T(8,128)(2,1)S(1)} %collective-permute-done.11.refs_1_), channel_id=1, source_target_pairs={{0,224},{1,225},{2,226},{3,227},{4,228},{5,229},{6,230},{7,231},{8... | collective-permute-start | bytes 589832 | tf_op jit(solution)/shard_map/ppermute | solution.py:33
  29.7 0.0 collective-permute-start.15
  29.7 1.4 %collective-permute-start.14 = (bf16[128,768]{1,0:T(8,128)(2,1)S(1)}, bf16[128,768]{1,0:T(8,128)(2,1)S(1)}, u32[]{:S(2)}, u32[]{:S(2)}) collective-permute-start(bf16[128,768]{1,0:T(8,128)(2,1)S(1)} %collective-permute-done.10.refs_0_), channel_id=1, source_target_pairs={{0,32},{1,33},{2,34},{3,35},{4,36},{5,37},{6,38},{7,39},{8,40},{9,... | collective-permute-start | bytes 589832 | tf_op jit(solution)/shard_map/ppermute | solution.py:33
  31.2 0.4 collective-permute-done.6.refs_0_
  31.5 0.0 collective-permute-start.7
  31.5 0.8 %shard_map.32 = (f32[1024,2048]{1,0:T(8,128)S(1)}, bf16[2048,768]{1,0:T(8,128)(2,1)S(1)}, f32[1,2048]{1,0:T(1,128)S(1)}) custom-call(bf16[128,768]{1,0:T(8,128)(2,1)S(1)} %collective-permute-done.8.refs_0_, bf16[128,768]{1,0:T(8,128)(2,1)S(1)} %collective-permute-done.9.refs_1_, ...), custom_call_target="tpu_custom_call", output_to_operand_aliasing={{0}: (6, {}), {1}: (7, {}), {2}: (8, {})} | custom-call | flops 402653184 | bytes 1 | tf_op jit(solution)/shard_map/pallas_call | solution.py:148
  32.4 0.8 %shard_map.33 = (f32[1024,2048]{1,0:T(8,128)S(1)}, bf16[2048,768]{1,0:T(8,128)(2,1)S(1)}, f32[1,2048]{1,0:T(1,128)S(1)}) custom-call(bf16[128,768]{1,0:T(8,128)(2,1)S(1)} %collective-permute-done.2.refs_0_, bf16[128,768]{1,0:T(8,128)(2,1)S(1)} %collective-permute-done.3.refs_1_, ...), custom_call_target="tpu_custom_call", output_to_operand_aliasing={{0}: (6, {}), {1}: (7, {}), {2}: (8, {})} | custom-call | flops 402653184 | bytes 1 | tf_op jit(solution)/shard_map/pallas_call | solution.py:148
  33.2 2.7 %collective-permute-start.13 = (bf16[128,768]{1,0:T(8,128)(2,1)S(1)}, bf16[128,768]{1,0:T(8,128)(2,1)S(1)}, u32[]{:S(2)}, u32[]{:S(2)}) collective-permute-start(bf16[128,768]{1,0:T(8,128)(2,1)S(1)} %collective-permute-done.12.refs_1_), channel_id=1, source_target_pairs={{0,224},{1,225},{2,226},{3,227},{4,228},{5,229},{6,230},{7,231},{8... | collective-permute-start | bytes 589832 | tf_op jit(solution)/shard_map/ppermute | solution.py:33
  35.9 0.8 %shard_map.34 = (f32[1024,2048]{1,0:T(8,128)S(1)}, bf16[2048,768]{1,0:T(8,128)(2,1)S(1)}, f32[1,2048]{1,0:T(1,128)S(1)}) custom-call(bf16[128,768]{1,0:T(8,128)(2,1)S(1)} %collective-permute-done.10.refs_0_, bf16[128,768]{1,0:T(8,128)(2,1)S(1)} %collective-permute-done.11.refs_1_, ...), custom_call_target="tpu_custom_call", output_to_operand_aliasing={{0}: (6, {}), {1}: (7, {}), {2}: (8, {})} | custom-call | flops 402653184 | bytes 1 | tf_op jit(solution)/shard_map/pallas_call | solution.py:148
  36.7 0.8 %shard_map.35 = (f32[1024,2048]{1,0:T(8,128)S(1)}, bf16[2048,768]{1,0:T(8,128)(2,1)S(1)}, f32[1,2048]{1,0:T(1,128)S(1)}) custom-call(bf16[128,768]{1,0:T(8,128)(2,1)S(1)} %collective-permute-done.6.refs_0_, bf16[128,768]{1,0:T(8,128)(2,1)S(1)} %collective-permute-done.15.refs_1_, ...), custom_call_target="tpu_custom_call", output_to_operand_aliasing={{0}: (6, {}), {1}: (7, {}), {2}: (8, {})} | custom-call | flops 402653184 | bytes 1 | tf_op jit(solution)/shard_map/pallas_call | solution.py:148
  37.5 0.8 %shard_map.36 = (f32[1024,2048]{1,0:T(8,128)S(1)}, bf16[2048,768]{1,0:T(8,128)(2,1)S(1)}, f32[1,2048]{1,0:T(1,128)S(1)}) custom-call(bf16[128,768]{1,0:T(8,128)(2,1)S(1)} %collective-permute-done.14.refs_0_, bf16[128,768]{1,0:T(8,128)(2,1)S(1)} %collective-permute-done.12.refs_1_, ...), custom_call_target="tpu_custom_call", output_to_operand_aliasing={{0}: (6, {}), {1}: (7, {}), {2}: (8, {})} | custom-call | flops 402653184 | bytes 1 | tf_op jit(solution)/shard_map/pallas_call | solution.py:148
  38.3 2.4 %collective-permute-done.13.refs_1_ = bf16[128,768]{1,0:T(8,128)(2,1)S(1)} collective-permute-done((bf16[128,768]{1,0:T(8,128)(2,1)S(1)}, bf16[128,768]{1,0:T(8,128)(2,1)S(1)}, u32[]{:S(2)}, u32[]{:S(2)}) %collective-permute-start.13) | collective-permute-done | bytes 196640 | tf_op jit(solution)/shard_map/ppermute | solution.py:33
  40.7 0.8 %shard_map.37 = (f32[1024,2048]{1,0:T(8,128)S(1)}, bf16[2048,768]{1,0:T(8,128)(2,1)S(1)}, f32[1,2048]{1,0:T(1,128)S(1)}) custom-call(bf16[128,768]{1,0:T(8,128)(2,1)S(1)} %collective-permute-done.7.refs_0_, bf16[128,768]{1,0:T(8,128)(2,1)S(1)} %collective-permute-done.13.refs_1_, ...), custom_call_target="tpu_custom_call", output_to_operand_aliasing={{0}: (6, {}), {1}: (7, {}), {2}: (8, {})} | custom-call | flops 402653184 | bytes 1 | tf_op jit(solution)/shard_map/pallas_call | solution.py:148
  41.5 1.6 %collective-permute-start.16 = (f32[16,128]{1,0:T(8,128)S(1)}, f32[16,128]{1,0:T(8,128)S(1)}, u32[]{:S(2)}, u32[]{:S(2)}) collective-permute-start(f32[16,128]{1,0:T(8,128)S(1)} %shard_map.38), channel_id=1, source_target_pairs={{0,16},{1,17},{2,18},{3,19},{4,20},{5,21},{6,22},{7,23},{8,24},{9,... | collective-permute-start | bytes 24584 | tf_op jit(solution)/shard_map/ppermute | solution.py:33
  43.2 1.5 %collective-permute-start.17 = (f32[16,128]{1,0:T(8,128)S(1)}, f32[16,128]{1,0:T(8,128)S(1)}, u32[]{:S(2)}, u32[]{:S(2)}) collective-permute-start(f32[16,128]{1,0:T(8,128)S(1)} %shard_map.38), channel_id=1, source_target_pairs={{0,1},{1,16},{2,3},{3,18},{4,5},{5,20},{6,7},{7,22},{8,9},{9,24},{... | collective-permute-start | bytes 24584 | tf_op jit(solution)/shard_map/ppermute | solution.py:33
  44.7 1.1 %collective-permute-start.18 = (f32[16,128]{1,0:T(8,128)S(1)}, f32[16,128]{1,0:T(8,128)S(1)}, u32[]{:S(2)}, u32[]{:S(2)}) collective-permute-start(f32[16,128]{1,0:T(8,128)S(1)} %shard_map.38), channel_id=1, source_target_pairs={{0,17},{1,0},{2,19},{3,2},{4,21},{5,4},{6,23},{7,6},{8,25},{9,8},{... | collective-permute-start | bytes 24584 | tf_op jit(solution)/shard_map/ppermute | solution.py:33
  45.8 1.0 %collective-permute-done.17 = f32[16,128]{1,0:T(8,128)S(1)} collective-permute-done((f32[16,128]{1,0:T(8,128)S(1)}, f32[16,128]{1,0:T(8,128)S(1)}, u32[]{:S(2)}, u32[]{:S(2)}) %collective-permute-start.17) | collective-permute-done | bytes 8224 | tf_op jit(solution)/shard_map/ppermute | solution.py:33
  46.9 0.3 collective-permute-done.18
  47.3 18.9 %all_to_all.5.parts_ref = f32[32,16,128]{2,1,0:T(8,128)S(1)} all-to-all(f32[32,16,128]{2,1,0:T(8,128)S(1)} %broadcast_in_dim.2), channel_id=1, replica_groups={{0,2,4,6,32,34,36,38,64,66,68,70,96,98,100,102,128,130,132,134,160,162,..., dimensions={0} | all-to-all | bytes 524288 | tf_op jit(solution)/shard_map/all_to_all | solution.py:334
  66.2 1.3 %shard_map.39 = (f32[320,896]{1,0:T(8,128)S(1)}, f32[8,2048]{1,0:T(8,128)S(1)}) custom-call(f32[1024,2048]{1,0:T(8,128)S(1)} %get-tuple-element.81.logits_ref, bf16[2048,768]{1,0:T(8,128)(2,1)S(1)} %get-tuple-element.82.group_ref, f32[32,16,128]{2,1,0:T(8,128)S(1)} %all_to_all.5.parts_ref), custom_call_target="tpu_custom_call" | custom-call | flops 1 | bytes 1 | tf_op jit(solution)/shard_map/pallas_call | solution.py:233
  67.5 6.4 %collective-permute-start.19 = (f32[320,896]{1,0:T(8,128)S(1)}, f32[320,896]{1,0:T(8,128)S(1)}, u32[]{:S(2)}, u32[]{:S(2)}) collective-permute-start(f32[320,896]{1,0:T(8,128)S(1)} %get-tuple-element.86), channel_id=1, source_target_pairs={{0,8},{1,9},{2,10},{3,11},{4,12},{5,13},{6,14},{7,15},{8,0},{9,1},... | collective-permute-start | bytes 3440648 | tf_op jit(solution)/shard_map/ppermute | solution.py:33
  73.9 0.8 shard_map.40
  74.7 0.1 collective-permute-start.20
  74.8 1.9 %shard_map.41.own_ref = f32[512,896]{1,0:T(8,128)S(1)} custom-call(f32[1024,2048]{1,0:T(8,128)S(1)} %get-tuple-element.81.logits_ref, bf16[2048,768]{1,0:T(8,128)(2,1)S(1)} %get-tuple-element.82.group_ref, f32[8,2048]{1,0:T(8,128)S(1)} %get-tuple-element.85.norm_ref, bf16[512,768]{1,0:T(8,128)(2,1)S(1)} %get-tuple-element.49.refs_3_.cent_ref), custom_call_target="tpu_custom_call" | custom-call | flops 1 | bytes 1 | tf_op jit(solution)/shard_map/pallas_call | solution.py:233
  76.7 0.6 collective-permute-done.20.refs_1_
  77.3 1.2 %shard_map.42 = f32[512,768]{1,0:T(8,128)} custom-call(f32[512,896]{1,0:T(8,128)S(1)} %shard_map.41.own_ref, f32[320,896]{1,0:T(8,128)S(1)} %collective-permute-done.19.refs_0_, f32[192,896]{1,0:T(8,128)S(1)} %collective-permute-done.20.refs_1_), custom_call_target="tpu_custom_call" | custom-call | flops 1179648 | bytes 1572864 | tf_op jit(solution)/shard_map/pallas_call | solution.py:270
  (18 shorter events, 0.1 us)
Async XLA Ops:
  0.0 17.7 %collective-permute-start.5 = (bf16[512,768]{1,0:T(8,128)(2,1)}, bf16[512,768]{1,0:T(8,128)(2,1)S(1)}, u32[]{:S(2)}, u32[]{:S(2)}) collective-permute-start(bf16[512,768]{1,0:T(8,128)(2,1)} %cent_ref.1), channel_id=1, source_target_pairs={{0,8},{1,9},{2,10},{3,11},{4,12},{5,13},{6,14},{7,15},{8,0},{9,1},... | collective-permute-start | bytes 2359304 | tf_op jit(solution)/shard_map/ppermute | solution.py:33
  3.2 8.6 %collective-permute-start.4 = (bf16[128,768]{1,0:T(8,128)(2,1)}, bf16[128,768]{1,0:T(8,128)(2,1)S(1)}, u32[]{:S(2)}, u32[]{:S(2)}) collective-permute-start(bf16[128,768]{1,0:T(8,128)(2,1)} %point_ref.1), channel_id=1, source_target_pairs={{0,17},{1,16},{2,19},{3,18},{4,21},{5,20},{6,23},{7,22},{8,25},{9,... | collective-permute-start | bytes 589832 | tf_op jit(solution)/shard_map/ppermute | solution.py:33
  4.0 11.1 %collective-permute-start = (bf16[128,768]{1,0:T(8,128)(2,1)}, bf16[128,768]{1,0:T(8,128)(2,1)S(1)}, u32[]{:S(2)}, u32[]{:S(2)}) collective-permute-start(bf16[128,768]{1,0:T(8,128)(2,1)} %point_ref.1), channel_id=1, source_target_pairs={{0,32},{1,33},{2,34},{3,35},{4,36},{5,37},{6,38},{7,39},{8,40},{9,... | collective-permute-start | bytes 589832 | tf_op jit(solution)/shard_map/ppermute | solution.py:33
  5.6 9.4 %collective-permute-start.1 = (bf16[128,768]{1,0:T(8,128)(2,1)}, bf16[128,768]{1,0:T(8,128)(2,1)S(1)}, u32[]{:S(2)}, u32[]{:S(2)}) collective-permute-start(bf16[128,768]{1,0:T(8,128)(2,1)} %point_ref.1), channel_id=1, source_target_pairs={{0,224},{1,225},{2,226},{3,227},{4,228},{5,229},{6,230},{7,231},{8... | collective-permute-start | bytes 589832 | tf_op jit(solution)/shard_map/ppermute | solution.py:33
  9.6 1.1 %copy-start = (bf16[512,768]{1,0:T(8,128)(2,1)S(1)}, bf16[512,768]{1,0:T(8,128)(2,1)}, u32[]{:S(2)}) copy-start(bf16[512,768]{1,0:T(8,128)(2,1)} %cent_ref.1) | copy-start | bytes 2359300
  10.7 0.9 %copy-start.1 = (bf16[128,768]{1,0:T(8,128)(2,1)S(1)}, bf16[128,768]{1,0:T(8,128)(2,1)}, u32[]{:S(2)}) copy-start(bf16[128,768]{1,0:T(8,128)(2,1)} %point_ref.1) | copy-start | bytes 589828
  11.9 7.7 %collective-permute-start.8 = (bf16[128,768]{1,0:T(8,128)(2,1)S(1)}, bf16[128,768]{1,0:T(8,128)(2,1)S(1)}, u32[]{:S(2)}, u32[]{:S(2)}) collective-permute-start(bf16[128,768]{1,0:T(8,128)(2,1)S(1)} %collective-permute-done.4.refs_1_), channel_id=1, source_target_pairs={{0,32},{1,33},{2,34},{3,35},{4,36},{5,37},{6,38},{7,39},{8,40},{9,... | collective-permute-start | bytes 589832 | tf_op jit(solution)/shard_map/ppermute | solution.py:33
  12.0 7.6 %collective-permute-start.9 = (bf16[128,768]{1,0:T(8,128)(2,1)S(1)}, bf16[128,768]{1,0:T(8,128)(2,1)S(1)}, u32[]{:S(2)}, u32[]{:S(2)}) collective-permute-start(bf16[128,768]{1,0:T(8,128)(2,1)S(1)} %collective-permute-done.4.refs_1_), channel_id=1, source_target_pairs={{0,224},{1,225},{2,226},{3,227},{4,228},{5,229},{6,230},{7,231},{8... | collective-permute-start | bytes 589832 | tf_op jit(solution)/shard_map/ppermute | solution.py:33
  15.0 8.7 %collective-permute-start.2 = (bf16[128,768]{1,0:T(8,128)(2,1)S(1)}, bf16[128,768]{1,0:T(8,128)(2,1)S(1)}, u32[]{:S(2)}, u32[]{:S(2)}) collective-permute-start(bf16[128,768]{1,0:T(8,128)(2,1)S(1)} %collective-permute-done.refs_0_), channel_id=1, source_target_pairs={{0,32},{1,33},{2,34},{3,35},{4,36},{5,37},{6,38},{7,39},{8,40},{9,... | collective-permute-start | bytes 589832 | tf_op jit(solution)/shard_map/ppermute | solution.py:33
  15.1 8.7 %collective-permute-start.3 = (bf16[128,768]{1,0:T(8,128)(2,1)S(1)}, bf16[128,768]{1,0:T(8,128)(2,1)S(1)}, u32[]{:S(2)}, u32[]{:S(2)}) collective-permute-start(bf16[128,768]{1,0:T(8,128)(2,1)S(1)} %collective-permute-done.1.refs_1_), channel_id=1, source_target_pairs={{0,224},{1,225},{2,226},{3,227},{4,228},{5,229},{6,230},{7,231},{8... | collective-permute-start | bytes 589832 | tf_op jit(solution)/shard_map/ppermute | solution.py:33
  19.5 7.8 %collective-permute-start.10 = (bf16[128,768]{1,0:T(8,128)(2,1)S(1)}, bf16[128,768]{1,0:T(8,128)(2,1)S(1)}, u32[]{:S(2)}, u32[]{:S(2)}) collective-permute-start(bf16[128,768]{1,0:T(8,128)(2,1)S(1)} %collective-permute-done.8.refs_0_), channel_id=1, source_target_pairs={{0,32},{1,33},{2,34},{3,35},{4,36},{5,37},{6,38},{7,39},{8,40},{9,... | collective-permute-start | bytes 589832 | tf_op jit(solution)/shard_map/ppermute | solution.py:33
  19.5 7.8 %collective-permute-start.11 = (bf16[128,768]{1,0:T(8,128)(2,1)S(1)}, bf16[128,768]{1,0:T(8,128)(2,1)S(1)}, u32[]{:S(2)}, u32[]{:S(2)}) collective-permute-start(bf16[128,768]{1,0:T(8,128)(2,1)S(1)} %collective-permute-done.9.refs_1_), channel_id=1, source_target_pairs={{0,224},{1,225},{2,226},{3,227},{4,228},{5,229},{6,230},{7,231},{8... | collective-permute-start | bytes 589832 | tf_op jit(solution)/shard_map/ppermute | solution.py:33
  23.8 7.8 %collective-permute-start.6 = (bf16[128,768]{1,0:T(8,128)(2,1)S(1)}, bf16[128,768]{1,0:T(8,128)(2,1)S(1)}, u32[]{:S(2)}, u32[]{:S(2)}) collective-permute-start(bf16[128,768]{1,0:T(8,128)(2,1)S(1)} %collective-permute-done.2.refs_0_), channel_id=1, source_target_pairs={{0,32},{1,33},{2,34},{3,35},{4,36},{5,37},{6,38},{7,39},{8,40},{9,... | collective-permute-start | bytes 589832 | tf_op jit(solution)/shard_map/ppermute | solution.py:33
  27.3 5.9 %collective-permute-start.12 = (bf16[128,768]{1,0:T(8,128)(2,1)S(1)}, bf16[128,768]{1,0:T(8,128)(2,1)S(1)}, u32[]{:S(2)}, u32[]{:S(2)}) collective-permute-start(bf16[128,768]{1,0:T(8,128)(2,1)S(1)} %collective-permute-done.11.refs_1_), channel_id=1, source_target_pairs={{0,224},{1,225},{2,226},{3,227},{4,228},{5,229},{6,230},{7,231},{8... | collective-permute-start | bytes 589832 | tf_op jit(solution)/shard_map/ppermute | solution.py:33
  29.7 7.0 %collective-permute-start.15 = (bf16[128,768]{1,0:T(8,128)(2,1)S(1)}, bf16[128,768]{1,0:T(8,128)(2,1)S(1)}, u32[]{:S(2)}, u32[]{:S(2)}) collective-permute-start(bf16[128,768]{1,0:T(8,128)(2,1)S(1)} %collective-permute-done.3.refs_1_), channel_id=1, source_target_pairs={{0,224},{1,225},{2,226},{3,227},{4,228},{5,229},{6,230},{7,231},{8... | collective-permute-start | bytes 589832 | tf_op jit(solution)/shard_map/ppermute | solution.py:33
  29.7 7.8 %collective-permute-start.14 = (bf16[128,768]{1,0:T(8,128)(2,1)S(1)}, bf16[128,768]{1,0:T(8,128)(2,1)S(1)}, u32[]{:S(2)}, u32[]{:S(2)}) collective-permute-start(bf16[128,768]{1,0:T(8,128)(2,1)S(1)} %collective-permute-done.10.refs_0_), channel_id=1, source_target_pairs={{0,32},{1,33},{2,34},{3,35},{4,36},{5,37},{6,38},{7,39},{8,40},{9,... | collective-permute-start | bytes 589832 | tf_op jit(solution)/shard_map/ppermute | solution.py:33
  31.5 6.8 %collective-permute-start.7 = (bf16[128,768]{1,0:T(8,128)(2,1)S(1)}, bf16[128,768]{1,0:T(8,128)(2,1)S(1)}, u32[]{:S(2)}, u32[]{:S(2)}) collective-permute-start(bf16[128,768]{1,0:T(8,128)(2,1)S(1)} %collective-permute-done.6.refs_0_), channel_id=1, source_target_pairs={{0,32},{1,33},{2,34},{3,35},{4,36},{5,37},{6,38},{7,39},{8,40},{9,... | collective-permute-start | bytes 589832 | tf_op jit(solution)/shard_map/ppermute | solution.py:33
  33.2 7.5 %collective-permute-start.13 = (bf16[128,768]{1,0:T(8,128)(2,1)S(1)}, bf16[128,768]{1,0:T(8,128)(2,1)S(1)}, u32[]{:S(2)}, u32[]{:S(2)}) collective-permute-start(bf16[128,768]{1,0:T(8,128)(2,1)S(1)} %collective-permute-done.12.refs_1_), channel_id=1, source_target_pairs={{0,224},{1,225},{2,226},{3,227},{4,228},{5,229},{6,230},{7,231},{8... | collective-permute-start | bytes 589832 | tf_op jit(solution)/shard_map/ppermute | solution.py:33
  41.5 4.3 %collective-permute-start.16 = (f32[16,128]{1,0:T(8,128)S(1)}, f32[16,128]{1,0:T(8,128)S(1)}, u32[]{:S(2)}, u32[]{:S(2)}) collective-permute-start(f32[16,128]{1,0:T(8,128)S(1)} %shard_map.38), channel_id=1, source_target_pairs={{0,16},{1,17},{2,18},{3,19},{4,20},{5,21},{6,22},{7,23},{8,24},{9,... | collective-permute-start | bytes 24584 | tf_op jit(solution)/shard_map/ppermute | solution.py:33
  43.2 3.7 %collective-permute-start.17 = (f32[16,128]{1,0:T(8,128)S(1)}, f32[16,128]{1,0:T(8,128)S(1)}, u32[]{:S(2)}, u32[]{:S(2)}) collective-permute-start(f32[16,128]{1,0:T(8,128)S(1)} %shard_map.38), channel_id=1, source_target_pairs={{0,1},{1,16},{2,3},{3,18},{4,5},{5,20},{6,7},{7,22},{8,9},{9,24},{... | collective-permute-start | bytes 24584 | tf_op jit(solution)/shard_map/ppermute | solution.py:33
  44.7 2.5 %collective-permute-start.18 = (f32[16,128]{1,0:T(8,128)S(1)}, f32[16,128]{1,0:T(8,128)S(1)}, u32[]{:S(2)}, u32[]{:S(2)}) collective-permute-start(f32[16,128]{1,0:T(8,128)S(1)} %shard_map.38), channel_id=1, source_target_pairs={{0,17},{1,0},{2,19},{3,2},{4,21},{5,4},{6,23},{7,6},{8,25},{9,8},{... | collective-permute-start | bytes 24584 | tf_op jit(solution)/shard_map/ppermute | solution.py:33
  67.5 9.8 %collective-permute-start.19 = (f32[320,896]{1,0:T(8,128)S(1)}, f32[320,896]{1,0:T(8,128)S(1)}, u32[]{:S(2)}, u32[]{:S(2)}) collective-permute-start(f32[320,896]{1,0:T(8,128)S(1)} %get-tuple-element.86), channel_id=1, source_target_pairs={{0,8},{1,9},{2,10},{3,11},{4,12},{5,13},{6,14},{7,15},{8,0},{9,1},... | collective-permute-start | bytes 3440648 | tf_op jit(solution)/shard_map/ppermute | solution.py:33
  74.7 2.6 %collective-permute-start.20 = (f32[192,896]{1,0:T(8,128)S(1)}, f32[192,896]{1,0:T(8,128)S(1)}, u32[]{:S(2)}, u32[]{:S(2)}) collective-permute-start(f32[192,896]{1,0:T(8,128)S(1)} %shard_map.40), channel_id=1, source_target_pairs={{0,8},{1,9},{2,10},{3,11},{4,12},{5,13},{6,14},{7,15},{8,0},{9,1},... | collective-permute-start | bytes 2064392 | tf_op jit(solution)/shard_map/ppermute | solution.py:33

commit v8 on v7

--- a/solution.py
+++ b/solution.py
@@ -301,8 +301,9 @@
 
     own, far = [points, points], [across, across]
     both_ways = lambda pair: [along_z(pair[0], 1), along_z(pair[1], -1)]
+    down_first = lambda pair: [along_z(pair[1], -1), along_z(pair[0], 1)][::-1]
     own = both_ways(own)
-    far = both_ways(after(far, held))
+    far = down_first(after(far, held))
     pending = [([held, across], [(0, 0), (0, 1)])]
     for step in (1, 2, 3):
         seen = [] if step == 1 else state[2]
@@ -313,7 +314,7 @@
         take(*pending.pop(0))
         seen = state[2]
         if step < 3:
-            next_far = both_ways(after(far, seen))
+            next_far = down_first(after(far, seen))
         else:
             next_far = [along_z(after(far[1], seen), -1)]
         if step > 1:

time: 78.8 us -> 78.8 us (level)
  no operation moved by 1% of the time
where the time goes in v8:
time: 78.8 us; the launch traced here: 78.6 us
  starting transfers between devices  35.5 us (45%)
  blocking collectives  18.9 us (24%)
  Pallas kernels  12.2 us (15%)
  waiting for transfers between devices  9.8 us (12%)
  local copies, waits for them, and re-layouts  2.08 us (3%)
    ppermute x21, starting transfers between devices, send(): return lax.ppermute(block, AXES, route)  35.5 us
    all_to_all x1, blocking collectives, shards(): lax.all_to_all(everywhere, AXES, 0, 0, axis_index_groups=groups_by(lambda...  18.9 us
    ppermute x21, waiting for transfers between devices, send(): return lax.ppermute(block, AXES, route)  9.8 us
    pallas_call x8, Pallas kernels, logits_of(): pl.pallas_call(functools.partial(logits_kernel, len(blocks), first, len(b...  6.45 us
    pallas_call x3, Pallas kernels, sums_call(): pl.pallas_call(kernel, in_specs=[IN_VMEM] * len(operands), out_specs=(IN_...  4 us
    unnamed x4, local copies, waits for them, and re-layouts  2.06 us
  transfers between devices with their start and end apart: 21, of which 8 were waited for; matrix products, arithmetic and copies ran while one was open for 0% of the time, Pallas kernels for 11%

profile of v8, /device:TPU:1, one launch (start us, length us, event | category | flops | bytes accessed | tf_op | source)
XLA Modules:
  0.0 78.6 jit_solution(4146162419758020022)
XLA Ops:
  0.0 3.2 %collective-permute-start.5 = (bf16[512,768]{1,0:T(8,128)(2,1)}, bf16[512,768]{1,0:T(8,128)(2,1)S(1)}, u32[]{:S(2)}, u32[]{:S(2)}) collective-permute-start(bf16[512,768]{1,0:T(8,128)(2,1)} %cent_ref.1), channel_id=1, source_target_pairs={{0,8},{1,9},{2,10},{3,11},{4,12},{5,13},{6,14},{7,15},{8,0},{9,1},... | collective-permute-start | bytes 2359304 | tf_op jit(solution)/shard_map/ppermute | solution.py:33
  3.2 0.7 collective-permute-start.4
  4.0 1.6 %collective-permute-start = (bf16[128,768]{1,0:T(8,128)(2,1)}, bf16[128,768]{1,0:T(8,128)(2,1)S(1)}, u32[]{:S(2)}, u32[]{:S(2)}) collective-permute-start(bf16[128,768]{1,0:T(8,128)(2,1)} %point_ref.1), channel_id=1, source_target_pairs={{0,32},{1,33},{2,34},{3,35},{4,36},{5,37},{6,38},{7,39},{8,40},{9,... | collective-permute-start | bytes 589832 | tf_op jit(solution)/shard_map/ppermute | solution.py:33
  5.6 3.9 %collective-permute-start.1 = (bf16[128,768]{1,0:T(8,128)(2,1)}, bf16[128,768]{1,0:T(8,128)(2,1)S(1)}, u32[]{:S(2)}, u32[]{:S(2)}) collective-permute-start(bf16[128,768]{1,0:T(8,128)(2,1)} %point_ref.1), channel_id=1, source_target_pairs={{0,224},{1,225},{2,226},{3,227},{4,228},{5,229},{6,230},{7,231},{8... | collective-permute-start | bytes 589832 | tf_op jit(solution)/shard_map/ppermute | solution.py:33
  9.6 1.1 %copy-done = bf16[512,768]{1,0:T(8,128)(2,1)S(1)} copy-done((bf16[512,768]{1,0:T(8,128)(2,1)S(1)}, bf16[512,768]{1,0:T(8,128)(2,1)}, u32[]{:S(2)}) %copy-start) | copy-done | bytes 786456
  10.7 0.9 %copy-done.1 = bf16[128,768]{1,0:T(8,128)(2,1)S(1)} copy-done((bf16[128,768]{1,0:T(8,128)(2,1)S(1)}, bf16[128,768]{1,0:T(8,128)(2,1)}, u32[]{:S(2)}) %copy-start.1) | copy-done | bytes 196632
  11.6 0.2 shard_map.28
  11.9 0.1 collective-permute-start.8
  12.0 3.1 %collective-permute-start.9 = (bf16[128,768]{1,0:T(8,128)(2,1)S(1)}, bf16[128,768]{1,0:T(8,128)(2,1)S(1)}, u32[]{:S(2)}, u32[]{:S(2)}) collective-permute-start(bf16[128,768]{1,0:T(8,128)(2,1)S(1)} %collective-permute-done.4.refs_1_), channel_id=1, source_target_pairs={{0,224},{1,225},{2,226},{3,227},{4,228},{5,229},{6,230},{7,231},{8... | collective-permute-start | bytes 589832 | tf_op jit(solution)/shard_map/ppermute | solution.py:33
  15.0 0.0 collective-permute-done.refs_0_
  15.1 2.7 %collective-permute-start.3 = (bf16[128,768]{1,0:T(8,128)(2,1)S(1)}, bf16[128,768]{1,0:T(8,128)(2,1)S(1)}, u32[]{:S(2)}, u32[]{:S(2)}) collective-permute-start(bf16[128,768]{1,0:T(8,128)(2,1)S(1)} %collective-permute-done.1.refs_1_), channel_id=1, source_target_pairs={{0,224},{1,225},{2,226},{3,227},{4,228},{5,229},{6,230},{7,231},{8... | collective-permute-start | bytes 589832 | tf_op jit(solution)/shard_map/ppermute | solution.py:33
  17.7 0.0 collective-permute-done.5.cent_ref.refs_2_
  17.7 0.2 shard_map.29.refs_4_
  18.0 0.8 %shard_map.30 = (f32[1024,2048]{1,0:T(8,128)S(1)}, bf16[2048,768]{1,0:T(8,128)(2,1)S(1)}, f32[1,2048]{1,0:T(1,128)S(1)}) custom-call(bf16[128,768]{1,0:T(8,128)(2,1)S(1)} %get-tuple-element.48.refs_0_, bf16[128,768]{1,0:T(8,128)(2,1)S(1)} %collective-permute-done.4.refs_1_, bf16[512,768]{1,0:T(8,128)(2,1)S(1)} %collective-permute-done.5.cent_ref.refs_2_, ...), custom_call_target="tpu_custom_call" | custom-call | flops 402653184 | bytes 1 | tf_op jit(solution)/shard_map/pallas_call | solution.py:148
  18.8 0.8 collective-permute-done.8.refs_0_
  19.5 0.0 collective-permute-done.9.refs_1_
  19.5 0.0 collective-permute-start.10
  19.5 2.7 %collective-permute-start.11 = (bf16[128,768]{1,0:T(8,128)(2,1)S(1)}, bf16[128,768]{1,0:T(8,128)(2,1)S(1)}, u32[]{:S(2)}, u32[]{:S(2)}) collective-permute-start(bf16[128,768]{1,0:T(8,128)(2,1)S(1)} %collective-permute-done.9.refs_1_), channel_id=1, source_target_pairs={{0,224},{1,225},{2,226},{3,227},{4,228},{5,229},{6,230},{7,231},{8... | collective-permute-start | bytes 589832 | tf_op jit(solution)/shard_map/ppermute | solution.py:33
  22.2 1.5 %collective-permute-done.2.refs_0_ = bf16[128,768]{1,0:T(8,128)(2,1)S(1)} collective-permute-done((bf16[128,768]{1,0:T(8,128)(2,1)S(1)}, bf16[128,768]{1,0:T(8,128)(2,1)S(1)}, u32[]{:S(2)}, u32[]{:S(2)}) %collective-permute-start.2) | collective-permute-done | bytes 196640 | tf_op jit(solution)/shard_map/ppermute | solution.py:33
  23.7 0.0 collective-permute-done.3.refs_1_
  23.8 0.8 %shard_map.31 = (f32[1024,2048]{1,0:T(8,128)S(1)}, bf16[2048,768]{1,0:T(8,128)(2,1)S(1)}, f32[1,2048]{1,0:T(1,128)S(1)}) custom-call(bf16[128,768]{1,0:T(8,128)(2,1)S(1)} %collective-permute-done.refs_0_, bf16[128,768]{1,0:T(8,128)(2,1)S(1)} %collective-permute-done.1.refs_1_, ...), custom_call_target="tpu_custom_call", output_to_operand_aliasing={{0}: (6, {}), {1}: (7, {}), {2}: (8, {})} | custom-call | flops 402653184 | bytes 1 | tf_op jit(solution)/shard_map/pallas_call | solution.py:148
  24.6 2.7 %collective-permute-done.10.refs_0_ = bf16[128,768]{1,0:T(8,128)(2,1)S(1)} collective-permute-done((bf16[128,768]{1,0:T(8,128)(2,1)S(1)}, bf16[128,768]{1,0:T(8,128)(2,1)S(1)}, u32[]{:S(2)}, u32[]{:S(2)}) %collective-permute-start.10) | collective-permute-done | bytes 196640 | tf_op jit(solution)/shard_map/ppermute | solution.py:33
  27.3 2.4 %collective-permute-start.12 = (bf16[128,768]{1,0:T(8,128)(2,1)S(1)}, bf16[128,768]{1,0:T(8,128)(2,1)S(1)}, u32[]{:S(2)}, u32[]{:S(2)}) collective-permute-start(bf16[128,768]{1,0:T(8,128)(2,1)S(1)} %collective-permute-done.11.refs_1_), channel_id=1, source_target_pairs={{0,224},{1,225},{2,226},{3,227},{4,228},{5,229},{6,230},{7,231},{8... | collective-permute-start | bytes 589832 | tf_op jit(solution)/shard_map/ppermute | solution.py:33
  29.7 0.0 collective-permute-start.15
  29.7 1.4 %collective-permute-start.14 = (bf16[128,768]{1,0:T(8,128)(2,1)S(1)}, bf16[128,768]{1,0:T(8,128)(2,1)S(1)}, u32[]{:S(2)}, u32[]{:S(2)}) collective-permute-start(bf16[128,768]{1,0:T(8,128)(2,1)S(1)} %collective-permute-done.10.refs_0_), channel_id=1, source_target_pairs={{0,32},{1,33},{2,34},{3,35},{4,36},{5,37},{6,38},{7,39},{8,40},{9,... | collective-permute-start | bytes 589832 | tf_op jit(solution)/shard_map/ppermute | solution.py:33
  31.2 0.4 collective-permute-done.6.refs_0_
  31.5 0.0 collective-permute-start.7
  31.5 0.8 %shard_map.32 = (f32[1024,2048]{1,0:T(8,128)S(1)}, bf16[2048,768]{1,0:T(8,128)(2,1)S(1)}, f32[1,2048]{1,0:T(1,128)S(1)}) custom-call(bf16[128,768]{1,0:T(8,128)(2,1)S(1)} %collective-permute-done.8.refs_0_, bf16[128,768]{1,0:T(8,128)(2,1)S(1)} %collective-permute-done.9.refs_1_, ...), custom_call_target="tpu_custom_call", output_to_operand_aliasing={{0}: (6, {}), {1}: (7, {}), {2}: (8, {})} | custom-call | flops 402653184 | bytes 1 | tf_op jit(solution)/shard_map/pallas_call | solution.py:148
  32.4 0.8 %shard_map.33 = (f32[1024,2048]{1,0:T(8,128)S(1)}, bf16[2048,768]{1,0:T(8,128)(2,1)S(1)}, f32[1,2048]{1,0:T(1,128)S(1)}) custom-call(bf16[128,768]{1,0:T(8,128)(2,1)S(1)} %collective-permute-done.2.refs_0_, bf16[128,768]{1,0:T(8,128)(2,1)S(1)} %collective-permute-done.3.refs_1_, ...), custom_call_target="tpu_custom_call", output_to_operand_aliasing={{0}: (6, {}), {1}: (7, {}), {2}: (8, {})} | custom-call | flops 402653184 | bytes 1 | tf_op jit(solution)/shard_map/pallas_call | solution.py:148
  33.2 2.7 %collective-permute-start.13 = (bf16[128,768]{1,0:T(8,128)(2,1)S(1)}, bf16[128,768]{1,0:T(8,128)(2,1)S(1)}, u32[]{:S(2)}, u32[]{:S(2)}) collective-permute-start(bf16[128,768]{1,0:T(8,128)(2,1)S(1)} %collective-permute-done.12.refs_1_), channel_id=1, source_target_pairs={{0,224},{1,225},{2,226},{3,227},{4,228},{5,229},{6,230},{7,231},{8... | collective-permute-start | bytes 589832 | tf_op jit(solution)/shard_map/ppermute | solution.py:33
  35.9 0.8 %shard_map.34 = (f32[1024,2048]{1,0:T(8,128)S(1)}, bf16[2048,768]{1,0:T(8,128)(2,1)S(1)}, f32[1,2048]{1,0:T(1,128)S(1)}) custom-call(bf16[128,768]{1,0:T(8,128)(2,1)S(1)} %collective-permute-done.10.refs_0_, bf16[128,768]{1,0:T(8,128)(2,1)S(1)} %collective-permute-done.11.refs_1_, ...), custom_call_target="tpu_custom_call", output_to_operand_aliasing={{0}: (6, {}), {1}: (7, {}), {2}: (8, {})} | custom-call | flops 402653184 | bytes 1 | tf_op jit(solution)/shard_map/pallas_call | solution.py:148
  36.7 0.8 %shard_map.35 = (f32[1024,2048]{1,0:T(8,128)S(1)}, bf16[2048,768]{1,0:T(8,128)(2,1)S(1)}, f32[1,2048]{1,0:T(1,128)S(1)}) custom-call(bf16[128,768]{1,0:T(8,128)(2,1)S(1)} %collective-permute-done.6.refs_0_, bf16[128,768]{1,0:T(8,128)(2,1)S(1)} %collective-permute-done.15.refs_1_, ...), custom_call_target="tpu_custom_call", output_to_operand_aliasing={{0}: (6, {}), {1}: (7, {}), {2}: (8, {})} | custom-call | flops 402653184 | bytes 1 | tf_op jit(solution)/shard_map/pallas_call | solution.py:148
  37.5 0.8 %shard_map.36 = (f32[1024,2048]{1,0:T(8,128)S(1)}, bf16[2048,768]{1,0:T(8,128)(2,1)S(1)}, f32[1,2048]{1,0:T(1,128)S(1)}) custom-call(bf16[128,768]{1,0:T(8,128)(2,1)S(1)} %collective-permute-done.14.refs_0_, bf16[128,768]{1,0:T(8,128)(2,1)S(1)} %collective-permute-done.12.refs_1_, ...), custom_call_target="tpu_custom_call", output_to_operand_aliasing={{0}: (6, {}), {1}: (7, {}), {2}: (8, {})} | custom-call | flops 402653184 | bytes 1 | tf_op jit(solution)/shard_map/pallas_call | solution.py:148
  38.3 2.4 %collective-permute-done.13.refs_1_ = bf16[128,768]{1,0:T(8,128)(2,1)S(1)} collective-permute-done((bf16[128,768]{1,0:T(8,128)(2,1)S(1)}, bf16[128,768]{1,0:T(8,128)(2,1)S(1)}, u32[]{:S(2)}, u32[]{:S(2)}) %collective-permute-start.13) | collective-permute-done | bytes 196640 | tf_op jit(solution)/shard_map/ppermute | solution.py:33
  40.7 0.8 %shard_map.37 = (f32[1024,2048]{1,0:T(8,128)S(1)}, bf16[2048,768]{1,0:T(8,128)(2,1)S(1)}, f32[1,2048]{1,0:T(1,128)S(1)}) custom-call(bf16[128,768]{1,0:T(8,128)(2,1)S(1)} %collective-permute-done.7.refs_0_, bf16[128,768]{1,0:T(8,128)(2,1)S(1)} %collective-permute-done.13.refs_1_, ...), custom_call_target="tpu_custom_call", output_to_operand_aliasing={{0}: (6, {}), {1}: (7, {}), {2}: (8, {})} | custom-call | flops 402653184 | bytes 1 | tf_op jit(solution)/shard_map/pallas_call | solution.py:148
  41.5 1.6 %collective-permute-start.16 = (f32[16,128]{1,0:T(8,128)S(1)}, f32[16,128]{1,0:T(8,128)S(1)}, u32[]{:S(2)}, u32[]{:S(2)}) collective-permute-start(f32[16,128]{1,0:T(8,128)S(1)} %shard_map.38), channel_id=1, source_target_pairs={{0,16},{1,17},{2,18},{3,19},{4,20},{5,21},{6,22},{7,23},{8,24},{9,... | collective-permute-start | bytes 24584 | tf_op jit(solution)/shard_map/ppermute | solution.py:33
  43.2 1.5 %collective-permute-start.17 = (f32[16,128]{1,0:T(8,128)S(1)}, f32[16,128]{1,0:T(8,128)S(1)}, u32[]{:S(2)}, u32[]{:S(2)}) collective-permute-start(f32[16,128]{1,0:T(8,128)S(1)} %shard_map.38), channel_id=1, source_target_pairs={{0,1},{1,16},{2,3},{3,18},{4,5},{5,20},{6,7},{7,22},{8,9},{9,24},{... | collective-permute-start | bytes 24584 | tf_op jit(solution)/shard_map/ppermute | solution.py:33
  44.7 1.1 %collective-permute-start.18 = (f32[16,128]{1,0:T(8,128)S(1)}, f32[16,128]{1,0:T(8,128)S(1)}, u32[]{:S(2)}, u32[]{:S(2)}) collective-permute-start(f32[16,128]{1,0:T(8,128)S(1)} %shard_map.38), channel_id=1, source_target_pairs={{0,17},{1,0},{2,19},{3,2},{4,21},{5,4},{6,23},{7,6},{8,25},{9,8},{... | collective-permute-start | bytes 24584 | tf_op jit(solution)/shard_map/ppermute | solution.py:33
  45.8 1.0 %collective-permute-done.17 = f32[16,128]{1,0:T(8,128)S(1)} collective-permute-done((f32[16,128]{1,0:T(8,128)S(1)}, f32[16,128]{1,0:T(8,128)S(1)}, u32[]{:S(2)}, u32[]{:S(2)}) %collective-permute-start.17) | collective-permute-done | bytes 8224 | tf_op jit(solution)/shard_map/ppermute | solution.py:33
  46.9 0.3 collective-permute-done.18
  47.3 18.9 %all_to_all.5.parts_ref = f32[32,16,128]{2,1,0:T(8,128)S(1)} all-to-all(f32[32,16,128]{2,1,0:T(8,128)S(1)} %broadcast_in_dim.2), channel_id=1, replica_groups={{0,2,4,6,32,34,36,38,64,66,68,70,96,98,100,102,128,130,132,134,160,162,..., dimensions={0} | all-to-all | bytes 524288 | tf_op jit(solution)/shard_map/all_to_all | solution.py:335
  66.2 1.3 %shard_map.39 = (f32[320,896]{1,0:T(8,128)S(1)}, f32[8,2048]{1,0:T(8,128)S(1)}) custom-call(f32[1024,2048]{1,0:T(8,128)S(1)} %get-tuple-element.81.logits_ref, bf16[2048,768]{1,0:T(8,128)(2,1)S(1)} %get-tuple-element.82.group_ref, f32[32,16,128]{2,1,0:T(8,128)S(1)} %all_to_all.5.parts_ref), custom_call_target="tpu_custom_call" | custom-call | flops 1 | bytes 1 | tf_op jit(solution)/shard_map/pallas_call | solution.py:233
  67.5 6.4 %collective-permute-start.19 = (f32[320,896]{1,0:T(8,128)S(1)}, f32[320,896]{1,0:T(8,128)S(1)}, u32[]{:S(2)}, u32[]{:S(2)}) collective-permute-start(f32[320,896]{1,0:T(8,128)S(1)} %get-tuple-element.86), channel_id=1, source_target_pairs={{0,8},{1,9},{2,10},{3,11},{4,12},{5,13},{6,14},{7,15},{8,0},{9,1},... | collective-permute-start | bytes 3440648 | tf_op jit(solution)/shard_map/ppermute | solution.py:33
  73.9 0.8 shard_map.40
  74.7 0.1 collective-permute-start.20
  74.8 1.9 %shard_map.41.own_ref = f32[512,896]{1,0:T(8,128)S(1)} custom-call(f32[1024,2048]{1,0:T(8,128)S(1)} %get-tuple-element.81.logits_ref, bf16[2048,768]{1,0:T(8,128)(2,1)S(1)} %get-tuple-element.82.group_ref, f32[8,2048]{1,0:T(8,128)S(1)} %get-tuple-element.85.norm_ref, bf16[512,768]{1,0:T(8,128)(2,1)S(1)} %get-tuple-element.49.refs_3_.cent_ref), custom_call_target="tpu_custom_call" | custom-call | flops 1 | bytes 1 | tf_op jit(solution)/shard_map/pallas_call | solution.py:233
  76.7 0.6 collective-permute-done.20.refs_1_
  77.3 1.2 %shard_map.42 = f32[512,768]{1,0:T(8,128)} custom-call(f32[512,896]{1,0:T(8,128)S(1)} %shard_map.41.own_ref, f32[320,896]{1,0:T(8,128)S(1)} %collective-permute-done.19.refs_0_, f32[192,896]{1,0:T(8,128)S(1)} %collective-permute-done.20.refs_1_), custom_call_target="tpu_custom_call" | custom-call | flops 1179648 | bytes 1572864 | tf_op jit(solution)/shard_map/pallas_call | solution.py:270
  (18 shorter events, 0.1 us)
Async XLA Ops:
  0.0 17.7 %collective-permute-start.5 = (bf16[512,768]{1,0:T(8,128)(2,1)}, bf16[512,768]{1,0:T(8,128)(2,1)S(1)}, u32[]{:S(2)}, u32[]{:S(2)}) collective-permute-start(bf16[512,768]{1,0:T(8,128)(2,1)} %cent_ref.1), channel_id=1, source_target_pairs={{0,8},{1,9},{2,10},{3,11},{4,12},{5,13},{6,14},{7,15},{8,0},{9,1},... | collective-permute-start | bytes 2359304 | tf_op jit(solution)/shard_map/ppermute | solution.py:33
  3.2 8.6 %collective-permute-start.4 = (bf16[128,768]{1,0:T(8,128)(2,1)}, bf16[128,768]{1,0:T(8,128)(2,1)S(1)}, u32[]{:S(2)}, u32[]{:S(2)}) collective-permute-start(bf16[128,768]{1,0:T(8,128)(2,1)} %point_ref.1), channel_id=1, source_target_pairs={{0,17},{1,16},{2,19},{3,18},{4,21},{5,20},{6,23},{7,22},{8,25},{9,... | collective-permute-start | bytes 589832 | tf_op jit(solution)/shard_map/ppermute | solution.py:33
  4.0 11.1 %collective-permute-start = (bf16[128,768]{1,0:T(8,128)(2,1)}, bf16[128,768]{1,0:T(8,128)(2,1)S(1)}, u32[]{:S(2)}, u32[]{:S(2)}) collective-permute-start(bf16[128,768]{1,0:T(8,128)(2,1)} %point_ref.1), channel_id=1, source_target_pairs={{0,32},{1,33},{2,34},{3,35},{4,36},{5,37},{6,38},{7,39},{8,40},{9,... | collective-permute-start | bytes 589832 | tf_op jit(solution)/shard_map/ppermute | solution.py:33
  5.6 9.4 %collective-permute-start.1 = (bf16[128,768]{1,0:T(8,128)(2,1)}, bf16[128,768]{1,0:T(8,128)(2,1)S(1)}, u32[]{:S(2)}, u32[]{:S(2)}) collective-permute-start(bf16[128,768]{1,0:T(8,128)(2,1)} %point_ref.1), channel_id=1, source_target_pairs={{0,224},{1,225},{2,226},{3,227},{4,228},{5,229},{6,230},{7,231},{8... | collective-permute-start | bytes 589832 | tf_op jit(solution)/shard_map/ppermute | solution.py:33
  9.6 1.1 %copy-start = (bf16[512,768]{1,0:T(8,128)(2,1)S(1)}, bf16[512,768]{1,0:T(8,128)(2,1)}, u32[]{:S(2)}) copy-start(bf16[512,768]{1,0:T(8,128)(2,1)} %cent_ref.1) | copy-start | bytes 2359300
  10.7 0.9 %copy-start.1 = (bf16[128,768]{1,0:T(8,128)(2,1)S(1)}, bf16[128,768]{1,0:T(8,128)(2,1)}, u32[]{:S(2)}) copy-start(bf16[128,768]{1,0:T(8,128)(2,1)} %point_ref.1) | copy-start | bytes 589828
  11.9 7.7 %collective-permute-start.8 = (bf16[128,768]{1,0:T(8,128)(2,1)S(1)}, bf16[128,768]{1,0:T(8,128)(2,1)S(1)}, u32[]{:S(2)}, u32[]{:S(2)}) collective-permute-start(bf16[128,768]{1,0:T(8,128)(2,1)S(1)} %collective-permute-done.4.refs_1_), channel_id=1, source_target_pairs={{0,32},{1,33},{2,34},{3,35},{4,36},{5,37},{6,38},{7,39},{8,40},{9,... | collective-permute-start | bytes 589832 | tf_op jit(solution)/shard_map/ppermute | solution.py:33
  12.0 7.6 %collective-permute-start.9 = (bf16[128,768]{1,0:T(8,128)(2,1)S(1)}, bf16[128,768]{1,0:T(8,128)(2,1)S(1)}, u32[]{:S(2)}, u32[]{:S(2)}) collective-permute-start(bf16[128,768]{1,0:T(8,128)(2,1)S(1)} %collective-permute-done.4.refs_1_), channel_id=1, source_target_pairs={{0,224},{1,225},{2,226},{3,227},{4,228},{5,229},{6,230},{7,231},{8... | collective-permute-start | bytes 589832 | tf_op jit(solution)/shard_map/ppermute | solution.py:33
  15.0 8.7 %collective-permute-start.2 = (bf16[128,768]{1,0:T(8,128)(2,1)S(1)}, bf16[128,768]{1,0:T(8,128)(2,1)S(1)}, u32[]{:S(2)}, u32[]{:S(2)}) collective-permute-start(bf16[128,768]{1,0:T(8,128)(2,1)S(1)} %collective-permute-done.refs_0_), channel_id=1, source_target_pairs={{0,32},{1,33},{2,34},{3,35},{4,36},{5,37},{6,38},{7,39},{8,40},{9,... | collective-permute-start | bytes 589832 | tf_op jit(solution)/shard_map/ppermute | solution.py:33
  15.1 8.7 %collective-permute-start.3 = (bf16[128,768]{1,0:T(8,128)(2,1)S(1)}, bf16[128,768]{1,0:T(8,128)(2,1)S(1)}, u32[]{:S(2)}, u32[]{:S(2)}) collective-permute-start(bf16[128,768]{1,0:T(8,128)(2,1)S(1)} %collective-permute-done.1.refs_1_), channel_id=1, source_target_pairs={{0,224},{1,225},{2,226},{3,227},{4,228},{5,229},{6,230},{7,231},{8... | collective-permute-start | bytes 589832 | tf_op jit(solution)/shard_map/ppermute | solution.py:33
  19.5 7.8 %collective-permute-start.10 = (bf16[128,768]{1,0:T(8,128)(2,1)S(1)}, bf16[128,768]{1,0:T(8,128)(2,1)S(1)}, u32[]{:S(2)}, u32[]{:S(2)}) collective-permute-start(bf16[128,768]{1,0:T(8,128)(2,1)S(1)} %collective-permute-done.8.refs_0_), channel_id=1, source_target_pairs={{0,32},{1,33},{2,34},{3,35},{4,36},{5,37},{6,38},{7,39},{8,40},{9,... | collective-permute-start | bytes 589832 | tf_op jit(solution)/shard_map/ppermute | solution.py:33
  19.5 7.8 %collective-permute-start.11 = (bf16[128,768]{1,0:T(8,128)(2,1)S(1)}, bf16[128,768]{1,0:T(8,128)(2,1)S(1)}, u32[]{:S(2)}, u32[]{:S(2)}) collective-permute-start(bf16[128,768]{1,0:T(8,128)(2,1)S(1)} %collective-permute-done.9.refs_1_), channel_id=1, source_target_pairs={{0,224},{1,225},{2,226},{3,227},{4,228},{5,229},{6,230},{7,231},{8... | collective-permute-start | bytes 589832 | tf_op jit(solution)/shard_map/ppermute | solution.py:33
  23.8 7.8 %collective-permute-start.6 = (bf16[128,768]{1,0:T(8,128)(2,1)S(1)}, bf16[128,768]{1,0:T(8,128)(2,1)S(1)}, u32[]{:S(2)}, u32[]{:S(2)}) collective-permute-start(bf16[128,768]{1,0:T(8,128)(2,1)S(1)} %collective-permute-done.2.refs_0_), channel_id=1, source_target_pairs={{0,32},{1,33},{2,34},{3,35},{4,36},{5,37},{6,38},{7,39},{8,40},{9,... | collective-permute-start | bytes 589832 | tf_op jit(solution)/shard_map/ppermute | solution.py:33
  27.3 5.9 %collective-permute-start.12 = (bf16[128,768]{1,0:T(8,128)(2,1)S(1)}, bf16[128,768]{1,0:T(8,128)(2,1)S(1)}, u32[]{:S(2)}, u32[]{:S(2)}) collective-permute-start(bf16[128,768]{1,0:T(8,128)(2,1)S(1)} %collective-permute-done.11.refs_1_), channel_id=1, source_target_pairs={{0,224},{1,225},{2,226},{3,227},{4,228},{5,229},{6,230},{7,231},{8... | collective-permute-start | bytes 589832 | tf_op jit(solution)/shard_map/ppermute | solution.py:33
  29.7 7.0 %collective-permute-start.15 = (bf16[128,768]{1,0:T(8,128)(2,1)S(1)}, bf16[128,768]{1,0:T(8,128)(2,1)S(1)}, u32[]{:S(2)}, u32[]{:S(2)}) collective-permute-start(bf16[128,768]{1,0:T(8,128)(2,1)S(1)} %collective-permute-done.3.refs_1_), channel_id=1, source_target_pairs={{0,224},{1,225},{2,226},{3,227},{4,228},{5,229},{6,230},{7,231},{8... | collective-permute-start | bytes 589832 | tf_op jit(solution)/shard_map/ppermute | solution.py:33
  29.7 7.8 %collective-permute-start.14 = (bf16[128,768]{1,0:T(8,128)(2,1)S(1)}, bf16[128,768]{1,0:T(8,128)(2,1)S(1)}, u32[]{:S(2)}, u32[]{:S(2)}) collective-permute-start(bf16[128,768]{1,0:T(8,128)(2,1)S(1)} %collective-permute-done.10.refs_0_), channel_id=1, source_target_pairs={{0,32},{1,33},{2,34},{3,35},{4,36},{5,37},{6,38},{7,39},{8,40},{9,... | collective-permute-start | bytes 589832 | tf_op jit(solution)/shard_map/ppermute | solution.py:33
  31.5 6.8 %collective-permute-start.7 = (bf16[128,768]{1,0:T(8,128)(2,1)S(1)}, bf16[128,768]{1,0:T(8,128)(2,1)S(1)}, u32[]{:S(2)}, u32[]{:S(2)}) collective-permute-start(bf16[128,768]{1,0:T(8,128)(2,1)S(1)} %collective-permute-done.6.refs_0_), channel_id=1, source_target_pairs={{0,32},{1,33},{2,34},{3,35},{4,36},{5,37},{6,38},{7,39},{8,40},{9,... | collective-permute-start | bytes 589832 | tf_op jit(solution)/shard_map/ppermute | solution.py:33
  33.2 7.5 %collective-permute-start.13 = (bf16[128,768]{1,0:T(8,128)(2,1)S(1)}, bf16[128,768]{1,0:T(8,128)(2,1)S(1)}, u32[]{:S(2)}, u32[]{:S(2)}) collective-permute-start(bf16[128,768]{1,0:T(8,128)(2,1)S(1)} %collective-permute-done.12.refs_1_), channel_id=1, source_target_pairs={{0,224},{1,225},{2,226},{3,227},{4,228},{5,229},{6,230},{7,231},{8... | collective-permute-start | bytes 589832 | tf_op jit(solution)/shard_map/ppermute | solution.py:33
  41.5 4.3 %collective-permute-start.16 = (f32[16,128]{1,0:T(8,128)S(1)}, f32[16,128]{1,0:T(8,128)S(1)}, u32[]{:S(2)}, u32[]{:S(2)}) collective-permute-start(f32[16,128]{1,0:T(8,128)S(1)} %shard_map.38), channel_id=1, source_target_pairs={{0,16},{1,17},{2,18},{3,19},{4,20},{5,21},{6,22},{7,23},{8,24},{9,... | collective-permute-start | bytes 24584 | tf_op jit(solution)/shard_map/ppermute | solution.py:33
  43.2 3.7 %collective-permute-start.17 = (f32[16,128]{1,0:T(8,128)S(1)}, f32[16,128]{1,0:T(8,128)S(1)}, u32[]{:S(2)}, u32[]{:S(2)}) collective-permute-start(f32[16,128]{1,0:T(8,128)S(1)} %shard_map.38), channel_id=1, source_target_pairs={{0,1},{1,16},{2,3},{3,18},{4,5},{5,20},{6,7},{7,22},{8,9},{9,24},{... | collective-permute-start | bytes 24584 | tf_op jit(solution)/shard_map/ppermute | solution.py:33
  44.7 2.5 %collective-permute-start.18 = (f32[16,128]{1,0:T(8,128)S(1)}, f32[16,128]{1,0:T(8,128)S(1)}, u32[]{:S(2)}, u32[]{:S(2)}) collective-permute-start(f32[16,128]{1,0:T(8,128)S(1)} %shard_map.38), channel_id=1, source_target_pairs={{0,17},{1,0},{2,19},{3,2},{4,21},{5,4},{6,23},{7,6},{8,25},{9,8},{... | collective-permute-start | bytes 24584 | tf_op jit(solution)/shard_map/ppermute | solution.py:33
  67.5 9.8 %collective-permute-start.19 = (f32[320,896]{1,0:T(8,128)S(1)}, f32[320,896]{1,0:T(8,128)S(1)}, u32[]{:S(2)}, u32[]{:S(2)}) collective-permute-start(f32[320,896]{1,0:T(8,128)S(1)} %get-tuple-element.86), channel_id=1, source_target_pairs={{0,8},{1,9},{2,10},{3,11},{4,12},{5,13},{6,14},{7,15},{8,0},{9,1},... | collective-permute-start | bytes 3440648 | tf_op jit(solution)/shard_map/ppermute | solution.py:33
  74.7 2.6 %collective-permute-start.20 = (f32[192,896]{1,0:T(8,128)S(1)}, f32[192,896]{1,0:T(8,128)S(1)}, u32[]{:S(2)}, u32[]{:S(2)}) collective-permute-start(f32[192,896]{1,0:T(8,128)S(1)} %shard_map.40), channel_id=1, source_target_pairs={{0,8},{1,9},{2,10},{3,11},{4,12},{5,13},{6,14},{7,15},{8,0},{9,1},... | collective-permute-start | bytes 2064392 | tf_op jit(solution)/shard_map/ppermute | solution.py:33
